TPU v7x, 32 devices: a whole 2x2x4 slice. The times are simulated.
32 devices in a mesh: seq: 4 (over z), mp: 8 (over y, x, core).
Axes of the slice: x: 2, y: 2, z: 4, core: 2. Of those that a mesh axis runs over, the one named last changes fastest.
Arguments:
- residual: bfloat16 [4096, 2048], P('seq', 'mp'), may hold values from -6 to 6
- attn_gain: float32 [2048], replicated, may hold values from 0.5 to 1.5
- w_mixer: bfloat16 [2048, 16, 768], P('seq', 'mp'), may hold values from -0.125 to 0.125
- w_gates: bfloat16 [2048, 16, 2], P('seq', 'mp'), may hold values from -0.125 to 0.125
- conv_taps: float32 [4, 16, 512], P(None, 'mp'), may hold values from -2.5 to 2.5
- decay_scale: float32 [16], P('mp'), may hold values from 0.00012207031 to 0.03
- dt_bias: float32 [16], P('mp'), may hold values from -1 to 1
- head_gain: float32 [16, 256], P('mp'), may hold values from 0.5 to 1.5
- w_out: bfloat16 [4096, 2048], P('mp', 'seq'), may hold values from -0.09375 to 0.09375
- ffn_gain: float32 [2048], replicated, may hold values from 0.5 to 1.5
- w_gate: bfloat16 [2048, 5504], P('seq', 'mp'), may hold values from -0.125 to 0.125
- w_up: bfloat16 [2048, 5504], P('seq', 'mp'), may hold values from -0.125 to 0.125
- w_down: bfloat16 [5504, 2048], P('mp', 'seq'), may hold values from -0.078125 to 0.078125
- out_grad: bfloat16 [4096, 2048], P('seq', 'mp'), may hold values from -6 to 6
- doc_ids: int32 [4096], replicated, may hold values from 0 to 2, as said below
Outputs:
- output: bfloat16 [4096, 2048], P('seq', 'mp')
- grad_residual: float32 [4096, 2048], P('seq', 'mp')
- grad_attn_gain: float32 [2048], replicated
- grad_w_mixer: float32 [2048, 16, 768], P('seq', 'mp')
- grad_w_gates: float32 [2048, 16, 2], P('seq', 'mp')
- grad_conv_taps: float32 [4, 16, 512], P(None, 'mp')
- grad_decay_scale: float32 [16], P('mp')
- grad_dt_bias: float32 [16], P('mp')
- grad_head_gain: float32 [16, 256], P('mp')
- grad_w_out: float32 [4096, 2048], P('mp', 'seq')
- grad_ffn_gain: float32 [2048], replicated
- grad_w_gate: float32 [2048, 5504], P('seq', 'mp')
- grad_w_up: float32 [2048, 5504], P('seq', 'mp')
- grad_w_down: float32 [5504, 2048], P('mp', 'seq')
Inputs may be any that keep to these rules, and one draw needn't show every extreme that they name: doc_ids never falls, starts at 0 and rises by at most 1 from one token to the next; there are three documents, the second begins among the first 1024 tokens and ends among the last 1024.
All inputs are finite; a program needn't handle non-finite values.
Results may differ from a plain program's by a relative error of at most 0.012.
The roundings to bfloat16 on the way count: a program that leaves them out, or rounds other values in their place, can miss the bound.
Values may be sent and summed in bfloat16 or wider, within the bound.
No kernel may reach another device: no remote copies, remote signals or barrier semaphores. Data moves between devices by JAX's collectives and lax.ppermute only.
A program may use at most 256 MiB of HBM per device.

v0:
```python
import jax
import jax.numpy as jnp
from jax import lax
from jax.sharding import PartitionSpec as P

DK = 128
DV = 256
SPAN = 64


def shifted(value, axis, steps):
    count = lax.axis_size(axis)
    initial, last = (max(0, -steps), min(count, count - steps))
    return lax.ppermute(value, axis, [(source, source + steps) for source in range(initial, last)])


def matmul(left_mat, right_mat):
    return jnp.dot(left_mat, right_mat, precision=lax.Precision.HIGHEST)


def rms_norm(values, gain_row):
    return values * lax.rsqrt(jnp.mean(values * values, axis=-1, keepdims=True) + 1e-05) * gain_row


def gated_norm(head_vals, gate_cols, gain_row):
    inverse = lax.rsqrt(jnp.mean(head_vals * head_vals, axis=-1, keepdims=True) + 1e-05)
    return head_vals * inverse * gain_row * jax.nn.silu(gate_cols)


def conv_gates(extended, extended_ids, gate_vals, tap_weights, scales, biases):
    tok_rows = gate_vals.shape[0]
    convolved = jnp.zeros((tok_rows,) + extended.shape[1:], jnp.float32)
    for offset in range(4):
        lagged = extended[3 - offset : 3 - offset + tok_rows]
        same_doc = (extended_ids[3 - offset : 3 - offset + tok_rows] == extended_ids[3:]).astype(
            jnp.float32
        )
        convolved = convolved + tap_weights[offset] * lagged * same_doc[:, None, None]
    activated = jax.nn.silu(convolved)
    queries = activated[..., :DK]
    key_rows = activated[..., DK : 2 * DK]
    value_rows = activated[..., 2 * DK :]
    queries = (
        queries
        * lax.rsqrt(jnp.sum(queries * queries, axis=-1, keepdims=True) + 1e-06)
        * DK ** (-0.5)
    )
    key_rows = key_rows * lax.rsqrt(jnp.sum(key_rows * key_rows, axis=-1, keepdims=True) + 1e-06)
    log_decay = -scales * jax.nn.softplus(gate_vals[..., 0] + biases)
    beta_gates = jax.nn.sigmoid(gate_vals[..., 1])
    return (queries, key_rows, value_rows, log_decay, beta_gates)


def solve_lower(system, right_side):
    return lax.linalg.triangular_solve(
        system, right_side, left_side=True, lower=True, unit_diagonal=True
    )


def span_prep(queries, key_rows, value_rows, log_decay, beta_gates, span_ids, prior_id):
    span_len = queries.shape[0]
    cumulative = jnp.cumsum(log_decay)
    row_index = lax.broadcasted_iota(jnp.int32, (span_len, span_len), 0)
    col_index = lax.broadcasted_iota(jnp.int32, (span_len, span_len), 1)
    same_doc = span_ids[:, None] == span_ids[None, :]
    inside = (row_index >= col_index) & same_doc
    strict = (row_index > col_index) & same_doc
    spread = jnp.where(inside, cumulative[:, None] - cumulative[None, :], 0.0)
    decays = jnp.where(inside, jnp.exp(spread), 0.0)
    carried = jnp.exp(cumulative) * (span_ids == prior_id).astype(jnp.float32)
    lower_part = jnp.where(strict, decays * matmul(key_rows, key_rows.T), 0.0) * beta_gates[:, None]
    system = jnp.eye(span_len, dtype=jnp.float32) + lower_part
    weighted_keys = solve_lower(system, (beta_gates * carried)[:, None] * key_rows)
    weighted_vals = solve_lower(system, beta_gates[:, None] * value_rows)
    scores = decays * matmul(queries, key_rows.T)
    return (
        weighted_keys,
        weighted_vals,
        scores,
        carried[:, None] * queries,
        decays[-1][:, None] * key_rows,
        carried[-1],
    )


def state_step(carried_state, prepared):
    weighted_keys, weighted_vals, scores, decayed_q, end_keys, end_gain = prepared
    pseudo_vals = weighted_vals - matmul(weighted_keys, carried_state.T)
    outputs = matmul(decayed_q, carried_state.T) + matmul(scores, pseudo_vals)
    next_state = end_gain * carried_state + matmul(pseudo_vals.T, end_keys)
    return (next_state, outputs)


def span_chain(prepared):
    weighted_keys, weighted_vals, scores, decayed_q, end_keys, end_gain = prepared
    key_dim = weighted_keys.shape[-1]
    val_dim = weighted_vals.shape[-1]

    def compose(carry_maps, pieces):
        transition, offset_map = carry_maps
        span_wkeys, span_wvals, span_ekeys, span_egain = pieces
        step_transition = span_egain * jnp.eye(key_dim, dtype=jnp.float32) - matmul(
            span_wkeys.T, span_ekeys
        )
        step_offset = matmul(span_wvals.T, span_ekeys)
        return (
            (
                matmul(transition, step_transition),
                matmul(offset_map, step_transition) + step_offset,
            ),
            None,
        )

    def per_head(head_wkeys, head_wvals, head_ekeys, head_egain):
        start_maps = (
            jnp.eye(key_dim, dtype=jnp.float32),
            jnp.zeros((val_dim, key_dim), jnp.float32),
        )
        final_maps, ignored = lax.scan(
            compose, start_maps, (head_wkeys, head_wvals, head_ekeys, head_egain)
        )
        return final_maps

    return jax.vmap(per_head)(weighted_keys, weighted_vals, end_keys, end_gain)


def run_states(prepared, start_state):

    def per_head(head_prep, head_start):
        ignored, outputs = lax.scan(state_step, head_start, head_prep)
        return outputs

    return jax.vmap(per_head)(prepared, start_state)


def widen(values, offset_at, full_size, along):
    new_shape = list(values.shape)
    new_shape[along] = full_size
    return lax.dynamic_update_slice_in_dim(
        jnp.zeros(tuple(new_shape), jnp.float32), values, offset_at, along
    )


def share_sum(partial_value):
    return lax.psum_scatter(partial_value, "mp", scatter_dimension=1, tiled=True)


def shards(
    residual,
    attn_gain,
    w_mixer,
    w_gates,
    conv_taps,
    decay_scale,
    dt_bias,
    head_gain,
    w_out,
    ffn_gain,
    w_gate,
    w_up,
    w_down,
    out_grad,
    doc_ids,
):
    tok_rows, cols_local = residual.shape
    seq_count = lax.axis_size("seq")
    mp_count = lax.axis_size("mp")
    seq_pos = lax.axis_index("seq")
    mp_pos = lax.axis_index("mp")
    head_count = w_mixer.shape[1]
    span_count = tok_rows // SPAN
    conv_width = 2 * DK + DV
    col_start = mp_pos * cols_local
    head_start = mp_pos * head_count

    def full_of(share):
        return lax.all_gather(share, "mp", axis=1, tiled=True)

    full_rows, full_grad = (
        lax.all_gather(residual, "mp", axis=1, tiled=True),
        lax.all_gather(out_grad, "mp", axis=1, tiled=True),
    )
    mixer_full, gates_full, out_full, gate_full, up_full, down_full = (
        lax.all_gather(w_mixer, "seq", axis=0, tiled=True),
        lax.all_gather(w_gates, "seq", axis=0, tiled=True),
        lax.all_gather(w_out, "seq", axis=1, tiled=True),
        lax.all_gather(w_gate, "seq", axis=0, tiled=True),
        lax.all_gather(w_up, "seq", axis=0, tiled=True),
        lax.all_gather(w_down, "seq", axis=1, tiled=True),
    )
    model_width = mixer_full.shape[0]
    mixer_mat = mixer_full.reshape(model_width, -1)
    gates_mat = gates_full.reshape(model_width, -1)
    padded_ids = jnp.concatenate([jnp.full((3,), -1, jnp.int32), doc_ids])
    extended_ids = lax.dynamic_slice_in_dim(padded_ids, seq_pos * tok_rows, tok_rows + 3)
    span_ids = extended_ids[3:].reshape(span_count, SPAN)
    priors = extended_ids[2 : 2 + tok_rows].reshape(span_count, SPAN)[:, 0]
    inputs_wide = full_rows.astype(jnp.float32)
    normed, norm_pull = jax.vjp(rms_norm, inputs_wide, attn_gain)
    normed_low = normed.astype(jnp.bfloat16)
    projected = jnp.dot(normed_low, mixer_mat, preferred_element_type=jnp.float32).reshape(
        tok_rows, head_count, -1
    )
    gate_pre = jnp.dot(normed_low, gates_mat, preferred_element_type=jnp.float32).reshape(
        tok_rows, head_count, 2
    )
    conv_in = projected[..., :conv_width]
    rim_rows = shifted(conv_in[-3:], "seq", 1)
    extended = jnp.concatenate([rim_rows, conv_in], axis=0)

    def front_part(ext_vals, gate_vals, tap_weights, scales, biases):
        return conv_gates(ext_vals, extended_ids, gate_vals, tap_weights, scales, biases)

    front_out, front_pull = jax.vjp(front_part, extended, gate_pre, conv_taps, decay_scale, dt_bias)

    def by_span(tensor):
        return jnp.moveaxis(tensor.reshape((span_count, SPAN) + tensor.shape[1:]), 2, 0)

    def prepare(queries, key_rows, value_rows, log_decay, beta_gates):
        per_span = jax.vmap(span_prep)
        per_head = jax.vmap(per_span, in_axes=(0, 0, 0, 0, 0, None, None))
        return per_head(
            by_span(queries),
            by_span(key_rows),
            by_span(value_rows),
            by_span(log_decay),
            by_span(beta_gates),
            span_ids,
            priors,
        )

    prepared, prep_pull = jax.vjp(prepare, *front_out)
    (transition, offset_map), map_pull = jax.vjp(span_chain, prepared)

    def advance(turn_index, moved_state):
        stepped = (
            jnp.einsum("hvj,hjk->hvk", moved_state, transition, precision=lax.Precision.HIGHEST)
            + offset_map
        )
        return shifted(stepped, "seq", 1)

    start_state = lax.fori_loop(0, seq_count - 1, advance, jnp.zeros_like(offset_map))
    outputs, run_pull = jax.vjp(run_states, prepared, start_state)
    head_vals = jnp.moveaxis(outputs, 0, 2).reshape(tok_rows, head_count, DV)
    head_out, tail_pull = jax.vjp(gated_norm, head_vals, projected[..., conv_width:], head_gain)
    mixed = head_out.astype(jnp.bfloat16).reshape(tok_rows, -1)
    branch_share = share_sum(jnp.dot(mixed, out_full, preferred_element_type=jnp.float32))
    residual_share = residual.astype(jnp.float32)
    middle_share = residual_share + branch_share
    middle = full_of(middle_share)
    normed2, norm2_pull = jax.vjp(rms_norm, middle, ffn_gain)
    normed2_low = normed2.astype(jnp.bfloat16)
    gate_val = jnp.dot(normed2_low, gate_full, preferred_element_type=jnp.float32)
    up_val = jnp.dot(normed2_low, up_full, preferred_element_type=jnp.float32)
    gate_sigmoid = jax.nn.sigmoid(gate_val)
    gate_silu = gate_val * gate_sigmoid
    hidden_low = (gate_silu * up_val).astype(jnp.bfloat16)
    ffn_part = share_sum(jnp.dot(hidden_low, down_full, preferred_element_type=jnp.float32))
    output = (middle_share + ffn_part).astype(jnp.bfloat16)
    grad_hidden = jnp.dot(full_grad, down_full.T, preferred_element_type=jnp.float32)
    grad_down_local = jnp.dot(hidden_low.T, full_grad, preferred_element_type=jnp.float32)
    grad_gate_low = (
        grad_hidden * up_val * gate_sigmoid * (1.0 + gate_val * (1.0 - gate_sigmoid))
    ).astype(jnp.bfloat16)
    grad_up_low = (grad_hidden * gate_silu).astype(jnp.bfloat16)
    grad_normed2_share = share_sum(
        jnp.dot(grad_gate_low, gate_full.T, preferred_element_type=jnp.float32)
        + jnp.dot(grad_up_low, up_full.T, preferred_element_type=jnp.float32)
    )
    grad_gate_local = jnp.dot(normed2_low.T, grad_gate_low, preferred_element_type=jnp.float32)
    grad_up_local = jnp.dot(normed2_low.T, grad_up_low, preferred_element_type=jnp.float32)
    grad_normed2 = full_of(grad_normed2_share)
    grad_middle_norm, grad_ffn_gain = norm2_pull(grad_normed2)
    grad_middle = full_grad.astype(jnp.float32) + grad_middle_norm
    grad_branch_low = grad_middle.astype(jnp.bfloat16)
    grad_middle_share = lax.dynamic_slice_in_dim(grad_middle, col_start, cols_local, 1)
    ffn_gain_share = lax.dynamic_slice_in_dim(grad_ffn_gain, col_start, cols_local)
    grad_mixed = jnp.dot(grad_branch_low, out_full.T, preferred_element_type=jnp.float32)
    grad_out_local = jnp.dot(mixed.T, grad_branch_low, preferred_element_type=jnp.float32)
    grad_head_vals, grad_gate_cols, grad_head_gain = tail_pull(
        grad_mixed.reshape(tok_rows, head_count, DV)
    )
    grad_prep_run, grad_start = run_pull(by_span(grad_head_vals))
    transition_turned = jnp.swapaxes(transition, 1, 2)

    def retreat(turn_index, moved_grad):
        stepped = (
            jnp.einsum(
                "hvj,hjk->hvk", moved_grad, transition_turned, precision=lax.Precision.HIGHEST
            )
            + grad_start
        )
        return shifted(stepped, "seq", -1)

    grad_end = lax.fori_loop(0, seq_count - 1, retreat, jnp.zeros_like(grad_start))
    grad_transition = jnp.einsum(
        "hvj,hvk->hjk", start_state, grad_end, precision=lax.Precision.HIGHEST
    )
    (grad_prep_map,) = map_pull((grad_transition, grad_end))
    grad_prep = jax.tree.map(jnp.add, grad_prep_run, grad_prep_map)
    grad_front = prep_pull(grad_prep)
    grad_extended, grad_gate_pre, grad_taps, grad_scales, grad_biases = front_pull(grad_front)
    grad_rim = shifted(grad_extended[:3], "seq", -1)
    grad_conv_in = grad_extended[3:] + jnp.pad(grad_rim, ((tok_rows - 3, 0), (0, 0), (0, 0)))
    grad_proj_low = (
        jnp.concatenate([grad_conv_in, grad_gate_cols], axis=-1)
        .astype(jnp.bfloat16)
        .reshape(tok_rows, -1)
    )
    grad_gates_low = grad_gate_pre.astype(jnp.bfloat16).reshape(tok_rows, -1)
    grad_normed_share = share_sum(
        jnp.dot(grad_proj_low, mixer_mat.T, preferred_element_type=jnp.float32)
        + jnp.dot(grad_gates_low, gates_mat.T, preferred_element_type=jnp.float32)
    )
    grad_mixer_local = jnp.dot(
        normed_low.T, grad_proj_low, preferred_element_type=jnp.float32
    ).reshape(model_width, head_count, -1)
    grad_gates_local = jnp.dot(
        normed_low.T, grad_gates_low, preferred_element_type=jnp.float32
    ).reshape(model_width, head_count, 2)
    grad_normed = full_of(grad_normed_share)
    grad_inputs_norm, grad_attn_gain = norm_pull(grad_normed)
    grad_residual = grad_middle_share + lax.dynamic_slice_in_dim(
        grad_inputs_norm, col_start, cols_local, 1
    )
    attn_gain_share = lax.dynamic_slice_in_dim(grad_attn_gain, col_start, cols_local)
    weight_sums = (
        lax.psum_scatter(grad_mixer_local, "seq", scatter_dimension=0, tiled=True),
        lax.psum_scatter(grad_gates_local, "seq", scatter_dimension=0, tiled=True),
        lax.psum_scatter(grad_out_local, "seq", scatter_dimension=1, tiled=True),
        lax.psum_scatter(grad_gate_local, "seq", scatter_dimension=0, tiled=True),
        lax.psum_scatter(grad_up_local, "seq", scatter_dimension=0, tiled=True),
        lax.psum_scatter(grad_down_local, "seq", scatter_dimension=1, tiled=True),
    )
    all_heads = head_count * mp_count
    small_sums = lax.psum(
        (
            widen(attn_gain_share, col_start, model_width, 0),
            widen(ffn_gain_share, col_start, model_width, 0),
            widen(grad_taps, head_start, all_heads, 1),
            widen(grad_scales, head_start, all_heads, 0),
            widen(grad_biases, head_start, all_heads, 0),
            widen(grad_head_gain, head_start, all_heads, 0),
        ),
        ("seq", "mp"),
    )

    def own_heads(summed, along):
        return lax.dynamic_slice_in_dim(summed, head_start, head_count, along)

    return (
        output,
        grad_residual,
        small_sums[0],
        weight_sums[0],
        weight_sums[1],
        own_heads(small_sums[2], 1),
        own_heads(small_sums[3], 0),
        own_heads(small_sums[4], 0),
        own_heads(small_sums[5], 0),
        weight_sums[2],
        small_sums[1],
        weight_sums[3],
        weight_sums[4],
        weight_sums[5],
    )


def solution(mesh):
    in_specs = (
        P("seq", "mp"),
        P(),
        P("seq", "mp", None),
        P("seq", "mp", None),
        P(None, "mp", None),
        P("mp"),
        P("mp"),
        P("mp", None),
        P("mp", "seq"),
        P(),
        P("seq", "mp"),
        P("seq", "mp"),
        P("mp", "seq"),
        P("seq", "mp"),
        P(),
    )
    out_specs = (
        P("seq", "mp"),
        P("seq", "mp"),
        P(),
        P("seq", "mp", None),
        P("seq", "mp", None),
        P(None, "mp", None),
        P("mp"),
        P("mp"),
        P("mp", None),
        P("mp", "seq"),
        P(),
        P("seq", "mp"),
        P("seq", "mp"),
        P("mp", "seq"),
    )
    return jax.shard_map(shards, mesh=mesh, in_specs=in_specs, out_specs=out_specs, check_vma=False)
```

profile of v0, /device:TPU:0, one launch (start us, length us, event | category | flops | bytes accessed | tf_op | source)
XLA Modules:
  0.0 2873.1 jit_solution(16526653178930978389)
XLA Ops:
  12.0 13.5 all_gather.34
  26.2 23.9 all-gather.11.cloned.1.call-done
  56.9 110.7 %all-gather.13.cloned.1.call-done = bf16[2048,2,768]{2,0,1:T(8,128)(2,1)} async-done(((bf16[512,2,768]{2,0,1:T(8,128)(2,1)}), bf16[2048,2,768]{2,0,1:T(8,128)(2,1)}) %all-gather.13.cloned.1.call-update) | async-done | bytes 6291472 | tf_op jit(solution)/shard_map/all_gather | solution.py:184
  167.6 8.6 copy.391
  176.3 10.1 fusion.117
  206.8 158.0 %custom-call.12 = f32[2,16,1,64,64]{3,4,2,1,0:T(8,128)S(1)} custom-call(f32[2,16,1,64,64]{4,3,2,1,0:T(8,128)} %get-tuple-element.1709), custom_call_target="InvertDiagBlocksLowerTriangular" | custom-call | tf_op jit(solution)/shard_map/jvp(vmap(vmap()))/triangular_solve | solution.py:55
  378.2 123.2 %while.124 = (s32[]{:T(128)}, f32[2,128,128]{1,2,0:T(8,128)S(1)}, f32[2,256,128]{1,2,0:T(8,128)S(1)}, f32[16,2,128,64]{2,3,1,0:T(8,128)}, f32[16,2,256,64]{2,3,1...) while((s32[]{:T(128)}, f32[2,128,128]{1,2,0:T(8,128)S(1)}, ...), condition=%wide.region_4.5_spmd.clone, body=%wide.region_3.4_spmd.clone.sunk | while | flops 226787328 | bytes 3740836 | solution.py:119
  503.1 27.7 while.120
  541.5 167.0 %while.121 = (s32[]{:T(128)}, f32[2,256,128]{2,1,0:T(8,128)S(1)}, f32[16,2,64,256]{3,2,1,0:T(8,128)}, f32[16,2,128,256]{2,3,1,0:T(8,128)}, f32[16,2,64,256]{3,2,...) while((s32[]{:T(128)}, f32[2,256,128]{2,1,0:T(8,128)S(1)}, ...), condition=%wide.region_9.10_spmd, body=%wide.region_8.9_spmd.sunk | while | flops 176357376 | bytes 3676329 | solution.py:130
  717.5 7.6 fusion.241
  725.2 71.6 %reduce-scatter.13.cloned.1.call-done = f32[1024,256]{1,0:T(8,128)} async-done(((f32[1024,2048]{1,0:T(8,128)}), f32[1024,256]{1,0:T(8,128)}) %reduce-scatter.13.cloned.1.call-update) | async-done | bytes 1048592 | tf_op jit(solution)/shard_map/reduce_scatter | solution.py:145
  802.6 52.8 %all-gather.17.cloned.1.call-done = f32[1024,2048]{1,0:T(8,128)} async-done(((f32[1024,256]{1,0:T(8,128)}), f32[1024,2048]{1,0:T(8,128)}) %all-gather.17.cloned.1.call-update) | async-done | bytes 8388624 | tf_op jit(solution)/shard_map/all_gather | solution.py:177
  863.9 51.1 %all-gather.19.cloned.1.call-done = bf16[2048,688]{0,1:T(8,128)(2,1)} async-done(((bf16[512,688]{0,1:T(8,128)(2,1)}), bf16[2048,688]{0,1:T(8,128)(2,1)}) %all-gather.19.cloned.1.call-update) | async-done | bytes 2818064 | tf_op jit(solution)/shard_map/all_gather | solution.py:187
  915.0 7.7 fusion.242
  922.8 50.7 %all-gather.21.cloned.1.call-done = bf16[2048,688]{0,1:T(8,128)(2,1)} async-done(((bf16[512,688]{0,1:T(8,128)(2,1)}), bf16[2048,688]{0,1:T(8,128)(2,1)}) %all-gather.21.cloned.1.call-update) | async-done | bytes 2818064 | tf_op jit(solution)/shard_map/all_gather | solution.py:188
  973.5 7.7 fusion.243
  981.3 50.7 %all-gather.23.cloned.1.call-done = bf16[688,2048]{1,0:T(8,128)(2,1)} async-done(((bf16[688,512]{1,0:T(8,128)(2,1)}), bf16[688,2048]{1,0:T(8,128)(2,1)}) %all-gather.23.cloned.1.call-update) | async-done | bytes 2818064 | tf_op jit(solution)/shard_map/all_gather | solution.py:189
  1032.0 38.2 %all-gather.25.cloned.1.call-done = bf16[1024,2048]{1,0:T(8,128)(2,1)} async-done(((bf16[1024,256]{1,0:T(8,128)(2,1)}), bf16[1024,2048]{1,0:T(8,128)(2,1)}) %all-gather.25.cloned.1.call-update) | async-done | bytes 4194320 | tf_op jit(solution)/shard_map/all_gather | solution.py:181
  1070.2 10.0 multiply_convert_fusion.2
  1090.1 71.4 %reduce-scatter.17.cloned.1.call-done = f32[1024,256]{1,0:T(8,128)} async-done(((f32[1024,2048]{1,0:T(8,128)}), f32[1024,256]{1,0:T(8,128)}) %reduce-scatter.17.cloned.1.call-update) | async-done | bytes 1048592 | tf_op jit(solution)/shard_map/reduce_scatter | solution.py:145
  1161.6 57.8 %all-gather.27.cloned.1.call-done = f32[1024,2048]{1,0:T(8,128)} async-done(((f32[1024,256]{1,0:T(8,128)}), f32[1024,2048]{1,0:T(8,128)}) %all-gather.27.cloned.1.call-update) | async-done | bytes 8388624 | tf_op jit(solution)/shard_map/all_gather | solution.py:177
  1219.4 7.7 multiply_reduce_fusion.1
  1254.7 274.2 %while.125 = (s32[]{:T(128)}, f32[2,256,128]{2,1,0:T(8,128)S(1)}, f32[16,2,64,128]{3,2,1,0:T(8,128)}, f32[16,2,64,256]{3,2,1,0:T(8,128)}, f32[16,2,64,64]{3,2,0,...) while((s32[]{:T(128)}, f32[2,256,128]{2,1,0:T(8,128)S(1)}, ...), condition=%wide.region_19.20_spmd.clone, body=%wide.region_17.19_spmd.clone.sunk | while | flops 353009664 | bytes 4727576 | solution.py:130
  1529.6 35.6 %while.122 = (s32[]{:T(128)}, f32[2,256,128]{2,1,0:T(8,128)}, f32[2,128,128]{2,1,0:T(8,128)S(1)}, f32[2,256,128]{2,1,0:T(8,128)S(1)}, s32[]{:T(128)}) while((s32[]{:T(128)}, f32[2,256,128]{2,1,0:T(8,128)}, f32[2,128,128]{2,1,0:T(8,128)S(1)}, f32[2,256,128]{2,1,0:T(8,128)S(1)}, s32[]{:T(128)}) %tuple.296), condition=%wide.region_21.22_spmd, body=%wide.region_20.21_spmd.sunk | while | flops 100728832 | bytes 1966181 | solution.py:295
  1532.9 9.4 collective-permute-done.1
  1545.6 8.6 collective-permute-done.1
  1557.5 7.6 collective-permute-done.1
  1573.0 245.4 %while.123 = (s32[]{:T(128)}, f32[2,128,128]{1,2,0:T(8,128)S(1)}, f32[2,256,128]{1,2,0:T(8,128)}, f32[16,2,64,128]{3,2,1,0:T(8,128)}, f32[16,2,64,256]{3,2,1,0:T...) while((s32[]{:T(128)}, f32[2,128,128]{1,2,0:T(8,128)S(1)}, ...), condition=%wide.region_24.25_spmd.clone, body=%wide.region_22.24_spmd.clone.sunk | while | flops 453197824 | bytes 4656337 | solution.py:119
  1873.9 7.6 pad_add_fusion
  1884.4 13.6 bitcast_add_fusion
  1899.8 7.2 fusion.244
  1919.0 13.0 fusion.125
  1932.1 38.6 %reduce-scatter.19.cloned.1.call-done = f32[1024,256]{1,0:T(8,128)} async-done(((f32[1024,2048]{1,0:T(8,128)}), f32[1024,256]{1,0:T(8,128)}) %reduce-scatter.19.cloned.1.call-update) | async-done | bytes 1048592 | tf_op jit(solution)/shard_map/reduce_scatter | solution.py:145
  1970.8 7.0 fusion.249
  1979.1 7.6 fusion.250
  1988.4 7.6 fusion.248
  1997.2 8.5 fusion.131
  2012.5 33.4 %reduce-scatter.15.cloned.1.call-done = f32[1024,256]{1,0:T(8,128)} async-done(((f32[1024,2048]{1,0:T(8,128)}), f32[1024,256]{1,0:T(8,128)}) %reduce-scatter.15.cloned.1.call-update) | async-done | bytes 1048592 | tf_op jit(solution)/shard_map/reduce_scatter | solution.py:145
  2049.4 124.3 %all-reduce.20.cloned.1.call-done = f32[4,16,512]{2,1,0:T(8,128)} async-done(((f32[4,16,512]{2,1,0:T(8,128)}), f32[4,16,512]{2,1,0:T(8,128)}) %all-reduce.20.cloned.1.call-update) | async-done | bytes 131088 | tf_op jit(solution)/shard_map/psum | solution.py:336
  2175.1 27.5 reduce-scatter.31.cloned.1.call-done
  2204.6 210.8 %reduce-scatter.21.cloned.1.call-done = f32[512,2,768]{2,0,1:T(8,128)} async-done(((f32[2048,2,768]{2,0,1:T(8,128)}), f32[512,2,768]{2,0,1:T(8,128)}) %reduce-scatter.21.cloned.1.call-update) | async-done | bytes 3145744 | tf_op jit(solution)/shard_map/reduce_scatter | solution.py:328
  2421.4 52.9 %all-gather.29.cloned.1.call-done = f32[1024,2048]{1,0:T(8,128)} async-done(((f32[1024,256]{1,0:T(8,128)}), f32[1024,2048]{1,0:T(8,128)}) %all-gather.29.cloned.1.call-update) | async-done | bytes 8388624 | tf_op jit(solution)/shard_map/all_gather | solution.py:177
  2474.4 8.0 multiply_reduce_fusion.2
  2482.6 45.0 %all-reduce.17 = (f32[2048]{0:T(1024)}, f32[16]{0:T(128)S(1)}, f32[16]{0:T(128)S(1)}, f32[16,256]{1,0:T(8,128)S(1)}, f32[2048]{0:T(1024)}) all-reduce(f32[2048]{0:T(1024)S(1)} %dynamic-slice_dynamic-update-slice_fusion.1, f32[16]{0:T(128)S(1)} %negate_dynamic-update-slice_fusion, ...), channel_id=1, replica_groups=mesh['seq'=4,'mp'=8] {'seq','mp'}, use_global_device_ids=true, to_apply=%region_38.40 | all-reduce | flops 8224 | bytes 65792 | tf_op jit(solution)/shard_map/psum | solution.py:336
  2532.7 45.8 %reduce-scatter.25.cloned.1.call-done = f32[512,688]{0,1:T(8,128)} async-done(((f32[2048,688]{0,1:T(8,128)}), f32[512,688]{0,1:T(8,128)}) %reduce-scatter.25.cloned.1.call-update) | async-done | bytes 1409040 | tf_op jit(solution)/shard_map/reduce_scatter | solution.py:331
  2578.4 103.6 %reduce-scatter.27.cloned.1.call-done = f32[512,688]{0,1:T(8,128)} async-done(((f32[2048,688]{0,1:T(8,128)}), f32[512,688]{0,1:T(8,128)}) %reduce-scatter.27.cloned.1.call-update) | async-done | bytes 1409040 | tf_op jit(solution)/shard_map/reduce_scatter | solution.py:332
  2682.0 103.5 %reduce-scatter.29.cloned.1.call-done = f32[688,512]{1,0:T(8,128)} async-done(((f32[688,2048]{1,0:T(8,128)}), f32[688,512]{1,0:T(8,128)}) %reduce-scatter.29.cloned.1.call-update) | async-done | bytes 1409040 | tf_op jit(solution)/shard_map/reduce_scatter | solution.py:333
  2785.6 80.3 %reduce-scatter.23.cloned.1.call-done = f32[512,512]{1,0:T(8,128)} async-done(((f32[512,2048]{1,0:T(8,128)}), f32[512,512]{1,0:T(8,128)}) %reduce-scatter.23.cloned.1.call-update) | async-done | bytes 1048592 | tf_op jit(solution)/shard_map/reduce_scatter | solution.py:330
  (1188 shorter events, 1072.6 us)
Async XLA Ops:
  7.2 42.9 %all-gather.11.cloned.1.call-start = ((), (), s32[]{:S(2)}) async-start(), calls=%async_computation.10 | async-start | bytes 4718592 | tf_op jit(solution)/shard_map/all_gather | solution.py:180
  8.0 159.7 %all-gather.13.cloned.1.call-start = ((), (), s32[]{:S(2)}) async-start(), calls=%async_computation.11 | async-start | bytes 7864320 | tf_op jit(solution)/shard_map/all_gather | solution.py:184
  10.7 42.6 %copy-start.115 = (f32[2048]{0:T(1024)S(1)}, f32[2048]{0:T(1024)}, u32[]{:S(2)}) copy-start(f32[2048]{0:T(1024)} %param.30) | copy-start | bytes 24580
  10.8 706.7 %all-gather.15.cloned.1.call-start = ((), (), s32[]{:S(2)}) async-start(), calls=%async_computation.12 | async-start | bytes 2621440 | tf_op jit(solution)/shard_map/all_gather | solution.py:186
  11.5 785.3 %reduce-scatter.13.cloned.1.call-start = ((), (), s32[]{:S(2)}) async-start(), calls=%async_computation.13 | async-start | bytes 9437184 | tf_op jit(solution)/shard_map/reduce_scatter | solution.py:145
  11.8 182.1 %copy-start.86 = (f32[1024]{0:T(1024)}, f32[1024]{0:T(1024)S(1)}, u32[]{:S(2)}) copy-start(f32[1024]{0:T(1024)S(1)} %get-tuple-element.1684) | copy-start | bytes 12292
  12.0 182.0 %copy-start.88 = (f32[1024]{0:T(1024)}, f32[1024]{0:T(1024)S(1)}, u32[]{:S(2)}) copy-start(f32[1024]{0:T(1024)S(1)} %get-tuple-element.1710) | copy-start | bytes 12292
  12.0 182.0 %copy-start.90 = (f32[1024]{0:T(1024)}, f32[1024]{0:T(1024)S(1)}, u32[]{:S(2)}) copy-start(f32[1024]{0:T(1024)S(1)} %get-tuple-element.1711) | copy-start | bytes 12292
  12.0 181.9 %copy-start.92 = (f32[2,512]{1,0:T(2,128)}, f32[2,512]{1,0:T(2,128)S(1)}, u32[]{:S(2)}) copy-start(f32[2,512]{1,0:T(2,128)S(1)} %get-tuple-element.1712) | copy-start | bytes 12292
  12.0 181.9 %copy-start.94 = (f32[2,512]{1,0:T(2,128)}, f32[2,512]{1,0:T(2,128)S(1)}, u32[]{:S(2)}) copy-start(f32[2,512]{1,0:T(2,128)S(1)} %get-tuple-element.1713) | copy-start | bytes 12292
  12.0 181.9 %copy-start.96 = (f32[2,512]{1,0:T(2,128)}, f32[2,512]{1,0:T(2,128)S(1)}, u32[]{:S(2)}) copy-start(f32[2,512]{1,0:T(2,128)S(1)} %get-tuple-element.1714) | copy-start | bytes 12292
  12.0 181.9 %copy-start.98 = (f32[2,512]{1,0:T(2,128)}, f32[2,512]{1,0:T(2,128)S(1)}, u32[]{:S(2)}) copy-start(f32[2,512]{1,0:T(2,128)S(1)} %get-tuple-element.1715) | copy-start | bytes 12292
  25.7 179.4 %copy-start.65 = (pred[64,64]{1,0:T(8,128)(4,1)}, pred[64,64]{1,0:T(8,128)(4,1)S(1)}, u32[]{:S(2)}) copy-start(pred[64,64]{1,0:T(8,128)(4,1)S(1)} %get-tuple-element.1731) | copy-start | bytes 12292
  26.2 178.9 %copy-start.48 = (pred[16,64,64]{2,1,0:T(8,128)(4,1)}, pred[16,64,64]{2,1,0:T(8,128)(4,1)S(1)}, u32[]{:S(2)}) copy-start(pred[16,64,64]{2,1,0:T(8,128)(4,1)S(1)} %get-tuple-element.1719) | copy-start | bytes 196612
  26.2 507.3 %copy-start.40 = (pred[16,64,64]{2,1,0:T(8,128)(4,1)}, pred[16,64,64]{2,1,0:T(8,128)(4,1)S(1)}, u32[]{:S(2)}) copy-start(pred[16,64,64]{2,1,0:T(8,128)(4,1)S(1)} %get-tuple-element.1720) | copy-start | bytes 196612
  53.5 122.7 %copy-start.106 = (f32[1024]{0:T(1024)}, f32[1024]{0:T(1024)S(1)}, u32[]{:S(2)}) copy-start(f32[1024]{0:T(1024)S(1)} %fusion.224) | copy-start | bytes 12292
  55.7 309.2 %copy-start.50 = (f32[16,64,2]{1,0,2:T(8,128)}, f32[16,64,2]{1,0,2:T(8,128)S(1)}, u32[]{:S(2)}) copy-start(f32[16,64,2]{1,0,2:T(8,128)S(1)} %div.70) | copy-start | bytes 24580
  56.9 133.5 %copy-start.54 = (f32[2,16,64]{2,1,0:T(8,128)}, f32[2,16,64]{2,1,0:T(8,128)S(1)}, u32[]{:S(2)}) copy-start(f32[2,16,64]{2,1,0:T(8,128)S(1)} %get-tuple-element.1679) | copy-start | bytes 24580
  189.0 4.8 collective-permute-start.2
  503.7 9.3 collective-permute-start
  513.4 8.8 collective-permute-start
  522.6 8.3 collective-permute-start
  725.1 130.3 %all-gather.17.cloned.1.call-start = ((), (), s32[]{:S(2)}) async-start(), calls=%async_computation.14 | async-start | bytes 9437184 | tf_op jit(solution)/shard_map/all_gather | solution.py:177
  799.3 115.7 %all-gather.19.cloned.1.call-start = ((), (), s32[]{:S(2)}) async-start(), calls=%async_computation.15 | async-start | bytes 3522560 | tf_op jit(solution)/shard_map/all_gather | solution.py:187
  799.9 173.6 %all-gather.21.cloned.1.call-start = ((), (), s32[]{:S(2)}) async-start(), calls=%async_computation.16 | async-start | bytes 3522560 | tf_op jit(solution)/shard_map/all_gather | solution.py:188
  800.7 231.3 %all-gather.23.cloned.1.call-start = ((), (), s32[]{:S(2)}) async-start(), calls=%async_computation.17 | async-start | bytes 3522560 | tf_op jit(solution)/shard_map/all_gather | solution.py:189
  801.4 268.8 %all-gather.25.cloned.1.call-start = ((), (), s32[]{:S(2)}) async-start(), calls=%async_computation.19 | async-start | bytes 4718592 | tf_op jit(solution)/shard_map/all_gather | solution.py:181
  802.2 57.5 %copy-start.69 = (f32[2048]{0:T(1024)S(1)}, f32[2048]{0:T(1024)}, u32[]{:S(2)}) copy-start(f32[2048]{0:T(1024)} %param.38) | copy-start | bytes 24580
  802.2 359.3 %reduce-scatter.17.cloned.1.call-start = ((), (), s32[]{:S(2)}) async-start(), calls=%async_computation.20 | async-start | bytes 9437184 | tf_op jit(solution)/shard_map/reduce_scatter | solution.py:145
  1090.0 129.3 %all-gather.27.cloned.1.call-start = ((), (), s32[]{:S(2)}) async-start(), calls=%async_computation.21 | async-start | bytes 9437184 | tf_op jit(solution)/shard_map/all_gather | solution.py:177
  1161.5 809.2 %reduce-scatter.19.cloned.1.call-start = ((), (), s32[]{:S(2)}) async-start(), calls=%async_computation.22 | async-start | bytes 9437184 | tf_op jit(solution)/shard_map/reduce_scatter | solution.py:145
  1531.6 10.7 collective-permute-start.1
  1544.3 9.9 collective-permute-start.1
  1556.2 8.9 collective-permute-start.1
  1864.1 17.5 collective-permute-start.3
  1898.0 147.8 %reduce-scatter.15.cloned.1.call-start = ((), (), s32[]{:S(2)}) async-start(), calls=%async_computation.18 | async-start | bytes 9437184 | tf_op jit(solution)/shard_map/reduce_scatter | solution.py:145
  1907.0 266.6 %all-reduce.20.cloned.1.call-start = ((), (), s32[]{:S(2)}) async-start(), calls=%async_computation.25 | async-start | bytes 262144 | tf_op jit(solution)/shard_map/psum | solution.py:336
  1907.8 294.7 %reduce-scatter.31.cloned.1.call-start = ((), (), s32[]{:S(2)}) async-start(), calls=%async_computation.30 | async-start | bytes 1310720
  1913.7 501.8 %reduce-scatter.21.cloned.1.call-start = ((), (), s32[]{:S(2)}) async-start(), calls=%async_computation.24 | async-start | bytes 15728640 | tf_op jit(solution)/shard_map/reduce_scatter | solution.py:328
  1932.1 542.3 %all-gather.29.cloned.1.call-start = ((), (), s32[]{:S(2)}) async-start(), calls=%async_computation.23 | async-start | bytes 9437184 | tf_op jit(solution)/shard_map/all_gather | solution.py:177
  1970.7 607.7 %reduce-scatter.25.cloned.1.call-start = ((), (), s32[]{:S(2)}) async-start(), calls=%async_computation.27 | async-start | bytes 7045120 | tf_op jit(solution)/shard_map/reduce_scatter | solution.py:331
  1977.8 704.2 %reduce-scatter.27.cloned.1.call-start = ((), (), s32[]{:S(2)}) async-start(), calls=%async_computation.28 | async-start | bytes 7045120 | tf_op jit(solution)/shard_map/reduce_scatter | solution.py:332
  1986.8 798.8 %reduce-scatter.29.cloned.1.call-start = ((), (), s32[]{:S(2)}) async-start(), calls=%async_computation.29 | async-start | bytes 7045120 | tf_op jit(solution)/shard_map/reduce_scatter | solution.py:333
  1996.0 869.9 %reduce-scatter.23.cloned.1.call-start = ((), (), s32[]{:S(2)}) async-start(), calls=%async_computation.26 | async-start | bytes 5242880 | tf_op jit(solution)/shard_map/reduce_scatter | solution.py:330
  2005.7 40.2 %copy-start.33 = (f32[1024,256]{1,0:T(8,128)S(1)}, f32[1024,256]{1,0:T(8,128)}, u32[]{:S(2)}) copy-start(f32[1024,256]{1,0:T(8,128)} %convert_add_fusion) | copy-start | bytes 3145732
  2005.7 42.3 %copy-start.64 = (f32[16,64,2]{1,0,2:T(8,128)S(1)}, f32[16,64,2]{1,0,2:T(8,128)}, u32[]{:S(2)}) copy-start(f32[16,64,2]{1,0,2:T(8,128)} %copy-done.63) | copy-start | bytes 24580
  2005.7 43.6 %copy-start.117 = (f32[2,256]{1,0:T(2,128)S(1)}, f32[2,256]{1,0:T(2,128)}, u32[]{:S(2)}) copy-start(f32[2,256]{1,0:T(2,128)} %get-tuple-element.1523) | copy-start | bytes 6148
  2421.4 107.9 %copy-start.101 = (f32[1024]{0:T(1024)S(1)}, f32[1024]{0:T(1024)}, u32[]{:S(2)}) copy-start(f32[1024]{0:T(1024)} %copy-done.100) | copy-start | bytes 12292
  (117 other events, 686.0 us)
Sparse Core Ops, SparseCore 0:
  9.9 40.1 all-gather.10
  52.2 115.3 all-gather.12
  169.2 44.1 all-gather.14
  725.2 71.5 reduce-scatter.12
  799.5 55.9 all-gather.16
  857.0 58.0 all-gather.18
  916.7 56.7 all-gather.20
  975.2 56.7 all-gather.22
  1034.0 36.1 all-gather.24
  1090.2 71.2 reduce-scatter.16
  1163.4 55.9 all-gather.26
  1898.2 72.4 reduce-scatter.18
  1974.5 71.2 reduce-scatter.14
  2051.2 122.3 all-reduce.19
  2176.4 26.1 reduce-scatter.30
  2204.9 210.5 reduce-scatter.20
  2417.3 56.9 all-gather.28
  2477.2 101.1 reduce-scatter.24
  2581.4 100.5 reduce-scatter.26
  2684.9 100.6 reduce-scatter.28
  2788.5 77.2 reduce-scatter.22
where the time goes:
time: 2890 us; the launch traced here: 2870 us
  waiting for transfers between devices  1440 us (50%)
  matrix products  771 us (27%)
  other arithmetic  291 us (10%)
  local copies, waits for them, and re-layouts  270 us (9%)
  blocking collectives  58.6 us (2%)
    dot_general x390, matrix products, matmul(): return jnp.dot(left_mat, right_mat, precision=lax.Precision.HIGHEST)  607 us
    reduce_scatter x4, waiting for transfers between devices, share_sum(): lax.psum_scatter(partial_value, 'mp', scatter_dimension=1, tiled=True)  215 us
    reduce_scatter x1, waiting for transfers between devices, shards(): lax.psum_scatter(grad_mixer_local, 'seq', scatter_dimension=0, tiled=True)  211 us
    all_gather x3, waiting for transfers between devices, full_of(): return lax.all_gather(share, 'mp', axis=1, tiled=True)  164 us
    another operation x4, other arithmetic, solve_lower(): lax.linalg.triangular_solve(system, right_side, left_side=True, lower=Tru...  158 us
    psum x1, waiting for transfers between devices, shards(): lax.psum((widen(attn_gain_share, col_start, model_width, 0), widen(ffn_ga...  124 us
    all_gather x1, waiting for transfers between devices, shards(): lax.all_gather(w_mixer, 'seq', axis=0, tiled=True)  111 us
    reduce_scatter x1, waiting for transfers between devices, shards(): lax.psum_scatter(grad_up_local, 'seq', scatter_dimension=0, tiled=True)  104 us
  transfers between devices with their start and end apart: 29, of which 26 were waited for; matrix products, arithmetic and copies ran while one was open for 23% of the time, Pallas kernels for 0%

commit v1 on v0

v1 whole, which is shorter than its diff:
```python
import functools
import jax
import jax.numpy as jnp
from jax import lax
from jax.experimental import pallas as pl
from jax.experimental.pallas import tpu as pltpu
from jax.sharding import PartitionSpec as P

DK = 128
DV = 256
CHUNK = 128
GATE_LANES = 8
F32 = jnp.float32
BF16 = jnp.bfloat16
NN = (((1,), (0,)), ((), ()))
NT = (((1,), (1,)), ((), ()))
VMEM_LIMIT = 48 * 1024 * 1024


def d1(left, right, dims=NN):
    return lax.dot_general(
        left.astype(BF16), right.astype(BF16), dims, preferred_element_type=F32
    )


def dx(left, right, dims=NN):
    if left.dtype == BF16 and right.dtype == BF16:
        return d1(left, right, dims)
    return d3(left.astype(F32), right.astype(F32), dims)


def split(value):
    high = value.astype(BF16)
    return high, (value - high.astype(F32)).astype(BF16)


def d3(left, right, dims=NN):
    lh, ll = split(left)
    rh, rl = split(right)
    return d1(lh, rh, dims) + (d1(lh, rl, dims) + d1(ll, rh, dims))


def params():
    return pltpu.CompilerParams(vmem_limit_bytes=VMEM_LIMIT)


def cost(flops, nbytes):
    return pl.CostEstimate(flops=int(flops), bytes_accessed=int(nbytes), transcendentals=0)


def spec(shape, index_map):
    return pl.BlockSpec(shape, index_map)


def rows_cols():
    row = lax.broadcasted_iota(jnp.int32, (CHUNK, CHUNK), 0)
    col = lax.broadcasted_iota(jnp.int32, (CHUNK, CHUNK), 1)
    return row, col


def to_row(column, row, col):
    return jnp.sum(jnp.where(row == col, column, 0.0), axis=0, keepdims=True)


def to_col(line, row, col):
    return jnp.sum(jnp.where(row == col, line, 0.0), axis=1, keepdims=True)


def decay_parts(gates, row, col):
    log_decay, beta, ids, prior = (gates[:, i : i + 1] for i in range(4))
    cum_row = jnp.sum(jnp.where(row <= col, log_decay, 0.0), axis=0, keepdims=True)
    cum_col = to_col(cum_row, row, col)
    same = ids == to_row(ids, row, col)
    inside = (row >= col) & same
    decays = jnp.where(inside, jnp.exp(jnp.where(inside, cum_col - cum_row, 0.0)), 0.0)
    carried = jnp.where(ids == prior, jnp.exp(cum_col), 0.0)
    last_ids = ids[CHUNK - 1 : CHUNK]
    last_cum = cum_col[CHUNK - 1 : CHUNK]
    to_end = jnp.where(ids == last_ids, jnp.exp(last_cum - cum_col), 0.0)
    return beta, decays, carried, to_end


def invert(lowers, row, col):
    eye = jnp.where(row == col, 1.0, 0.0)
    found = None
    shift = 0
    while (1 << shift) < CHUNK:
        mask = ((row >> (shift + 1)) == (col >> (shift + 1))) & (
            (row >> shift) > (col >> shift)
        )
        masked = [jnp.where(mask, lower, 0.0) for lower in lowers]
        if found is None:
            found = [eye - m for m in masked]
        else:
            low = [x.astype(BF16) for x in found]
            inner = [d1(m, x) for m, x in zip(masked, low)]
            outer = [d1(x, y) for x, y in zip(low, inner)]
            found = [x - y for x, y in zip(found, outer)]
        shift += 1
    rest = [d3(lower, x) for lower, x in zip(lowers, found)]
    rest = [(eye - x) - r for x, r in zip(found, rest)]
    return [x + d1(x, r) for x, r in zip(found, rest)]


def prep_kernel(
    group, qk_ref, gt_ref, t_ref, tt_ref, a_ref, at_ref, lk_ref, w_ref, p_ref, pt_ref, m_ref, mt_ref
):
    row, col = rows_cols()
    queries, keys, parts = [], [], []
    for c in range(group):
        block = qk_ref[c * CHUNK : (c + 1) * CHUNK, :]
        queries.append(block[:, :DK])
        keys.append(block[:, DK:])
        parts.append(decay_parts(gt_ref[0, c * CHUNK : (c + 1) * CHUNK, :], row, col))
    gram = [d3(k, k, NT) for k in keys]
    scores = [dx(q, k, NT) for q, k in zip(queries, keys)]
    kept = [jnp.where(row > col, p[1] * g, 0.0) for p, g in zip(parts, gram)]
    lowers = [x * p[0] for x, p in zip(kept, parts)]
    inverses = invert(lowers, row, col)
    eye = jnp.where(row == col, 1.0, 0.0)
    for c in range(group):
        beta, decays, carried, to_end = parts[c]
        inverse = inverses[c]
        t_ref[0, c] = inverse
        tt_ref[0, c] = inverses[c].T
        score = decays * scores[c]
        a_ref[0, c] = score
        at_ref[0, c] = score.T
        lk_ref[0, c] = kept[c]
        wkeys = dx(inverse, (beta * carried) * keys[c])
        w_ref[0, c] = wkeys
        reach = carried * queries[c] - dx(score, wkeys)
        p_ref[0, c] = reach
        pt_ref[0, c] = reach.T
        end_keys = to_end * keys[c]
        step = carried[CHUNK - 1 : CHUNK] * eye - dx(end_keys.T, wkeys)
        m_ref[0, c] = step
        mt_ref[0, c] = step.T


def delta_prep(qk, gates):
    heads, tokens, _ = gates.shape
    count = tokens // CHUNK
    group = min(4, count)
    rows = group * CHUNK
    low = jax.ShapeDtypeStruct((heads, count, CHUNK, CHUNK), F32)
    wide = jax.ShapeDtypeStruct((heads, count, DK, DK), F32)
    out_spec = spec((1, group, CHUNK, CHUNK), lambda h, g: (h, g, 0, 0))
    return pl.pallas_call(
        functools.partial(prep_kernel, group),
        grid=(heads, count // group),
        in_specs=[
            spec((rows, 2 * DK), lambda h, g: (g, 2 * h)),
            spec((1, rows, GATE_LANES), lambda h, g: (h, g, 0)),
        ],
        out_specs=[out_spec] * 10,
        out_shape=[low] * 8 + [wide] * 2,
        compiler_params=params(),
        cost_estimate=cost(heads * count * 40 * 2 * CHUNK**3 * 8, heads * count * CHUNK * CHUNK * 24),
        name="delta_prep",
    )(qk, gates)


def trans_kernel(heads, count, m_ref, mt_ref, fwd_ref, back_ref):
    row, col = rows_cols()
    eye = jnp.where(row == col, 1.0, 0.0)
    fwd = [eye] * heads
    back = [eye] * heads
    for h in range(heads):
        fwd_ref[h, 0] = eye
        back_ref[h, count] = eye
    for c in range(count):
        if c == 0:
            fwd = [m_ref[h, 0] for h in range(heads)]
            back = [mt_ref[h, count - 1] for h in range(heads)]
        else:
            fwd = [d3(m_ref[h, c], fwd[h]) for h in range(heads)]
            back = [d3(mt_ref[h, count - 1 - c], back[h]) for h in range(heads)]
        for h in range(heads):
            fwd_ref[h, c + 1] = fwd[h]
            back_ref[h, count - 1 - c] = back[h]


def delta_trans(steps, steps_turned):
    heads, count = steps.shape[:2]
    shape = jax.ShapeDtypeStruct((heads, count + 1, DK, DK), F32)
    return pl.pallas_call(
        functools.partial(trans_kernel, heads, count),
        out_shape=[shape, shape],
        compiler_params=params(),
        cost_estimate=cost(heads * count * 6 * 2 * DK**3 * 8, heads * count * DK * DK * 16),
        name="delta_trans",
    )(steps, steps_turned)


def values_kernel(
    heads, group, qkv_ref, gt_ref, t_ref, a_ref, m_ref, ut_ref, o_ref, s_ref, end_ref, state
):
    @pl.when(pl.program_id(0) == 0)
    def _():
        state[...] = jnp.zeros_like(state)

    row, col = rows_cols()
    pairs = [(h, c) for c in range(group) for h in range(heads)]
    offsets = {}
    for h, c in pairs:
        at = slice(c * CHUNK, (c + 1) * CHUNK)
        beta, _, _, to_end = decay_parts(gt_ref[h, at, :], row, col)
        pseudo = dx(t_ref[h, c], beta * qkv_ref[at, (2 * h + 1) * DV : (2 * h + 2) * DV])
        ut_ref[h, c] = pseudo
        o_ref[at, h * DV : (h + 1) * DV] = dx(a_ref[h, c], pseudo)
        end_keys = to_end * qkv_ref[at, (4 * h + 1) * DK : (4 * h + 2) * DK]
        offsets[h, c] = dx(end_keys.T, pseudo)
    held = [state[h] for h in range(heads)]
    for c in range(group):
        for h in range(heads):
            s_ref[h, c] = held[h]
        held = [d3(m_ref[h, c], held[h]) + offsets[h, c] for h in range(heads)]
    for h in range(heads):
        state[h] = held[h]
        end_ref[h] = held[h]


def delta_values(qkv, gates, inverse, scores, steps):
    heads, tokens, _ = gates.shape
    count = tokens // CHUNK
    group = min(4, count)
    rows = group * CHUNK
    square = spec((heads, group, CHUNK, CHUNK), lambda g: (0, g, 0, 0))
    tall = spec((heads, group, CHUNK, DV), lambda g: (0, g, 0, 0))
    return pl.pallas_call(
        functools.partial(values_kernel, heads, group),
        grid=(count // group,),
        in_specs=[
            spec((rows, heads * 2 * DV), lambda g: (g, 0)),
            spec((heads, rows, GATE_LANES), lambda g: (0, g, 0)),
            square,
            square,
            square,
        ],
        out_specs=[
            tall,
            spec((rows, heads * DV), lambda g: (g, 0)),
            tall,
            spec((heads, DK, DV), lambda g: (0, 0, 0)),
        ],
        out_shape=[
            jax.ShapeDtypeStruct((heads, count, CHUNK, DV), F32),
            jax.ShapeDtypeStruct((tokens, heads * DV), F32),
            jax.ShapeDtypeStruct((heads, count, DK, DV), F32),
            jax.ShapeDtypeStruct((heads, DK, DV), F32),
        ],
        scratch_shapes=[pltpu.VMEM((heads, DK, DV), F32)],
        compiler_params=params(),
        cost_estimate=cost(heads * count * 12 * 2 * CHUNK**3 * 8, heads * count * CHUNK * 4000),
        name="delta_values",
    )(qkv, gates, inverse, scores, steps)


def output_kernel(
    heads, group, start_ref, s0_ref, tc_ref, p_ref, w_ref, ut_ref, o0_ref, gain_ref, *refs
):
    g_refs, (mixed_ref, o_ref, s_ref, u_ref) = refs[:heads], refs[heads:]
    for c in range(group):
        for h in range(heads):
            at = slice(c * CHUNK, (c + 1) * CHUNK)
            cols = slice(h * DV, (h + 1) * DV)
            held = s0_ref[h, c] + d3(tc_ref[h, c], start_ref[h])
            low = held
            s_ref[h, c] = low
            u_ref[h, c] = (ut_ref[h, c].astype(F32) - dx(w_ref[h, c], low))
            out = o0_ref[at, cols] + dx(p_ref[h, c], low)
            o_ref[at, cols] = out
            gate = g_refs[h][at, :]
            inv = lax.rsqrt(jnp.mean(out * out, axis=-1, keepdims=True) + 1e-05)
            mixed = out * inv * gain_ref[h : h + 1, :] * (gate * jax.nn.sigmoid(gate))
            mixed_ref[at, cols] = mixed.astype(BF16)


def gate_specs(heads, rows, place):
    return [
        spec((rows, DV), functools.partial(lambda h, g: (place(g), 3 * h + 2), h))
        for h in range(heads)
    ]


def delta_output(start, states, trans, reach, wkeys, pseudo, local_out, raw, gain):
    heads, count = states.shape[:2]
    tokens = count * CHUNK
    group = min(2, count)
    rows = group * CHUNK
    square = spec((heads, group, CHUNK, CHUNK), lambda g: (0, g, 0, 0))
    tall = spec((heads, group, CHUNK, DV), lambda g: (0, g, 0, 0))
    flat = spec((rows, heads * DV), lambda g: (g, 0))
    low = jax.ShapeDtypeStruct((heads, count, CHUNK, DV), F32)
    return pl.pallas_call(
        functools.partial(output_kernel, heads, group),
        grid=(count // group,),
        in_specs=[
            spec((heads, DK, DV), lambda g: (0, 0, 0)),
            tall,
            square,
            square,
            square,
            tall,
            flat,
            spec((heads, DV), lambda g: (0, 0)),
        ]
        + gate_specs(heads, rows, lambda g: g),
        out_specs=[flat, flat, tall, tall],
        out_shape=[
            jax.ShapeDtypeStruct((tokens, heads * DV), BF16),
            jax.ShapeDtypeStruct((tokens, heads * DV), F32),
            low,
            low,
        ],
        compiler_params=params(),
        cost_estimate=cost(heads * count * 10 * 2 * CHUNK**3 * 8, heads * count * CHUNK * 6000),
        name="delta_output",
    )(start, states, trans, reach, wkeys, pseudo, local_out, gain, *([raw] * heads))


def tail_kernel(
    heads, group, dm_ref, o_ref, gain_ref, pt_ref, mt_ref, *refs
):
    g_refs = refs[:heads]
    do_ref, dg_ref, dgain_ref, ds_ref, dstart_ref, state = refs[heads:]

    @pl.when(pl.program_id(0) == 0)
    def _():
        state[...] = jnp.zeros_like(state)
        dgain_ref[...] = jnp.zeros_like(dgain_ref)

    pushed = {}
    for c in range(group):
        for h in range(heads):
            at = slice(c * CHUNK, (c + 1) * CHUNK)
            cols = slice(h * DV, (h + 1) * DV)
            out = o_ref[at, cols]
            gate = g_refs[h][at, :]
            back = dm_ref[at, cols]
            gain = gain_ref[h : h + 1, :]
            sig = jax.nn.sigmoid(gate)
            silu = gate * sig
            inv = lax.rsqrt(jnp.mean(out * out, axis=-1, keepdims=True) + 1e-05)
            hat = out * inv
            dgain_ref[h : h + 1, :] += jnp.sum(back * hat * silu, axis=0, keepdims=True)
            scaled = back * gain
            dg_ref[at, cols] = (scaled * hat * (sig * (1.0 + gate * (1.0 - sig)))).astype(BF16)
            dhat = scaled * silu
            dout = inv * (dhat - hat * jnp.mean(dhat * hat, axis=-1, keepdims=True))
            low = dout
            do_ref[at, cols] = low
            pushed[h, c] = dx(pt_ref[h, c], low)
    held = [state[h] for h in range(heads)]
    for c in reversed(range(group)):
        for h in range(heads):
            ds_ref[h, c] = held[h]
        held = [d3(mt_ref[h, c], held[h]) + pushed[h, c] for h in range(heads)]
    for h in range(heads):
        state[h] = held[h]
        dstart_ref[h] = held[h]


def delta_tail(grad_mixed, outs, raw, gain, reach_turned, steps_turned):
    heads, count = steps_turned.shape[:2]
    tokens = count * CHUNK
    group = min(2, count)
    rows = group * CHUNK
    last = count // group - 1
    square = spec((heads, group, CHUNK, CHUNK), lambda g: (0, last - g, 0, 0))
    tall = spec((heads, group, CHUNK, DV), lambda g: (0, last - g, 0, 0))
    flat = spec((rows, heads * DV), lambda g: (last - g, 0))
    return pl.pallas_call(
        functools.partial(tail_kernel, heads, group),
        grid=(count // group,),
        in_specs=[flat, flat, spec((heads, DV), lambda g: (0, 0)), square, square]
        + gate_specs(heads, rows, lambda g: last - g),
        out_specs=[
            flat,
            flat,
            spec((heads, DV), lambda g: (0, 0)),
            tall,
            spec((heads, DK, DV), lambda g: (0, 0, 0)),
        ],
        out_shape=[
            jax.ShapeDtypeStruct((tokens, heads * DV), F32),
            jax.ShapeDtypeStruct((tokens, heads * DV), BF16),
            jax.ShapeDtypeStruct((heads, DV), F32),
            jax.ShapeDtypeStruct((heads, count, DK, DV), F32),
            jax.ShapeDtypeStruct((heads, DK, DV), F32),
        ],
        scratch_shapes=[pltpu.VMEM((heads, DK, DV), F32)],
        compiler_params=params(),
        cost_estimate=cost(heads * count * 10 * 2 * CHUNK**3 * 8, heads * count * CHUNK * 6000),
        name="delta_tail",
    )(grad_mixed, outs, gain, reach_turned, steps_turned, *([raw] * heads))


def grads_kernel(
    heads, group, end_ref, qkv_ref, gt_ref, tt_ref, a_ref, at_ref, lk_ref, u_ref, s_ref,
    ds_ref, back_ref, do_ref, dqkv_ref, dgt_ref,
):
    row, col = rows_cols()
    lane = lax.broadcasted_iota(jnp.int32, (CHUNK, GATE_LANES), 1)
    pairs = [(h, c) for c in range(group) for h in range(heads)]
    at = {(h, c): slice(c * CHUNK, (c + 1) * CHUNK) for h, c in pairs}
    parts = {(h, c): decay_parts(gt_ref[h, at[h, c], :], row, col) for h, c in pairs}
    keys = {(h, c): qkv_ref[at[h, c], (4 * h + 1) * DK : (4 * h + 2) * DK] for h, c in pairs}
    queries = {(h, c): qkv_ref[at[h, c], 4 * h * DK : (4 * h + 1) * DK] for h, c in pairs}
    vals = {(h, c): qkv_ref[at[h, c], (2 * h + 1) * DV : (2 * h + 2) * DV] for h, c in pairs}
    douts = {(h, c): do_ref[at[h, c], h * DV : (h + 1) * DV] for h, c in pairs}
    after = {(h, c): ds_ref[h, c] + d3(back_ref[h, c], end_ref[h]) for h, c in pairs}
    after_low = {p: after[p] for p in pairs}
    du = {
        (h, c): dx(at_ref[h, c], douts[h, c])
        + dx(parts[h, c][3] * keys[h, c], after_low[h, c])
        for h, c in pairs
    }
    x = {(h, c): dx(tt_ref[h, c], du[h, c]) for h, c in pairs}
    x_low = {p: x[p] for p in pairs}
    y = {(h, c): -dx(x_low[h, c], s_ref[h, c], NT) for h, c in pairs}
    da = {(h, c): dx(douts[h, c], u_ref[h, c], NT) for h, c in pairs}
    dqd = {(h, c): dx(douts[h, c], s_ref[h, c], NT) for h, c in pairs}
    dke = {(h, c): dx(u_ref[h, c], after_low[h, c], NT) for h, c in pairs}
    dl = {(h, c): dx(x_low[h, c], u_ref[h, c], NT) for h, c in pairs}
    for h, c in pairs:
        p = (h, c)
        beta, decays, carried, to_end = parts[p]
        key, query = keys[p], queries[p]
        kept = lk_ref[h, c].astype(F32)
        low_grad = jnp.where(row > col, -dl[p], 0.0)
        dg = jnp.sum(s_ref[h, c].astype(F32) * after[p], axis=0, keepdims=True)
        dg = jnp.sum(dg, axis=1, keepdims=True)
        yk = jnp.sum(y[p] * key, axis=-1, keepdims=True)
        dbeta = jnp.sum(x[p] * vals[p], axis=-1, keepdims=True) + carried * yk
        dbeta = dbeta + jnp.sum(low_grad * kept, axis=-1, keepdims=True)
        dcarried = beta * yk + jnp.sum(dqd[p] * query, axis=-1, keepdims=True)
        dend = jnp.sum(dke[p] * key, axis=-1, keepdims=True) * to_end
        scaled = low_grad * beta
        gram = scaled * decays
        score = da[p] * decays
        dqkv_ref[at[p], (2 * h + 1) * DV : (2 * h + 2) * DV] = beta * x[p]
        dqkv_ref[at[p], 4 * h * DK : (4 * h + 1) * DK] = carried * dqd[p] + dx(score, key)
        dqkv_ref[at[p], (4 * h + 1) * DK : (4 * h + 2) * DK] = (
            (beta * carried) * y[p]
            + to_end * dke[p]
            + dx(gram + gram.T, key)
            + dx(score.T, query)
        )
        spread = scaled * kept + da[p] * a_ref[h, c].astype(F32)
        dcum = jnp.sum(spread, axis=-1, keepdims=True)
        dcum = dcum - to_col(jnp.sum(spread, axis=0, keepdims=True), row, col)
        dcum = dcum - dend + dcarried * carried
        tail = jnp.sum(dend, axis=0, keepdims=True) + dg * carried[CHUNK - 1 : CHUNK]
        line = jnp.sum(jnp.where(row >= col, dcum, 0.0), axis=0, keepdims=True) + tail
        dlog = to_col(line, row, col)
        dgt_ref[h, at[p], :] = jnp.where(lane == 0, dlog, jnp.where(lane == 1, dbeta, 0.0))


def delta_grads(grad_end, qkv, gates, inv_turned, scores, scores_turned, kept, u, s, ds, back, dout):
    heads, tokens, _ = gates.shape
    count = tokens // CHUNK
    group = min(2, count)
    rows = group * CHUNK
    square = spec((heads, group, CHUNK, CHUNK), lambda g: (0, g, 0, 0))
    tall = spec((heads, group, CHUNK, DV), lambda g: (0, g, 0, 0))
    flat = spec((rows, heads * DV), lambda g: (g, 0))
    gate_spec = spec((heads, rows, GATE_LANES), lambda g: (0, g, 0))
    wide = spec((rows, heads * 2 * DV), lambda g: (g, 0))
    return pl.pallas_call(
        functools.partial(grads_kernel, heads, group),
        grid=(count // group,),
        in_specs=[
            spec((heads, DK, DV), lambda g: (0, 0, 0)),
            wide,
            gate_spec,
            square,
            square,
            square,
            square,
            tall,
            tall,
            tall,
            square,
            flat,
        ],
        out_specs=[wide, gate_spec],
        out_shape=[
            jax.ShapeDtypeStruct((tokens, heads * 2 * DV), F32),
            jax.ShapeDtypeStruct((heads, tokens, GATE_LANES), F32),
        ],
        compiler_params=params(),
        cost_estimate=cost(heads * count * 30 * 2 * CHUNK**3 * 8, heads * count * CHUNK * 12000),
        name="delta_grads",
    )(grad_end, qkv, gates, inv_turned, scores, scores_turned, kept, u, s, ds, back, dout)


def front_act(x, rim, mask_ref, taps, tokens):
    extended = jnp.concatenate([rim, x], axis=0)
    lags = [x]
    for lag in range(1, 4):
        moved = pltpu.roll(extended, lag, 0)[8:]
        lags.append(moved * mask_ref[:, 3 + lag : 4 + lag])
    conv = taps[0:1] * lags[0]
    for lag in range(1, 4):
        conv = conv + taps[lag : lag + 1] * lags[lag]
    return conv, lags


def front_kernel(x_ref, rim_ref, mask_ref, taps_ref, y_ref):
    tokens = x_ref.shape[0]
    conv, _ = front_act(x_ref[...], rim_ref[...], mask_ref, taps_ref[...], tokens)
    act = conv * jax.nn.sigmoid(conv)
    kind = pl.program_id(0) & 3

    @pl.when(kind < 2)
    def _():
        inv = lax.rsqrt(jnp.sum(act * act, axis=-1, keepdims=True) + 1e-06)
        y_ref[...] = act * (inv * jnp.where(kind == 0, DK**-0.5, 1.0))

    @pl.when(kind >= 2)
    def _():
        y_ref[...] = act


def raw_block(c):
    return (c >> 2) * 6 + (c & 3)


def front(raw, rim, masks, taps):
    tokens, cols = raw.shape[0], taps.shape[1]
    block = spec((tokens, DK), lambda c: (0, c))
    return pl.pallas_call(
        front_kernel,
        grid=(cols // DK,),
        in_specs=[
            spec((tokens, DK), lambda c: (0, raw_block(c))),
            spec((8, DK), lambda c: (0, raw_block(c))),
            spec((tokens, 8), lambda c: (0, 0)),
            spec((4, DK), lambda c: (0, c)),
        ],
        out_specs=block,
        out_shape=jax.ShapeDtypeStruct((tokens, cols), F32),
        compiler_params=params(),
        cost_estimate=cost(tokens * cols * 40, tokens * cols * 8),
        name="front",
    )(raw, rim, masks, taps)


def front_back_kernel(
    x_ref, rim_ref, mask_ref, taps_ref, dy_ref, dg_ref, dx_ref, edge_ref, drim_ref, dtaps_ref
):
    tokens = x_ref.shape[0]
    kind = lax.rem(pl.program_id(0), 6)

    @pl.when(kind >= 4)
    def _():
        grad = dg_ref[...]
        dx_ref[...] = grad
        edge_ref[...] = grad[tokens - 16 :].astype(F32)
        drim_ref[...] = jnp.zeros((8, DK), F32)
        dtaps_ref[...] = jnp.zeros((4, DK), F32)

    def through(normalize):
        taps = taps_ref[...]
        conv, lags = front_act(x_ref[...], rim_ref[...], mask_ref, taps, tokens)
        sig = jax.nn.sigmoid(conv)
        back = dy_ref[...]
        if normalize:
            act = conv * sig
            inv = lax.rsqrt(jnp.sum(act * act, axis=-1, keepdims=True) + 1e-06)
            unit = act * inv
            back = back * jnp.where(kind == 0, DK**-0.5, 1.0)
            back = inv * (back - unit * jnp.sum(back * unit, axis=-1, keepdims=True))
        dconv = back * (sig * (1.0 + conv * (1.0 - sig)))
        zeros = jnp.zeros((8, DK), F32)
        total = jnp.concatenate([zeros, taps[0:1] * dconv], axis=0)
        for lag in range(4):
            dtaps_ref[lag : lag + 1, :] = jnp.sum(dconv * lags[lag], axis=0, keepdims=True)
            if lag:
                part = (taps[lag : lag + 1] * dconv) * mask_ref[:, 3 + lag : 4 + lag]
                part = jnp.concatenate([zeros, part], axis=0)
                total = total + pltpu.roll(part, tokens + 8 - lag, 0)
        drim_ref[...] = total[:8]
        dx_ref[...] = total[8:].astype(BF16)
        edge_ref[...] = total[tokens - 8 :]

    @pl.when(kind < 2)
    def _():
        through(True)

    @pl.when((kind >= 2) & (kind < 4))
    def _():
        through(False)


def act_block(c):
    return lax.div(c, 6) * 4 + jnp.minimum(lax.rem(c, 6), 3)


def gate_block(c):
    return lax.div(c, 6) * 2 + jnp.maximum(lax.rem(c, 6) - 4, 0)


def front_back(raw, rim, masks, taps, dqkv, dg):
    tokens, cols = raw.shape
    block = spec((tokens, DK), lambda c: (0, c))
    return pl.pallas_call(
        front_back_kernel,
        grid=(cols // DK,),
        in_specs=[
            block,
            spec((8, DK), lambda c: (0, c)),
            spec((tokens, 8), lambda c: (0, 0)),
            spec((4, DK), lambda c: (0, act_block(c))),
            spec((tokens, DK), lambda c: (0, act_block(c))),
            spec((tokens, DK), lambda c: (0, gate_block(c))),
        ],
        out_specs=[
            block,
            spec((16, DK), lambda c: (0, c)),
            spec((8, DK), lambda c: (0, c)),
            spec((4, DK), lambda c: (0, c)),
        ],
        out_shape=[
            jax.ShapeDtypeStruct((tokens, cols), BF16),
            jax.ShapeDtypeStruct((16, cols), F32),
            jax.ShapeDtypeStruct((8, cols), F32),
            jax.ShapeDtypeStruct((4, cols), F32),
        ],
        compiler_params=params(),
        cost_estimate=cost(tokens * cols * 80, tokens * cols * 10),
        name="front_back",
    )(raw, rim, masks, taps, dqkv, dg)


def flip(value, bit):
    count = lax.axis_size("mp")
    return lax.ppermute(value, "mp", [(i, i ^ (1 << bit)) for i in range(count)])


def bit_count():
    return lax.axis_size("mp").bit_length() - 1


def exchange(values, bits):
    values = lax.optimization_barrier(tuple(values))
    return lax.optimization_barrier(tuple(flip(v, b) for v, b in zip(values, bits)))


def gather_mp(share):
    bits = bit_count()
    half = share.shape[0] // 2
    orders = (list(range(bits - 1, 0, -1)), list(range(1, bits)))
    held = [share[w * half : (w + 1) * half][None] for w in range(2)]
    rels = [[0], [0]]
    for turn in range(bits - 1):
        now = [order[turn] for order in orders]
        got = exchange(held, now)
        held = [jnp.concatenate([h, g], axis=0) for h, g in zip(held, got)]
        rels = [rel + [r | (1 << bit) for r in rel] for rel, bit in zip(rels, now)]
    got = exchange(held, [0, 0])
    return [(h, g, rel) for h, g, rel in zip(held, got, rels)]


def gathered_specs(found, tile, tiles):
    specs = []
    for which, (held, other, rel) in enumerate(found):
        shape = (held.shape[0], tile, held.shape[2])
        if which == 0:
            index = lambda i, m: (0, jnp.minimum(i, tiles - 1), 0)
        else:
            index = lambda i, m: (0, jnp.maximum(i - tiles, 0), 0)
        specs += [spec(shape, index)] * 2
    return specs


def gathered_args(found):
    return [x for held, other, rel in found for x in (held, other)]


def gathered_blocks(found, refs, which):
    held, other = refs[2 * which], refs[2 * which + 1]
    rel = found[which][2]
    blocks = [(r, held[i].astype(F32)) for i, r in enumerate(rel)]
    return blocks + [(r | 1, other[i].astype(F32)) for i, r in enumerate(rel)]


def place(mp_ref, r, cols):
    return pl.ds(pl.multiple_of((mp_ref[0] ^ r) * cols, cols), cols)


def norm_kernel(rels, cols, tiles, mode, *refs):
    mp_ref, refs = refs[0], refs[1:]
    found = [(None, None, rel) for rel in rels]
    if mode == "plain":
        out_ref = refs[4]
    else:
        gain_ref, out_ref, inv_ref = refs[4:7]
    for which in range(2):

        @pl.when((pl.program_id(0) < tiles) == (which == 0))
        def _():
            blocks = gathered_blocks(found, refs, which)
            if mode == "plain":
                for r, x in blocks:
                    out_ref[:, place(mp_ref, r, cols)] = x.astype(BF16)
                return
            total = sum(jnp.sum(x * x, axis=-1, keepdims=True) for _, x in blocks)
            inv = lax.rsqrt(total * (1.0 / (cols * len(blocks))) + 1e-05)
            for r, x in blocks:
                at = place(mp_ref, r, cols)
                out_ref[:, at] = (x * inv * gain_ref[:, at]).astype(BF16)
            inv_ref[...] = jnp.broadcast_to(inv, inv_ref.shape)


def assemble(found, mp_pos, gain=None):
    half, cols = found[0][0].shape[1:]
    rels = [f[2] for f in found]
    width = cols * 2 * len(rels[0])
    tokens = 2 * half
    tile = min(256, half)
    tiles = half // tile
    mode = "plain" if gain is None else "norm"
    row_spec = spec((tile, width), lambda i, m: (i, 0))
    in_specs = gathered_specs(found, tile, tiles)
    out_specs = [row_spec]
    out_shape = [jax.ShapeDtypeStruct((tokens, width), BF16)]
    args = gathered_args(found)
    if gain is not None:
        in_specs.append(spec((1, width), lambda i, m: (0, 0)))
        args.append(gain.reshape(1, width))
        out_specs.append(spec((tile, 128), lambda i, m: (i, 0)))
        out_shape.append(jax.ShapeDtypeStruct((tokens, 128), F32))
    return pl.pallas_call(
        functools.partial(norm_kernel, rels, cols, tiles, mode),
        grid_spec=pltpu.PrefetchScalarGridSpec(
            num_scalar_prefetch=1,
            grid=(2 * tiles,),
            in_specs=in_specs,
            out_specs=out_specs,
        ),
        out_shape=out_shape,
        compiler_params=params(),
        cost_estimate=cost(tokens * width * 10, tokens * width * 4),
        name="assemble",
    )(mp_pos.reshape(1).astype(jnp.int32), *args)


def norm_back_kernel(rels, cols, tiles, *refs):
    mp_ref, refs = refs[0], refs[1:]
    found = [(None, None, rel) for rel in rels]
    grads, mids = refs[:4], refs[4:8]
    up_ref, gain_ref, own_grad_ref, own_mid_ref, out_ref, own_out_ref, dgain_ref = refs[8:]

    @pl.when(pl.program_id(0) == 0)
    def _():
        dgain_ref[...] = jnp.zeros_like(dgain_ref)

    for which in range(2):

        @pl.when((pl.program_id(0) < tiles) == (which == 0))
        def _():
            grad = gathered_blocks(found, grads, which)
            mid = gathered_blocks(found, mids, which)
            scale = 1.0 / (cols * len(grad))
            total = sum(jnp.sum(x * x, axis=-1, keepdims=True) for _, x in mid)
            inv = lax.rsqrt(total * scale + 1e-05)
            scaled = [(r, g * gain_ref[:, place(mp_ref, r, cols)]) for r, g in grad]
            mean = sum(
                jnp.sum(g * x, axis=-1, keepdims=True) for (_, g), (_, x) in zip(scaled, mid)
            )
            shrink = inv * inv * (mean * scale)
            for (r, g), (_, x) in zip(scaled, mid):
                at = place(mp_ref, r, cols)
                out_ref[:, at] = (up_ref[:, at].astype(F32) + inv * (g - x * shrink)).astype(BF16)
            at = place(mp_ref, 0, cols)
            own_grad, own_mid = own_grad_ref[...], own_mid_ref[...]
            own_out_ref[...] = up_ref[:, at].astype(F32) + inv * (
                own_grad * gain_ref[:, at] - own_mid * shrink
            )
            dgain_ref[...] += jnp.sum(own_grad * own_mid * inv, axis=0, keepdims=True)


def norm_back(found_grad, found_mid, full_grad, gain, own_grad, own_mid, mp_pos):
    half, cols = found_grad[0][0].shape[1:]
    rels = [f[2] for f in found_grad]
    tokens, width = full_grad.shape
    tile = min(256, half)
    tiles = half // tile
    row_spec = spec((tile, width), lambda i, m: (i, 0))
    own_spec = spec((tile, cols), lambda i, m: (i, 0))
    return pl.pallas_call(
        functools.partial(norm_back_kernel, rels, cols, tiles),
        grid_spec=pltpu.PrefetchScalarGridSpec(
            num_scalar_prefetch=1,
            grid=(2 * tiles,),
            in_specs=gathered_specs(found_grad, tile, tiles)
            + gathered_specs(found_mid, tile, tiles)
            + [row_spec, spec((1, width), lambda i, m: (0, 0)), own_spec, own_spec],
            out_specs=[row_spec, own_spec, spec((1, cols), lambda i, m: (0, 0))],
        ),
        out_shape=[
            jax.ShapeDtypeStruct((tokens, width), BF16),
            jax.ShapeDtypeStruct((tokens, cols), F32),
            jax.ShapeDtypeStruct((1, cols), F32),
        ],
        compiler_params=params(),
        cost_estimate=cost(tokens * width * 20, tokens * width * 8),
        name="norm_back",
    )(
        mp_pos.reshape(1).astype(jnp.int32),
        *gathered_args(found_grad),
        *gathered_args(found_mid),
        full_grad,
        gain.reshape(1, width),
        own_grad,
        own_mid,
    )


def block_kernel(turns, mp_ref, *refs):
    out_ref = refs[2 * len(turns)]
    total = None
    for i, turned in enumerate(turns):
        part = d1(refs[2 * i][...], refs[2 * i + 1][...], NN if turned is False else NT)
        total = part if total is None else total + part
    out_ref[0] = total.astype(out_ref.dtype)


def right_index(parity, turned, g, m):
    at = (2 * g + parity) ^ m[0]
    return (at, 0) if turned else (0, at)


def spaced_index(parity, cols, rows, g, m):
    at = ((2 * g + parity) ^ m[0]) * cols
    return (pl.multiple_of(at + lax.div(at, rows) * 16, 16), 0)


def block_products(terms, mp_pos, cols, parity):
    tokens = terms[0][0].shape[0]
    count = lax.axis_size("mp") // 2
    in_specs, args, flops = [], [], 0
    for left, right, turned in terms:
        depth = left.shape[1]
        in_specs.append(spec((tokens, depth), lambda g, m: (0, 0)))
        if turned is None:
            rows = right.shape[0] // lax.axis_size("seq") - 16
            index = functools.partial(spaced_index, parity, cols, rows)
            in_specs.append(pl.BlockSpec((pl.Element(cols), pl.Element(depth)), index))
        else:
            index = functools.partial(right_index, parity, turned)
            in_specs.append(spec((cols, depth) if turned else (depth, cols), index))
        args += [left, right]
        flops += 2 * tokens * depth * cols * count
    return pl.pallas_call(
        functools.partial(block_kernel, [t[2] for t in terms]),
        grid_spec=pltpu.PrefetchScalarGridSpec(
            num_scalar_prefetch=1,
            grid=(count,),
            in_specs=in_specs,
            out_specs=spec((1, tokens, cols), lambda g, m: (g, 0, 0)),
        ),
        out_shape=jax.ShapeDtypeStruct((count, tokens, cols), BF16 if parity else F32),
        compiler_params=params(),
        cost_estimate=cost(flops, tokens * cols * count * 4),
        name="block_products",
    )(mp_pos.reshape(1).astype(jnp.int32), *args)


def reduce_mp(terms, mp_pos, cols):
    sent = flip(block_products(terms, mp_pos, cols, 1), 0)
    kept = block_products(terms, mp_pos, cols, 0)
    bits = bit_count()
    half = kept.shape[1] // 2
    orders = (list(range(1, bits)), list(range(bits - 1, 0, -1)))
    rels = [[2 * i for i in range(kept.shape[0])] for _ in orders]
    helds = []
    for which in range(2):
        at = slice(which * half, (which + 1) * half)
        helds.append({r: kept[i, at] + sent[i, at].astype(F32) for i, r in enumerate(rels[which])})
    for turn in range(bits - 1):
        aways = [[r for r in rels[w] if (r >> orders[w][turn]) & 1] for w in range(2)]
        gots = exchange(
            [jnp.stack([helds[w][r].astype(BF16) for r in aways[w]]) for w in range(2)],
            [orders[w][turn] for w in range(2)],
        )
        for w in range(2):
            bit = orders[w][turn]
            rels[w] = [r for r in rels[w] if not (r >> bit) & 1]
            helds[w] = {
                r: helds[w][r] + gots[w][aways[w].index(r | (1 << bit))].astype(F32) for r in rels[w]
            }
    return jnp.concatenate([helds[0][0], helds[1][0]], axis=0)


def sum_mp(value):
    for bit in range(bit_count()):
        value = value + flip(value, bit)
    return value


def sum_seq(value):
    count = lax.axis_size("seq")
    total = value
    for step in range(1, count):
        total = total + lax.ppermute(value, "seq", [(i, (i + step) % count) for i in range(count)])
    return total


def shifted(value, steps):
    count = lax.axis_size("seq")
    first, last = max(0, -steps), min(count, count - steps)
    return lax.ppermute(value, "seq", [(i, i + steps) for i in range(first, last)])


def batched(left, right):
    return jnp.einsum("hde,hev->hdv", left, right, precision=lax.Precision.HIGHEST)


def dot(left, right, dims=NN):
    return lax.dot_general(left, right, dims, preferred_element_type=F32)


TN = (((0,), (0,)), ((), ()))


def first_kernel(heads, count, rows, x_ref, w_ref, mask_ref, scale_ref, bias_ref, raw_ref, pre_ref, gate_ref):
    raw, pre = None, None
    for s in range(count):
        at = s * (rows + 16)
        part = x_ref[:, s * rows : (s + 1) * rows]
        left = d1(part, w_ref[at : at + rows, :])
        right = d1(part, w_ref[at + rows : at + rows + 16, :rows], NT)
        raw = left if raw is None else raw + left
        pre = right if pre is None else pre + right
    raw_ref[...] = raw
    pre_ref[...] = pre
    masks = mask_ref[...]
    lane = lax.broadcasted_iota(jnp.int32, masks.shape, 1)
    for h in range(heads):
        x = pre[:, 2 * h : 2 * h + 1] + bias_ref[h]
        soft = jnp.maximum(x, 0.0) + jnp.log1p(jnp.exp(-jnp.abs(x)))
        beta = jax.nn.sigmoid(pre[:, 2 * h + 1 : 2 * h + 2])
        gate_ref[h] = jnp.where(
            lane == 0, -scale_ref[h] * soft, jnp.where(lane == 1, beta, masks)
        )


def project_first(normed, mixer, masks, scale, bias):
    tokens, width = normed.shape
    count = lax.axis_size("seq")
    rows, cols = mixer.shape[0] // count - 16, mixer.shape[1]
    heads = scale.shape[0]
    tile = 256
    scalar = pl.BlockSpec(memory_space=pltpu.SMEM)
    return pl.pallas_call(
        functools.partial(first_kernel, heads, count, rows),
        grid=(tokens // tile,),
        in_specs=[
            spec((tile, width), lambda i: (i, 0)),
            spec(mixer.shape, lambda i: (0, 0)),
            spec((tile, 8), lambda i: (i, 0)),
            scalar,
            scalar,
        ],
        out_specs=[
            spec((tile, cols), lambda i: (i, 0)),
            spec((tile, 16), lambda i: (i, 0)),
            spec((heads, tile, 8), lambda i: (0, i, 0)),
        ],
        out_shape=[
            jax.ShapeDtypeStruct((tokens, cols), F32),
            jax.ShapeDtypeStruct((tokens, 16), F32),
            jax.ShapeDtypeStruct((heads, tokens, 8), F32),
        ],
        compiler_params=params(),
        cost_estimate=cost(2 * tokens * width * cols, tokens * width * 2 + width * cols * 2),
        name="project_first",
    )(normed, mixer, masks, scale, bias)


def gates_back_kernel(heads, pre_ref, dg_ref, scale_ref, bias_ref, low_ref, sums_ref):
    pre = pre_ref[...]
    lane = lax.broadcasted_iota(jnp.int32, pre.shape, 1)
    line = lax.broadcasted_iota(jnp.int32, (1, 128), 1)
    low = jnp.zeros(pre.shape, F32)
    for h in range(heads):
        x = pre[:, 2 * h : 2 * h + 1] + bias_ref[h]
        soft = jnp.maximum(x, 0.0) + jnp.log1p(jnp.exp(-jnp.abs(x)))
        beta = jax.nn.sigmoid(pre[:, 2 * h + 1 : 2 * h + 2])
        dlog = dg_ref[h][:, 0:1]
        dx = dlog * (-scale_ref[h] * jax.nn.sigmoid(x))
        db = dg_ref[h][:, 1:2] * (beta * (1.0 - beta))
        low = jnp.where(lane == 2 * h, dx, jnp.where(lane == 2 * h + 1, db, low))
        dscale = jnp.sum(-dlog * soft, axis=0, keepdims=True)
        dbias = jnp.sum(dx, axis=0, keepdims=True)
        sums_ref[h : h + 1, :] = jnp.where(line == 0, dscale, jnp.where(line == 1, dbias, 0.0))
    low_ref[...] = low.astype(BF16)


def gates_back(pre, dgates, scale, bias):
    tokens = pre.shape[0]
    heads = scale.shape[0]
    scalar = pl.BlockSpec(memory_space=pltpu.SMEM)
    whole = pl.BlockSpec(memory_space=pltpu.VMEM)
    return pl.pallas_call(
        functools.partial(gates_back_kernel, heads),
        in_specs=[whole, whole, scalar, scalar],
        out_specs=[whole, whole],
        out_shape=[
            jax.ShapeDtypeStruct((tokens, 16), BF16),
            jax.ShapeDtypeStruct((heads, 128), F32),
        ],
        compiler_params=params(),
        cost_estimate=cost(tokens * 1000, tokens * 1024),
        name="gates_back",
    )(pre, dgates, scale, bias)


def ffn_kernel(units, at, x_ref, dy_ref, gu_ref, down_ref, hid_ref, dgu_ref):
    x = x_ref[...]
    gate = d1(x, gu_ref[:, :units])
    up = d1(x, gu_ref[:, at : at + units])
    back = d1(dy_ref[...], down_ref[...], NT)
    sig = jax.nn.sigmoid(gate)
    silu = gate * sig
    hid_ref[...] = (silu * up).astype(BF16)
    dgu_ref[:, units:at] = jnp.zeros((x.shape[0], at - units), BF16)
    dgu_ref[:, :units] = (back * up * sig * (1.0 + gate * (1.0 - sig))).astype(BF16)
    dgu_ref[:, at : at + units] = (back * silu).astype(BF16)


def ffn(normed2, full_grad, gu_full, down_full):
    tokens, width = normed2.shape
    units = down_full.shape[0]
    both = gu_full.shape[1]
    tile = 256
    row_spec = spec((tile, width), lambda i: (i, 0))
    return pl.pallas_call(
        functools.partial(ffn_kernel, units, both - units),
        grid=(tokens // tile,),
        in_specs=[
            row_spec,
            row_spec,
            spec((width, both), lambda i: (0, 0)),
            spec((units, width), lambda i: (0, 0)),
        ],
        out_specs=[
            spec((tile, units), lambda i: (i, 0)),
            spec((tile, both), lambda i: (i, 0)),
        ],
        out_shape=[
            jax.ShapeDtypeStruct((tokens, units), BF16),
            jax.ShapeDtypeStruct((tokens, both), BF16),
        ],
        compiler_params=params(),
        cost_estimate=cost(6 * tokens * width * units, tokens * width * 4 + width * units * 6),
        name="ffn",
    )(normed2, full_grad, gu_full, down_full)


def after(value, *earlier):
    return lax.optimization_barrier((value, earlier))[0]


def ring_gather(value):
    pairs = [(shifted(value, 1), shifted(value, -1))]
    for _ in range(2, lax.axis_size("seq")):
        pairs.append((shifted(pairs[-1][0], 1), shifted(pairs[-1][1], -1)))
    return pairs


def together(*values):
    return lax.optimization_barrier(values)


def join_ring(own, pairs, axis):
    seq_count = lax.axis_size("seq")
    seq_pos = lax.axis_index("seq")
    size = own.shape[axis]
    shape = list(own.shape)
    shape[axis] = size * seq_count
    full = jnp.zeros(tuple(shape), own.dtype)
    full = lax.dynamic_update_slice_in_dim(full, own, seq_pos * size, axis)
    for j in range(1, seq_count):
        piece = jnp.where(seq_pos >= j, pairs[j - 1][0], pairs[seq_count - j - 1][1])
        at = lax.rem(seq_pos - j + seq_count, seq_count) * size
        full = lax.dynamic_update_slice_in_dim(full, piece, at, axis)
    return full


def chain(steps, ends, sign):
    total = shifted(ends.astype(BF16), sign).astype(F32)
    for _ in range(lax.axis_size("seq") - 2):
        total = shifted((batched(steps, total) + ends).astype(BF16), sign).astype(F32)
    return total


def scatter_seq(value, axis):
    return lax.psum_scatter(value, "seq", scatter_dimension=axis, tiled=True).astype(F32)


def shards(
    residual,
    attn_gain,
    w_mixer,
    w_gates,
    conv_taps,
    decay_scale,
    dt_bias,
    head_gain,
    w_out,
    ffn_gain,
    w_gate,
    w_up,
    w_down,
    out_grad,
    doc_ids,
):
    tokens, cols = residual.shape
    seq_count = lax.axis_size("seq")
    mp_count = lax.axis_size("mp")
    seq_pos = lax.axis_index("seq")
    mp_pos = lax.axis_index("mp")
    rows, heads = w_mixer.shape[:2]
    width = rows * seq_count

    padded = jnp.concatenate([jnp.full((3,), -1, jnp.int32), doc_ids])
    window = lax.dynamic_slice_in_dim(padded, seq_pos * tokens, tokens + 3)
    ids = window[3:]
    prior = jnp.repeat(window[2 : 2 + tokens].reshape(-1, CHUNK)[:, 0], CHUNK)
    same = [(window[3 - j : 3 - j + tokens] == ids).astype(F32) for j in range(1, 4)]
    ids_f, prior_f = ids.astype(F32), prior.astype(F32)
    zero = jnp.zeros((tokens,), F32)
    masks = jnp.stack([zero] * 2 + [ids_f, prior_f] + same + [zero], axis=1)

    units = w_gate.shape[1]
    spare = -units % 128
    mix_cols = heads * (2 * DK + 2 * DV)
    gate_part = jnp.pad(
        w_gates.reshape(rows, 2 * heads).T, ((0, 16 - 2 * heads), (0, mix_cols - rows))
    )
    mixer_part = jnp.concatenate([w_mixer.reshape(rows, mix_cols), gate_part])
    do_part = jnp.concatenate([w_out, w_down])
    gu_part = jnp.concatenate([w_gate, jnp.zeros((rows, spare), BF16), w_up], axis=1)
    mixer_full = lax.all_gather(mixer_part, "seq", axis=0, tiled=True)
    found_res = gather_mp(residual)
    do_full = lax.all_gather(after(do_part, found_res[0][0]), "seq", axis=1, tiled=True)

    normed, inv1 = assemble(found_res, mp_pos, attn_gain)
    gu_full = lax.all_gather(after(gu_part, normed), "seq", axis=0, tiled=True)
    found_og = gather_mp(after(out_grad, normed))
    full_grad = assemble(found_og, mp_pos)[0]
    mixer_full = after(mixer_full, full_grad)
    raw, gate_pre, gates = project_first(normed, mixer_full, masks, decay_scale, dt_bias)
    taps = conv_taps.reshape(4, heads * 2 * DV)
    rim = shifted(raw[tokens - 8 :], 1)
    qkv = front(raw, rim, masks, taps)

    inverse, inv_turned, scores, scores_turned, kept, wkeys, reach, reach_turned, steps, steps_turned = (
        delta_prep(qkv, gates)
    )
    trans, back = delta_trans(steps, steps_turned)
    pseudo, local_out, states, state_end = delta_values(qkv, gates, inverse, scores, steps)
    start = chain(trans[:, -1], state_end, 1)
    mixed, outs, held, corrected = delta_output(
        start, states, trans, reach, wkeys, pseudo, local_out, raw, head_gain
    )

    out_full, down_full = do_full[: w_out.shape[0]], do_full[w_out.shape[0] :]
    branch = reduce_mp([(mixed, out_full, False)], mp_pos, cols)
    middle = residual.astype(F32) + branch
    found_mid = gather_mp(middle.astype(BF16))
    normed2, _ = assemble(found_mid, mp_pos, ffn_gain)
    hidden, grad_gu = ffn(normed2, full_grad, gu_full, down_full)
    part_gu = dot(normed2, grad_gu, TN).astype(BF16)
    grad_normed2 = reduce_mp([(grad_gu, gu_full, True)], mp_pos, cols)
    dw_gu = lax.psum_scatter(part_gu, "seq", scatter_dimension=0, tiled=True)
    part_down = dot(hidden, full_grad, TN).astype(BF16)
    grad_normed2 = after(grad_normed2, part_gu)
    found_gn2 = gather_mp(grad_normed2.astype(BF16))

    grad_branch, grad_middle, dffn_gain = norm_back(
        found_gn2, found_mid, full_grad, ffn_gain, grad_normed2, middle, mp_pos
    )
    grad_mixed = dot(grad_branch, out_full, NT)
    part_out = dot(mixed, grad_branch, TN).astype(BF16)
    dw_do = lax.psum_scatter(
        jnp.concatenate([part_out, part_down]), "seq", scatter_dimension=1, tiled=True
    )
    ffn_part = reduce_mp([(after(hidden, grad_branch), down_full, False)], mp_pos, cols)
    output = (middle + ffn_part).astype(BF16)

    dout, dg_raw, dhead_gain, dstates, dstart = delta_tail(
        grad_mixed, outs, raw, head_gain, reach_turned, steps_turned
    )
    grad_end = chain(back[:, 0], dstart, -1)
    grad_end = after(grad_end, output, part_out)
    dqkv, dgates = delta_grads(
        grad_end, qkv, gates, inv_turned, scores, scores_turned, kept, corrected, held,
        dstates, back[:, 1:], dout,
    )
    dproj, edge, drim, dtaps = front_back(raw, rim, masks, taps, dqkv, dg_raw)
    edge = jnp.concatenate([edge[:8], edge[8:] + shifted(drim, -1)])
    dproj = lax.dynamic_update_slice_in_dim(dproj, edge.astype(BF16), tokens - 16, 0)
    dgate_low, gate_sums = gates_back(gate_pre, dgates, decay_scale, dt_bias)

    part_mixer = dot(normed, dproj, TN).astype(BF16)
    dw_mixer = lax.psum_scatter(part_mixer, "seq", scatter_dimension=0, tiled=True)
    part_gates = dot(dgate_low, normed, TN)
    gates_full = jnp.swapaxes(
        mixer_full.reshape(seq_count, rows + 16, mix_cols)[:, rows:, :rows], 0, 1
    ).reshape(16, width)
    grad_normed = reduce_mp(
        [(dproj, mixer_full, None), (dgate_low, gates_full, False)], mp_pos, cols
    )
    own_gain = lax.dynamic_slice_in_dim(attn_gain, mp_pos * cols, cols)
    own_res = residual.astype(F32)
    inv1 = inv1[:, :1]
    scaled = grad_normed * own_gain
    mean = jnp.sum(scaled * own_res, axis=-1).reshape(-1, 128)
    mean = sum_mp(mean).reshape(tokens, 1) * (1.0 / width)
    grad_residual = grad_middle + inv1 * (scaled - own_res * (inv1 * inv1 * mean))
    dattn_gain = jnp.sum(grad_normed * own_res * inv1, axis=0)

    dtaps = dtaps.reshape(4, heads, 2 * DK + 2 * DV)[:, :, : 2 * DK + DV]
    small = [
        dattn_gain, dffn_gain, dhead_gain, gate_sums[:, 0], gate_sums[:, 1], dtaps,
        part_gates[: 2 * heads],
    ]
    packed = jnp.concatenate([value.reshape(-1) for value in small])
    packed = jnp.pad(packed, (0, -packed.shape[0] % 1024)).reshape(-1, 128)
    packed = sum_seq(packed).reshape(-1)
    sums, at = [], 0
    for value in small:
        sums.append(packed[at : at + value.size].reshape(value.shape))
        at += value.size
    gains = jnp.stack([sums[0], sums[1].reshape(-1)])
    gains = lax.dynamic_update_slice(jnp.zeros((2, width), F32), gains, (0, mp_pos * cols))
    gains = sum_mp(gains)
    dw_gates = lax.dynamic_slice_in_dim(sums[6], seq_pos * rows, rows, 1)
    return (
        output,
        grad_residual,
        gains[0],
        dw_mixer.astype(F32).reshape(rows, heads, 2 * DK + 2 * DV),
        dw_gates.T.reshape(rows, heads, 2),
        sums[5],
        sums[3],
        sums[4],
        sums[2],
        dw_do[: w_out.shape[0]].astype(F32),
        gains[1],
        dw_gu[:, :units].astype(F32),
        dw_gu[:, units + spare :].astype(F32),
        dw_do[w_out.shape[0] :].astype(F32),
    )


def solution(mesh):
    in_specs = (
        P("seq", "mp"),
        P(),
        P("seq", "mp", None),
        P("seq", "mp", None),
        P(None, "mp", None),
        P("mp"),
        P("mp"),
        P("mp", None),
        P("mp", "seq"),
        P(),
        P("seq", "mp"),
        P("seq", "mp"),
        P("mp", "seq"),
        P("seq", "mp"),
        P(),
    )
    out_specs = (
        P("seq", "mp"),
        P("seq", "mp"),
        P(),
        P("seq", "mp", None),
        P("seq", "mp", None),
        P(None, "mp", None),
        P("mp"),
        P("mp"),
        P("mp", None),
        P("mp", "seq"),
        P(),
        P("seq", "mp"),
        P("seq", "mp"),
        P("mp", "seq"),
    )
    return jax.shard_map(shards, mesh=mesh, in_specs=in_specs, out_specs=out_specs, check_vma=False)
```

time: 2890 us -> 717 us (0.25)
  waiting for transfers between devices: 1440 us -> 321 us
  matrix products: 771 us -> 37.8 us
  other arithmetic: 291 us -> 34.6 us
  local copies, waits for them, and re-layouts: 270 us -> 40.3 us
  Pallas kernels: 0 us -> 181 us
  blocking collectives: 58.6 us -> 0 us
  starting transfers between devices: 20.9 us -> 77.9 us
    reduce_scatter x9 -> x3, waiting for transfers between devices: 759 us -> 26.9 us  [the longest x1 26.9 us: shards(): lax.psum_scatter(part_mixer, 'seq', scatter_dimension=0, tiled=True)]
    dot_general x417 -> x10, matrix products: 755 us -> 37.8 us  [the longest x6 36.7 us: dot(): return lax.dot_general(left, right, dims, preferred_element_type=F32)]
    all_gather x10 -> x3, waiting for transfers between devices: 489 us -> 95.8 us  [the longest x1 53 us: shards(): mixer_full = lax.all_gather(mixer_part, 'seq', axis=0, tiled=True)]
    pallas_call x0 -> x23, Pallas kernels: none -> 181 us  [the longest x8 38.2 us: block_products(): pl.pallas_call(functools.partial(block_kernel, [t[2] for t in terms]), gr...]
    ppermute x8 -> x61, waiting for transfers between devices: 39.1 us -> 198 us  [the longest x50 135 us: flip(): return lax.ppermute(value, 'mp', [(i, i ^ 1 << bit) for i in range(count)])]
    another operation x11 -> x10, other arithmetic: 159 us -> 0.51 us  [the longest x8 0.41 us: reduce_mp(): jnp.stack([helds[w][r].astype(BF16) for r in aways[w]])]
    dynamic_update_slice x148 -> x0, local copies, waits for them, and re-layouts: 142 us -> none  [the longest x64 72.2 us: per_head(): ignored, outputs = lax.scan(state_step, head_start, head_prep)]
    psum x1 -> x0, waiting for transfers between devices: 124 us -> none  [shards(): lax.psum((widen(attn_gain_share, col_start, model_width, 0), widen(ffn_ga...]
  transfers between devices with their start and end apart: 29 -> 67, of which waited for: 26 -> 52; matrix products, arithmetic and copies ran while one was open for 23% -> 11% of each run, Pallas kernels for 0% -> 23%
where the time goes in v1:
time: 717 us; the launch traced here: 709 us
  waiting for transfers between devices  321 us (45%)
  Pallas kernels  181 us (25%)
  starting transfers between devices  77.9 us (11%)
  local copies, waits for them, and re-layouts  40.3 us (6%)
  matrix products  37.8 us (5%)
  other arithmetic  34.6 us (5%)
  between operations  15.9 us (2%)
    ppermute x50, waiting for transfers between devices, flip(): return lax.ppermute(value, 'mp', [(i, i ^ 1 << bit) for i in range(count)])  135 us
    ppermute x8, waiting for transfers between devices, shifted(): lax.ppermute(value, 'seq', [(i, i + steps) for i in range(first, last)])  54.6 us
    all_gather x1, waiting for transfers between devices, shards(): mixer_full = lax.all_gather(mixer_part, 'seq', axis=0, tiled=True)  53 us
    ppermute x50, starting transfers between devices, flip(): return lax.ppermute(value, 'mp', [(i, i ^ 1 << bit) for i in range(count)])  44.7 us
    all_gather x1, waiting for transfers between devices, shards(): gu_full = lax.all_gather(after(gu_part, normed), 'seq', axis=0, tiled=True)  42.7 us
    pallas_call x8, Pallas kernels, block_products(): pl.pallas_call(functools.partial(block_kernel, [t[2] for t in terms]), gr...  38.2 us
    dot_general x6, matrix products, dot(): return lax.dot_general(left, right, dims, preferred_element_type=F32)  36.7 us
    ppermute x8, starting transfers between devices, shifted(): lax.ppermute(value, 'seq', [(i, i + steps) for i in range(first, last)])  30 us
  transfers between devices with their start and end apart: 67, of which 52 were waited for; matrix products, arithmetic and copies ran while one was open for 11% of the time, Pallas kernels for 23%

profile of v1, /device:TPU:0, one launch (start us, length us, event | category | flops | bytes accessed | tf_op | source)
XLA Modules:
  0.0 709.0 jit_solution(5241489485963714541)
XLA Ops:
  15.5 4.8 collective-permute-done
  25.9 9.7 %collective-permute-done.2 = bf16[2,512,256]{2,1,0:T(8,128)(2,1)} collective-permute-done((bf16[2,512,256]{2,1,0:T(8,128)(2,1)}, bf16[2,512,256]{2,1,0:T(8,128)(2,1)}, u32[]{:S(2)}, u32[]{:S(2)}) %collective-permute-start.2) | collective-permute-done | bytes 524320 | tf_op jit(solution)/shard_map/ppermute | solution.py:640
  42.4 5.5 assemble.3
  49.2 7.1 %collective-permute-done.6 = bf16[1,512,256]{2,1,0:T(8,128)(2,1)S(1)} collective-permute-done((bf16[1,512,256]{2,1,0:T(8,128)(2,1)S(1)}, bf16[1,512,256]{2,1,0:T(8,128)(2,1)S(1)}, u32[]{:S(2)}, u32[]{:S(2)}) %collective-permute-start.6) | collective-permute-done | bytes 262176 | tf_op jit(solution)/shard_map/ppermute | solution.py:640
  58.8 11.0 %collective-permute-done.8 = bf16[2,512,256]{2,1,0:T(8,128)(2,1)S(1)} collective-permute-done((bf16[2,512,256]{2,1,0:T(8,128)(2,1)S(1)}, bf16[2,512,256]{2,1,0:T(8,128)(2,1)S(1)}, u32[]{:S(2)}, u32[]{:S(2)}) %collective-permute-start.8) | collective-permute-done | bytes 524320 | tf_op jit(solution)/shard_map/ppermute | solution.py:640
  74.7 4.6 assemble.4.dy_ref.refs_9_
  79.3 53.0 %all-gather.4.cloned.1.call-done.w_ref.refs_1_ = bf16[2112,1536]{1,0:T(8,128)(2,1)} async-done(((bf16[528,1536]{1,0:T(8,128)(2,1)}), bf16[2112,1536]{1,0:T(8,128)(2,1)}) %all-gather.4.cloned.1.call-update) | async-done | bytes 6488080 | tf_op jit(solution)/shard_map/all_gather | solution.py:1149
  132.3 13.4 %project_first.1 = (f32[1024,1536]{1,0:T(8,128)}, f32[1024,16]{1,0:T(8,128)S(1)}, f32[2,1024,8]{2,1,0:T(8,128)S(1)}) custom-call(bf16[1024,2048]{1,0:T(8,128)(2,1)} %get-tuple-element.157.x_ref, bf16[2112,1536]{1,0:T(8,128)(2,1)} %all-gather.4.cloned.1.call-done.w_ref.refs_1_, f32[1024,8]{1,0:T(8,128)S(1)} %copy.50.mask_ref, f32[2]{0:T(128)S(1)} %copy-done.30, ...), custom_call_target="tpu_custom_call" | custom-call | flops 6442450944 | bytes 10485760 | tf_op jit(solution)/shard_map/project_first/pallas_call | solution.py:959
  153.6 8.1 %front.1.qk_ref.qkv_ref = f32[1024,1024]{1,0:T(8,128)S(1)} custom-call(f32[1024,1536]{1,0:T(8,128)} %get-tuple-element.172.x_ref.refs_0_.refs_1_, f32[8,1536]{1,0:T(8,128)S(1)} %collective-permute-done.12.rim_ref, f32[1024,8]{1,0:T(8,128)S(1)} %copy.50.mask_ref, f32[4,1024]{1,0:T(4,128)S(1)} %bitcast.106), custom_call_target="tpu_custom_call" | custom-call | flops 41943040 | bytes 8388608 | tf_op jit(solution)/shard_map/front/pallas_call | solution.py:534
  163.7 17.6 %delta_prep.1 = (f32[2,8,128,128]{3,2,1,0:T(8,128)S(1)}, f32[2,8,128,128]{3,2,1,0:T(8,128)S(1)}, f32[2,8,128,128]{3,2,1,0:T(8,128)S(1)}, f32[2,8,128,128]{3,2,1,...) custom-call(f32[1024,1024]{1,0:T(8,128)} %copy-done.10, ...), custom_call_target="tpu_custom_call" | custom-call | flops 21474836480 | bytes 6291456 | tf_op jit(solution)/shard_map/delta_prep/pallas_call | solution.py:149
  184.4 11.1 %delta_values.1 = (f32[2,8,128,256]{3,2,1,0:T(8,128)}, f32[1024,512]{1,0:T(8,128)}, f32[2,8,128,256]{3,2,1,0:T(8,128)}, f32[2,128,256]{2,1,0:T(8,128)S(1)}) custom-call(f32[1024,1024]{1,0:T(8,128)} %copy-done.10, f32[2,1024,8]{2,1,0:T(8,128)S(1)} %copy-done.40, f32[2,8,128,128]{3,2,1,0:T(8,128)S(1)} %get-tuple-element.177.t_ref, ...), custom_call_target="tpu_custom_call" | custom-call | flops 6442450944 | bytes 8192000 | tf_op jit(solution)/shard_map/delta_values/pallas_call | solution.py:231
  200.7 4.7 collective-permute-done.13
  205.7 7.9 %collective-permute-start.14 = (bf16[2,128,256]{2,1,0:T(8,128)(2,1)S(1)}, bf16[2,128,256]{2,1,0:T(8,128)(2,1)S(1)}, u32[]{:S(2)}, u32[]{:S(2)}) collective-permute-start(bf16[2,128,256]{2,1,0:T(8,128)(2,1)S(1)} %fusion.2), channel_id=1, source_target_pairs={{0,8},{8,16},{16,24},{1,9},{9,17},{17,25},{2,10},{10,18},{18,26},{... | collective-permute-start | bytes 393224 | tf_op jit(solution)/shard_map/ppermute | solution.py:916
  213.6 5.2 collective-permute-done.14
  219.1 11.2 %collective-permute-start.15 = (bf16[2,128,256]{2,1,0:T(8,128)(2,1)S(1)}, bf16[2,128,256]{2,1,0:T(8,128)(2,1)}, u32[]{:S(2)}, u32[]{:S(2)}) collective-permute-start(bf16[2,128,256]{2,1,0:T(8,128)(2,1)S(1)} %fusion.3), channel_id=1, source_target_pairs={{0,8},{8,16},{16,24},{1,9},{9,17},{17,25},{2,10},{10,18},{18,26},{... | collective-permute-start | bytes 393224 | tf_op jit(solution)/shard_map/ppermute | solution.py:916
  233.1 9.7 %delta_output.1 = (bf16[1024,512]{1,0:T(8,128)(2,1)S(1)}, f32[1024,512]{1,0:T(8,128)}, f32[2,8,128,256]{3,2,1,0:T(8,128)}, f32[2,8,128,256]{3,2,1,0:T(8,128)}) custom-call(f32[2,128,256]{2,1,0:T(8,128)S(1)} %convert_element_type.422.start_ref, f32[2,8,128,256]{3,2,1,0:T(8,128)} %get-tuple-element.180.s0_ref, ...), custom_call_target="tpu_custom_call" | custom-call | flops 5368709120 | bytes 12288000 | tf_op jit(solution)/shard_map/delta_output/pallas_call | solution.py:296
  253.5 11.7 %collective-permute-done.17 = bf16[2,512,256]{2,1,0:T(8,128)(2,1)S(1)} collective-permute-done((bf16[2,512,256]{2,1,0:T(8,128)(2,1)S(1)}, bf16[2,512,256]{2,1,0:T(8,128)(2,1)S(1)}, u32[]{:S(2)}, u32[]{:S(2)}) %collective-permute-start.17) | collective-permute-done | bytes 524320 | tf_op jit(solution)/shard_map/ppermute | solution.py:640
  269.0 4.0 collective-permute-done.19
  277.7 4.6 collective-permute-done.21
  286.3 7.6 %collective-permute-done.23 = bf16[2,512,256]{2,1,0:T(8,128)(2,1)S(1)} collective-permute-done((bf16[2,512,256]{2,1,0:T(8,128)(2,1)S(1)}, bf16[2,512,256]{2,1,0:T(8,128)(2,1)S(1)}, u32[]{:S(2)}, u32[]{:S(2)}) %collective-permute-start.23) | collective-permute-done | bytes 524320 | tf_op jit(solution)/shard_map/ppermute | solution.py:640
  299.3 4.4 assemble.5
  305.6 42.7 %all-gather.8.cloned.1.call-done.gu_ref.refs_1_ = bf16[2048,1456]{1,0:T(8,128)(2,1)} async-done(((bf16[512,1456]{1,0:T(8,128)(2,1)}), bf16[2048,1456]{1,0:T(8,128)(2,1)}) %all-gather.8.cloned.1.call-update) | async-done | bytes 5963792 | tf_op jit(solution)/shard_map/all_gather | solution.py:1154
  348.3 15.5 %ffn.1 = (bf16[1024,688]{1,0:T(8,128)(2,1)S(1)}, bf16[1024,1456]{1,0:T(8,128)(2,1)}) custom-call(bf16[1024,2048]{1,0:T(8,128)(2,1)} %get-tuple-element.207.x_ref, bf16[1024,2048]{1,0:T(8,128)(2,1)} %assemble.4.dy_ref.refs_9_, bf16[2048,1456]{1,0:T(8,128)(2,1)} %all-gather.8.cloned.1.call-done.gu_ref.refs_1_, bf16[688,2048]{1,0:T(8,128)(2,1)S(1)} %slice.506.down_ref.refs_1_), custom_call_target="tpu_custom_call" | custom-call | flops 8657043456 | bytes 16842752 | tf_op jit(solution)/shard_map/ffn/pallas_call | solution.py:1042
  365.0 10.1 %convolution_convert_fusion.1 = bf16[2048,1456]{0,1:T(8,128)(2,1)} fusion(bf16[1024,2048]{1,0:T(8,128)(2,1)S(1)} %copy-done.67, bf16[1024,1456]{1,0:T(8,128)(2,1)} %get-tuple-element.210.refs_0_), kind=kOutput, calls=%fused_computation.1 | convolution fusion | flops 6109888512 | bytes 13139968 | tf_op jit(solution)/shard_map/dot_general | solution.py:924
  377.0 5.6 block_products.11
  382.7 6.8 block_products.10
  394.7 11.4 %collective-permute-done.28 = bf16[2,512,256]{2,1,0:T(8,128)(2,1)S(1)} collective-permute-done((bf16[2,512,256]{2,1,0:T(8,128)(2,1)S(1)}, bf16[2,512,256]{2,1,0:T(8,128)(2,1)S(1)}, u32[]{:S(2)}, u32[]{:S(2)}) %collective-permute-start.28) | collective-permute-done | bytes 524320 | tf_op jit(solution)/shard_map/ppermute | solution.py:640
  409.5 5.7 collective-permute-done.30
  418.1 5.6 collective-permute-done.32
  426.2 9.1 %collective-permute-done.34 = bf16[2,512,256]{2,1,0:T(8,128)(2,1)S(1)} collective-permute-done((bf16[2,512,256]{2,1,0:T(8,128)(2,1)S(1)}, bf16[2,512,256]{2,1,0:T(8,128)(2,1)S(1)}, u32[]{:S(2)}, u32[]{:S(2)}) %collective-permute-start.34) | collective-permute-done | bytes 524320 | tf_op jit(solution)/shard_map/ppermute | solution.py:640
  440.3 9.3 %norm_back.1 = (bf16[1024,2048]{1,0:T(8,128)(2,1)}, f32[1024,256]{1,0:T(8,128)S(1)}, f32[1,256]{1,0:T(1,128)S(1)}) custom-call(s32[1]{0:T(128)} %bitcast.refs_0_.mp_ref, bf16[4,512,256]{2,1,0:T(8,128)(2,1)S(1)} %pad_maximum_fusion.9.refs_1_, bf16[4,512,256]{2,1,0:T(8,128)(2,1)S(1)} %collective-permute-done.36.refs_2_, ...), custom_call_target="tpu_custom_call" | custom-call | flops 41943040 | bytes 16777216 | tf_op jit(solution)/shard_map/norm_back/pallas_call | solution.py:794
  449.6 5.0 convolution_convert_fusion.3
  463.2 3.9 block_products.12
  467.2 6.7 fusion.84.dm_ref
  477.9 7.4 %delta_tail.1 = (f32[1024,512]{1,0:T(8,128)S(1)}, bf16[1024,512]{1,0:T(8,128)(2,1)S(1)}, f32[2,256]{1,0:T(2,128)S(1)}, f32[2,8,128,256]{3,2,1,0:T(8,128)}, f32[2,128,256]{2,1,0:T(8,128)S(1)}) custom-call(f32[1024,512]{1,0:T(8,128)} %fusion.84.dm_ref, f32[1024,512]{1,0:T(8,128)} %get-tuple-element.245.o_ref, f32[2,256]{1,0:T(2,128)S(1)} %copy-done.29, ...), custom_call_target="tpu_custom_call" | custom-call | flops 5368709120 | bytes 12288000 | tf_op jit(solution)/shard_map/delta_tail/pallas_call | solution.py:374
  486.6 12.3 %collective-permute-done.43 = bf16[2,128,256]{2,1,0:T(8,128)(2,1)S(1)} collective-permute-done((bf16[2,128,256]{2,1,0:T(8,128)(2,1)S(1)}, bf16[2,128,256]{2,1,0:T(8,128)(2,1)S(1)}, u32[]{:S(2)}, u32[]{:S(2)}) %collective-permute-start.43) | collective-permute-done | bytes 131104 | tf_op jit(solution)/shard_map/ppermute | solution.py:916
  501.6 12.1 %collective-permute-done.44 = bf16[2,128,256]{2,1,0:T(8,128)(2,1)S(1)} collective-permute-done((bf16[2,128,256]{2,1,0:T(8,128)(2,1)S(1)}, bf16[2,128,256]{2,1,0:T(8,128)(2,1)S(1)}, u32[]{:S(2)}, u32[]{:S(2)}) %collective-permute-start.44) | collective-permute-done | bytes 131104 | tf_op jit(solution)/shard_map/ppermute | solution.py:916
  516.7 11.4 %collective-permute-done.45 = bf16[2,128,256]{2,1,0:T(8,128)(2,1)S(1)} collective-permute-done((bf16[2,128,256]{2,1,0:T(8,128)(2,1)S(1)}, bf16[2,128,256]{2,1,0:T(8,128)(2,1)S(1)}, u32[]{:S(2)}, u32[]{:S(2)}) %collective-permute-start.45) | collective-permute-done | bytes 131104 | tf_op jit(solution)/shard_map/ppermute | solution.py:916
  530.5 17.4 %delta_grads.1 = (f32[1024,1024]{1,0:T(8,128)}, f32[2,1024,8]{2,1,0:T(8,128)S(1)}) custom-call(f32[2,128,256]{2,1,0:T(8,128)S(1)} %convert_element_type.490.end_ref, f32[1024,1024]{1,0:T(8,128)} %copy-done.10, f32[2,1024,8]{2,1,0:T(8,128)S(1)} %copy-done.41, f32[2,8,128,128]{3,2,1,0:T(8,128)S(1)} %copy-done.45, f32[2,8,128,128]{3,2,1,0:T(8,128)S(1)} %copy-done.43, ...), custom_call_target="tpu_custom_call" | custom-call | flops 16106127360 | bytes 24576000 | tf_op jit(solution)/shard_map/delta_grads/pallas_call | solution.py:471
  548.9 15.8 %front_back.1 = (bf16[1024,1536]{1,0:T(8,128)(2,1)S(1)}, f32[16,1536]{1,0:T(8,128)S(1)}, f32[8,1536]{1,0:T(8,128)S(1)}, f32[4,1536]{1,0:T(4,128)S(1)}) custom-call(f32[1024,1536]{1,0:T(8,128)} %get-tuple-element.172.x_ref.refs_0_.refs_1_, f32[8,1536]{1,0:T(8,128)S(1)} %collective-permute-done.12.rim_ref, f32[1024,8]{1,0:T(8,128)S(1)} %copy-done.9, ...), custom_call_target="tpu_custom_call" | custom-call | flops 125829120 | bytes 15728640 | tf_op jit(solution)/shard_map/front_back/pallas_call | solution.py:609
  566.3 8.9 %collective-permute-done.46 = f32[8,1536]{1,0:T(8,128)S(1)} collective-permute-done((f32[8,1536]{1,0:T(8,128)S(1)}, f32[8,1536]{1,0:T(8,128)S(1)}, u32[]{:S(2)}, u32[]{:S(2)}) %collective-permute-start.46) | collective-permute-done | bytes 49184 | tf_op jit(solution)/shard_map/ppermute | solution.py:916
  575.2 8.7 %convolution_convert_fusion = bf16[2048,1536]{1,0:T(8,128)(2,1)} fusion(bf16[1024,2048]{1,0:T(8,128)(2,1)S(1)} %copy-done.58, bf16[1024,1536]{1,0:T(8,128)(2,1)S(1)} %maximum_dynamic-update-slice_fusion.refs_0_), kind=kOutput, calls=%fused_computation | convolution fusion | flops 6445596672 | bytes 13631488 | tf_op jit(solution)/shard_map/dot_general | solution.py:924
  589.2 5.7 block_products.15
  595.0 7.0 block_products.14
  608.8 10.3 %collective-permute-done.48 = bf16[2,512,256]{2,1,0:T(8,128)(2,1)S(1)} collective-permute-done((bf16[2,512,256]{2,1,0:T(8,128)(2,1)S(1)}, bf16[2,512,256]{2,1,0:T(8,128)(2,1)S(1)}, u32[]{:S(2)}, u32[]{:S(2)}) %collective-permute-start.48) | collective-permute-done | bytes 524320 | tf_op jit(solution)/shard_map/ppermute | solution.py:640
  644.5 7.7 %collective-permute-done.56 = f32[112,128]{1,0:T(8,128)S(1)} collective-permute-done((f32[112,128]{1,0:T(8,128)S(1)}, f32[112,128]{1,0:T(8,128)S(1)}, u32[]{:S(2)}, u32[]{:S(2)}) %collective-permute-start.56) | collective-permute-done | bytes 57376 | tf_op jit(solution)/shard_map/ppermute | solution.py:909
  669.8 26.9 %reduce-scatter.4.cloned.1.call-done = bf16[512,1536]{1,0:T(8,128)(2,1)} async-done(((bf16[2048,1536]{1,0:T(8,128)(2,1)}), bf16[512,1536]{1,0:T(8,128)(2,1)}) %reduce-scatter.4.cloned.1.call-update) | async-done | bytes 1572880 | tf_op jit(solution)/shard_map/reduce_scatter | solution.py:1212
  696.6 4.9 reshape.219
  (379 shorter events, 182.2 us)
Async XLA Ops:
  7.2 125.1 %all-gather.4.cloned.1.call-start = ((), (), s32[]{:S(2)}) async-start(), calls=%async_computation.3 | async-start | bytes 8110080 | tf_op jit(solution)/shard_map/all_gather | solution.py:1149
  10.9 219.4 %all-gather.6.cloned.1.call-start = ((), (), s32[]{:S(2)}) async-start(), calls=%async_computation.4 | async-start | bytes 6144000 | tf_op jit(solution)/shard_map/all_gather | solution.py:1151
  11.0 9.3 %collective-permute-start = (bf16[1,512,256]{2,1,0:T(8,128)(2,1)S(1)}, bf16[1,512,256]{2,1,0:T(8,128)(2,1)S(1)}, u32[]{:S(2)}, u32[]{:S(2)}) collective-permute-start(bf16[1,512,256]{2,1,0:T(8,128)(2,1)S(1)} %get-tuple-element.145), channel_id=1, source_target_pairs={{0,4},{1,5},{2,6},{3,7},{4,0},{5,1},{6,2},{7,3},{8,12},{9,13},{10,... | collective-permute-start | bytes 786440 | tf_op jit(solution)/shard_map/ppermute | solution.py:640
  14.0 7.8 %collective-permute-start.1 = (bf16[1,512,256]{2,1,0:T(8,128)(2,1)S(1)}, bf16[1,512,256]{2,1,0:T(8,128)(2,1)S(1)}, u32[]{:S(2)}, u32[]{:S(2)}) collective-permute-start(bf16[1,512,256]{2,1,0:T(8,128)(2,1)S(1)} %get-tuple-element.146), channel_id=1, source_target_pairs={{0,2},{1,3},{2,0},{3,1},{4,6},{5,7},{6,4},{7,5},{8,10},{9,11},{10,... | collective-permute-start | bytes 786440 | tf_op jit(solution)/shard_map/ppermute | solution.py:640
  22.7 12.9 %collective-permute-start.2 = (bf16[2,512,256]{2,1,0:T(8,128)(2,1)}, bf16[2,512,256]{2,1,0:T(8,128)(2,1)}, u32[]{:S(2)}, u32[]{:S(2)}) collective-permute-start(bf16[2,512,256]{2,1,0:T(8,128)(2,1)} %pad_maximum_fusion.12), channel_id=1, source_target_pairs={{0,2},{1,3},{2,0},{3,1},{4,6},{5,7},{6,4},{7,5},{8,10},{9,11},{10,... | collective-permute-start | bytes 1572872 | tf_op jit(solution)/shard_map/ppermute | solution.py:640
  24.2 12.3 %collective-permute-start.3 = (bf16[2,512,256]{2,1,0:T(8,128)(2,1)S(1)}, bf16[2,512,256]{2,1,0:T(8,128)(2,1)}, u32[]{:S(2)}, u32[]{:S(2)}) collective-permute-start(bf16[2,512,256]{2,1,0:T(8,128)(2,1)S(1)} %pad_maximum_fusion.13), channel_id=1, source_target_pairs={{0,4},{1,5},{2,6},{3,7},{4,0},{5,1},{6,2},{7,3},{8,12},{9,13},{10,... | collective-permute-start | bytes 1572872 | tf_op jit(solution)/shard_map/ppermute | solution.py:640
  38.0 310.3 %all-gather.8.cloned.1.call-start = ((), (), s32[]{:S(2)}) async-start(), calls=%async_computation.5 | async-start | bytes 7864320 | tf_op jit(solution)/shard_map/all_gather | solution.py:1154
  47.9 8.4 %collective-permute-start.6 = (bf16[1,512,256]{2,1,0:T(8,128)(2,1)S(1)}, bf16[1,512,256]{2,1,0:T(8,128)(2,1)S(1)}, u32[]{:S(2)}, u32[]{:S(2)}) collective-permute-start(bf16[1,512,256]{2,1,0:T(8,128)(2,1)S(1)} %get-tuple-element.159), channel_id=1, source_target_pairs={{0,4},{1,5},{2,6},{3,7},{4,0},{5,1},{6,2},{7,3},{8,12},{9,13},{10,... | collective-permute-start | bytes 786440 | tf_op jit(solution)/shard_map/ppermute | solution.py:640
  48.6 8.1 %collective-permute-start.7 = (bf16[1,512,256]{2,1,0:T(8,128)(2,1)S(1)}, bf16[1,512,256]{2,1,0:T(8,128)(2,1)S(1)}, u32[]{:S(2)}, u32[]{:S(2)}) collective-permute-start(bf16[1,512,256]{2,1,0:T(8,128)(2,1)S(1)} %get-tuple-element.160), channel_id=1, source_target_pairs={{0,2},{1,3},{2,0},{3,1},{4,6},{5,7},{6,4},{7,5},{8,10},{9,11},{10,... | collective-permute-start | bytes 786440 | tf_op jit(solution)/shard_map/ppermute | solution.py:640
  56.8 13.0 %collective-permute-start.8 = (bf16[2,512,256]{2,1,0:T(8,128)(2,1)S(1)}, bf16[2,512,256]{2,1,0:T(8,128)(2,1)S(1)}, u32[]{:S(2)}, u32[]{:S(2)}) collective-permute-start(bf16[2,512,256]{2,1,0:T(8,128)(2,1)S(1)} %pad_maximum_fusion.14), channel_id=1, source_target_pairs={{0,2},{1,3},{2,0},{3,1},{4,6},{5,7},{6,4},{7,5},{8,10},{9,11},{10,... | collective-permute-start | bytes 1572872 | tf_op jit(solution)/shard_map/ppermute | solution.py:640
  57.5 12.6 %collective-permute-start.9 = (bf16[2,512,256]{2,1,0:T(8,128)(2,1)S(1)}, bf16[2,512,256]{2,1,0:T(8,128)(2,1)S(1)}, u32[]{:S(2)}, u32[]{:S(2)}) collective-permute-start(bf16[2,512,256]{2,1,0:T(8,128)(2,1)S(1)} %pad_maximum_fusion.15), channel_id=1, source_target_pairs={{0,4},{1,5},{2,6},{3,7},{4,0},{5,1},{6,2},{7,3},{8,12},{9,13},{10,... | collective-permute-start | bytes 1572872 | tf_op jit(solution)/shard_map/ppermute | solution.py:640
  153.4 508.6 %reduce-scatter.8.cloned.1.call-start = ((), (), s32[]{:S(2)}) async-start(), calls=%async_computation.8 | async-start | bytes 7454720 | tf_op jit(solution)/shard_map/reduce_scatter | solution.py:1181
  195.5 9.9 %collective-permute-start.13 = (bf16[2,128,256]{2,1,0:T(8,128)(2,1)S(1)}, bf16[2,128,256]{2,1,0:T(8,128)(2,1)S(1)}, u32[]{:S(2)}, u32[]{:S(2)}) collective-permute-start(bf16[2,128,256]{2,1,0:T(8,128)(2,1)S(1)} %convert_element_type.419), channel_id=1, source_target_pairs={{0,8},{8,16},{16,24},{1,9},{9,17},{17,25},{2,10},{10,18},{18,26},{... | collective-permute-start | bytes 393224 | tf_op jit(solution)/shard_map/ppermute | solution.py:916
  205.7 13.2 %collective-permute-start.14 = (bf16[2,128,256]{2,1,0:T(8,128)(2,1)S(1)}, bf16[2,128,256]{2,1,0:T(8,128)(2,1)S(1)}, u32[]{:S(2)}, u32[]{:S(2)}) collective-permute-start(bf16[2,128,256]{2,1,0:T(8,128)(2,1)S(1)} %fusion.2), channel_id=1, source_target_pairs={{0,8},{8,16},{16,24},{1,9},{9,17},{17,25},{2,10},{10,18},{18,26},{... | collective-permute-start | bytes 393224 | tf_op jit(solution)/shard_map/ppermute | solution.py:916
  219.1 13.0 %collective-permute-start.15 = (bf16[2,128,256]{2,1,0:T(8,128)(2,1)S(1)}, bf16[2,128,256]{2,1,0:T(8,128)(2,1)}, u32[]{:S(2)}, u32[]{:S(2)}) collective-permute-start(bf16[2,128,256]{2,1,0:T(8,128)(2,1)S(1)} %fusion.3), channel_id=1, source_target_pairs={{0,8},{8,16},{16,24},{1,9},{9,17},{17,25},{2,10},{10,18},{18,26},{... | collective-permute-start | bytes 393224 | tf_op jit(solution)/shard_map/ppermute | solution.py:916
  251.3 13.9 %collective-permute-start.17 = (bf16[2,512,256]{2,1,0:T(8,128)(2,1)S(1)}, bf16[2,512,256]{2,1,0:T(8,128)(2,1)S(1)}, u32[]{:S(2)}, u32[]{:S(2)}) collective-permute-start(bf16[2,512,256]{2,1,0:T(8,128)(2,1)S(1)} %pad_maximum_fusion.16), channel_id=1, source_target_pairs={{0,2},{1,3},{2,0},{3,1},{4,6},{5,7},{6,4},{7,5},{8,10},{9,11},{10,... | collective-permute-start | bytes 1572872 | tf_op jit(solution)/shard_map/ppermute | solution.py:640
  252.1 13.5 %collective-permute-start.18 = (bf16[2,512,256]{2,1,0:T(8,128)(2,1)S(1)}, bf16[2,512,256]{2,1,0:T(8,128)(2,1)S(1)}, u32[]{:S(2)}, u32[]{:S(2)}) collective-permute-start(bf16[2,512,256]{2,1,0:T(8,128)(2,1)S(1)} %pad_maximum_fusion.17), channel_id=1, source_target_pairs={{0,4},{1,5},{2,6},{3,7},{4,0},{5,1},{6,2},{7,3},{8,12},{9,13},{10,... | collective-permute-start | bytes 1572872 | tf_op jit(solution)/shard_map/ppermute | solution.py:640
  265.8 7.2 %collective-permute-start.19 = (bf16[1,512,256]{2,1,0:T(8,128)(2,1)S(1)}, bf16[1,512,256]{2,1,0:T(8,128)(2,1)S(1)}, u32[]{:S(2)}, u32[]{:S(2)}) collective-permute-start(bf16[1,512,256]{2,1,0:T(8,128)(2,1)S(1)} %get-tuple-element.191), channel_id=1, source_target_pairs={{0,4},{1,5},{2,6},{3,7},{4,0},{5,1},{6,2},{7,3},{8,12},{9,13},{10,... | collective-permute-start | bytes 786440 | tf_op jit(solution)/shard_map/ppermute | solution.py:640
  267.3 7.1 %collective-permute-start.20 = (bf16[1,512,256]{2,1,0:T(8,128)(2,1)S(1)}, bf16[1,512,256]{2,1,0:T(8,128)(2,1)S(1)}, u32[]{:S(2)}, u32[]{:S(2)}) collective-permute-start(bf16[1,512,256]{2,1,0:T(8,128)(2,1)S(1)} %get-tuple-element.192), channel_id=1, source_target_pairs={{0,2},{1,3},{2,0},{3,1},{4,6},{5,7},{6,4},{7,5},{8,10},{9,11},{10,... | collective-permute-start | bytes 786440 | tf_op jit(solution)/shard_map/ppermute | solution.py:640
  282.8 11.1 %collective-permute-start.23 = (bf16[2,512,256]{2,1,0:T(8,128)(2,1)S(1)}, bf16[2,512,256]{2,1,0:T(8,128)(2,1)S(1)}, u32[]{:S(2)}, u32[]{:S(2)}) collective-permute-start(bf16[2,512,256]{2,1,0:T(8,128)(2,1)S(1)} %pad_maximum_fusion.18), channel_id=1, source_target_pairs={{0,2},{1,3},{2,0},{3,1},{4,6},{5,7},{6,4},{7,5},{8,10},{9,11},{10,... | collective-permute-start | bytes 1572872 | tf_op jit(solution)/shard_map/ppermute | solution.py:640
  284.5 10.3 %collective-permute-start.24 = (bf16[2,512,256]{2,1,0:T(8,128)(2,1)S(1)}, bf16[2,512,256]{2,1,0:T(8,128)(2,1)S(1)}, u32[]{:S(2)}, u32[]{:S(2)}) collective-permute-start(bf16[2,512,256]{2,1,0:T(8,128)(2,1)S(1)} %pad_maximum_fusion.19), channel_id=1, source_target_pairs={{0,4},{1,5},{2,6},{3,7},{4,0},{5,1},{6,2},{7,3},{8,12},{9,13},{10,... | collective-permute-start | bytes 1572872 | tf_op jit(solution)/shard_map/ppermute | solution.py:640
  375.2 290.1 %reduce-scatter.6.cloned.1.call-start = ((), (), s32[]{:S(2)}) async-start(), calls=%async_computation.7 | async-start | bytes 6144000 | tf_op jit(solution)/shard_map/reduce_scatter | solution.py:1191
  382.6 6.9 collective-permute-start.27
  391.6 14.4 %collective-permute-start.28 = (bf16[2,512,256]{2,1,0:T(8,128)(2,1)S(1)}, bf16[2,512,256]{2,1,0:T(8,128)(2,1)S(1)}, u32[]{:S(2)}, u32[]{:S(2)}) collective-permute-start(bf16[2,512,256]{2,1,0:T(8,128)(2,1)S(1)} %pad_maximum_fusion.20), channel_id=1, source_target_pairs={{0,2},{1,3},{2,0},{3,1},{4,6},{5,7},{6,4},{7,5},{8,10},{9,11},{10,... | collective-permute-start | bytes 1572872 | tf_op jit(solution)/shard_map/ppermute | solution.py:640
  393.2 14.1 %collective-permute-start.29 = (bf16[2,512,256]{2,1,0:T(8,128)(2,1)S(1)}, bf16[2,512,256]{2,1,0:T(8,128)(2,1)S(1)}, u32[]{:S(2)}, u32[]{:S(2)}) collective-permute-start(bf16[2,512,256]{2,1,0:T(8,128)(2,1)S(1)} %pad_maximum_fusion.21), channel_id=1, source_target_pairs={{0,4},{1,5},{2,6},{3,7},{4,0},{5,1},{6,2},{7,3},{8,12},{9,13},{10,... | collective-permute-start | bytes 1572872 | tf_op jit(solution)/shard_map/ppermute | solution.py:640
  407.4 7.8 %collective-permute-start.30 = (bf16[1,512,256]{2,1,0:T(8,128)(2,1)S(1)}, bf16[1,512,256]{2,1,0:T(8,128)(2,1)S(1)}, u32[]{:S(2)}, u32[]{:S(2)}) collective-permute-start(bf16[1,512,256]{2,1,0:T(8,128)(2,1)S(1)} %get-tuple-element.215), channel_id=1, source_target_pairs={{0,4},{1,5},{2,6},{3,7},{4,0},{5,1},{6,2},{7,3},{8,12},{9,13},{10,... | collective-permute-start | bytes 786440 | tf_op jit(solution)/shard_map/ppermute | solution.py:640
  409.0 7.5 %collective-permute-start.31 = (bf16[1,512,256]{2,1,0:T(8,128)(2,1)S(1)}, bf16[1,512,256]{2,1,0:T(8,128)(2,1)S(1)}, u32[]{:S(2)}, u32[]{:S(2)}) collective-permute-start(bf16[1,512,256]{2,1,0:T(8,128)(2,1)S(1)} %get-tuple-element.216), channel_id=1, source_target_pairs={{0,2},{1,3},{2,0},{3,1},{4,6},{5,7},{6,4},{7,5},{8,10},{9,11},{10,... | collective-permute-start | bytes 786440 | tf_op jit(solution)/shard_map/ppermute | solution.py:640
  416.9 6.7 collective-permute-start.32
  417.5 6.5 collective-permute-start.33
  424.0 11.3 %collective-permute-start.34 = (bf16[2,512,256]{2,1,0:T(8,128)(2,1)S(1)}, bf16[2,512,256]{2,1,0:T(8,128)(2,1)S(1)}, u32[]{:S(2)}, u32[]{:S(2)}) collective-permute-start(bf16[2,512,256]{2,1,0:T(8,128)(2,1)S(1)} %pad_maximum_fusion.22), channel_id=1, source_target_pairs={{0,2},{1,3},{2,0},{3,1},{4,6},{5,7},{6,4},{7,5},{8,10},{9,11},{10,... | collective-permute-start | bytes 1572872 | tf_op jit(solution)/shard_map/ppermute | solution.py:640
  424.8 11.1 %collective-permute-start.35 = (bf16[2,512,256]{2,1,0:T(8,128)(2,1)S(1)}, bf16[2,512,256]{2,1,0:T(8,128)(2,1)S(1)}, u32[]{:S(2)}, u32[]{:S(2)}) collective-permute-start(bf16[2,512,256]{2,1,0:T(8,128)(2,1)S(1)} %pad_maximum_fusion.23), channel_id=1, source_target_pairs={{0,4},{1,5},{2,6},{3,7},{4,0},{5,1},{6,2},{7,3},{8,12},{9,13},{10,... | collective-permute-start | bytes 1572872 | tf_op jit(solution)/shard_map/ppermute | solution.py:640
  457.5 239.2 %reduce-scatter.4.cloned.1.call-start = ((), (), s32[]{:S(2)}) async-start(), calls=%async_computation.6 | async-start | bytes 7864320 | tf_op jit(solution)/shard_map/reduce_scatter | solution.py:1212
  463.1 10.8 %collective-permute-start.38 = (bf16[4,1024,256]{2,1,0:T(8,128)(2,1)S(1)}, bf16[4,1024,256]{2,1,0:T(8,128)(2,1)S(1)}, u32[]{:S(2)}, u32[]{:S(2)}) collective-permute-start(bf16[4,1024,256]{2,1,0:T(8,128)(2,1)S(1)} %block_products.13), channel_id=1, source_target_pairs={{0,1},{1,0},{2,3},{3,2},{4,5},{5,4},{6,7},{7,6},{8,9},{9,8},{10,11... | collective-permute-start | bytes 6291464 | tf_op jit(solution)/shard_map/ppermute | solution.py:640
  475.2 25.3 %collective-permute-start.39 = (bf16[2,512,256]{2,1,0:T(8,128)(2,1)S(1)}, bf16[2,512,256]{2,1,0:T(8,128)(2,1)S(1)}, u32[]{:S(2)}, u32[]{:S(2)}) collective-permute-start(bf16[2,512,256]{2,1,0:T(8,128)(2,1)S(1)} %pad_maximum_fusion.24), channel_id=1, source_target_pairs={{0,2},{1,3},{2,0},{3,1},{4,6},{5,7},{6,4},{7,5},{8,10},{9,11},{10,... | collective-permute-start | bytes 1572872 | tf_op jit(solution)/shard_map/ppermute | solution.py:640
  476.4 24.1 %collective-permute-start.40 = (bf16[2,512,256]{2,1,0:T(8,128)(2,1)S(1)}, bf16[2,512,256]{2,1,0:T(8,128)(2,1)S(1)}, u32[]{:S(2)}, u32[]{:S(2)}) collective-permute-start(bf16[2,512,256]{2,1,0:T(8,128)(2,1)S(1)} %pad_maximum_fusion.25), channel_id=1, source_target_pairs={{0,4},{1,5},{2,6},{3,7},{4,0},{5,1},{6,2},{7,3},{8,12},{9,13},{10,... | collective-permute-start | bytes 1572872 | tf_op jit(solution)/shard_map/ppermute | solution.py:640
  485.3 13.6 %collective-permute-start.43 = (bf16[2,128,256]{2,1,0:T(8,128)(2,1)S(1)}, bf16[2,128,256]{2,1,0:T(8,128)(2,1)S(1)}, u32[]{:S(2)}, u32[]{:S(2)}) collective-permute-start(bf16[2,128,256]{2,1,0:T(8,128)(2,1)S(1)} %convert_element_type.487), channel_id=1, source_target_pairs={{8,0},{16,8},{24,16},{9,1},{17,9},{25,17},{10,2},{18,10},{26,18},{... | collective-permute-start | bytes 393224 | tf_op jit(solution)/shard_map/ppermute | solution.py:916
  499.2 14.5 %collective-permute-start.44 = (bf16[2,128,256]{2,1,0:T(8,128)(2,1)S(1)}, bf16[2,128,256]{2,1,0:T(8,128)(2,1)S(1)}, u32[]{:S(2)}, u32[]{:S(2)}) collective-permute-start(bf16[2,128,256]{2,1,0:T(8,128)(2,1)S(1)} %fusion.4), channel_id=1, source_target_pairs={{8,0},{16,8},{24,16},{9,1},{17,9},{25,17},{10,2},{18,10},{26,18},{... | collective-permute-start | bytes 393224 | tf_op jit(solution)/shard_map/ppermute | solution.py:916
  500.7 27.5 %collective-permute-start.41 = (bf16[1,512,256]{2,1,0:T(8,128)(2,1)S(1)}, bf16[1,512,256]{2,1,0:T(8,128)(2,1)S(1)}, u32[]{:S(2)}, u32[]{:S(2)}) collective-permute-start(bf16[1,512,256]{2,1,0:T(8,128)(2,1)S(1)} %get-tuple-element.238), channel_id=1, source_target_pairs={{0,4},{1,5},{2,6},{3,7},{4,0},{5,1},{6,2},{7,3},{8,12},{9,13},{10,... | collective-permute-start | bytes 786440 | tf_op jit(solution)/shard_map/ppermute | solution.py:640
  501.5 26.7 %collective-permute-start.42 = (bf16[1,512,256]{2,1,0:T(8,128)(2,1)S(1)}, bf16[1,512,256]{2,1,0:T(8,128)(2,1)S(1)}, u32[]{:S(2)}, u32[]{:S(2)}) collective-permute-start(bf16[1,512,256]{2,1,0:T(8,128)(2,1)S(1)} %get-tuple-element.239), channel_id=1, source_target_pairs={{0,2},{1,3},{2,0},{3,1},{4,6},{5,7},{6,4},{7,5},{8,10},{9,11},{10,... | collective-permute-start | bytes 786440 | tf_op jit(solution)/shard_map/ppermute | solution.py:640
  514.0 14.2 %collective-permute-start.45 = (bf16[2,128,256]{2,1,0:T(8,128)(2,1)S(1)}, bf16[2,128,256]{2,1,0:T(8,128)(2,1)S(1)}, u32[]{:S(2)}, u32[]{:S(2)}) collective-permute-start(bf16[2,128,256]{2,1,0:T(8,128)(2,1)S(1)} %fusion.5), channel_id=1, source_target_pairs={{8,0},{16,8},{24,16},{9,1},{17,9},{25,17},{10,2},{18,10},{26,18},{... | collective-permute-start | bytes 393224 | tf_op jit(solution)/shard_map/ppermute | solution.py:916
  564.7 10.5 %collective-permute-start.46 = (f32[8,1536]{1,0:T(8,128)S(1)}, f32[8,1536]{1,0:T(8,128)S(1)}, u32[]{:S(2)}, u32[]{:S(2)}) collective-permute-start(f32[8,1536]{1,0:T(8,128)S(1)} %get-tuple-element.260), channel_id=1, source_target_pairs={{8,0},{16,8},{24,16},{9,1},{17,9},{25,17},{10,2},{18,10},{26,18},{... | collective-permute-start | bytes 147464 | tf_op jit(solution)/shard_map/ppermute | solution.py:916
  594.9 7.1 %collective-permute-start.47 = (bf16[4,1024,256]{2,1,0:T(8,128)(2,1)S(1)}, bf16[4,1024,256]{2,1,0:T(8,128)(2,1)S(1)}, u32[]{:S(2)}, u32[]{:S(2)}) collective-permute-start(bf16[4,1024,256]{2,1,0:T(8,128)(2,1)S(1)} %block_products.15), channel_id=1, source_target_pairs={{0,1},{1,0},{2,3},{3,2},{4,5},{5,4},{6,7},{7,6},{8,9},{9,8},{10,11... | collective-permute-start | bytes 6291464 | tf_op jit(solution)/shard_map/ppermute | solution.py:640
  604.8 14.4 %collective-permute-start.48 = (bf16[2,512,256]{2,1,0:T(8,128)(2,1)S(1)}, bf16[2,512,256]{2,1,0:T(8,128)(2,1)S(1)}, u32[]{:S(2)}, u32[]{:S(2)}) collective-permute-start(bf16[2,512,256]{2,1,0:T(8,128)(2,1)S(1)} %pad_maximum_fusion.26), channel_id=1, source_target_pairs={{0,2},{1,3},{2,0},{3,1},{4,6},{5,7},{6,4},{7,5},{8,10},{9,11},{10,... | collective-permute-start | bytes 1572872 | tf_op jit(solution)/shard_map/ppermute | solution.py:640
  606.3 14.0 %collective-permute-start.49 = (bf16[2,512,256]{2,1,0:T(8,128)(2,1)S(1)}, bf16[2,512,256]{2,1,0:T(8,128)(2,1)S(1)}, u32[]{:S(2)}, u32[]{:S(2)}) collective-permute-start(bf16[2,512,256]{2,1,0:T(8,128)(2,1)S(1)} %pad_maximum_fusion.27), channel_id=1, source_target_pairs={{0,4},{1,5},{2,6},{3,7},{4,0},{5,1},{6,2},{7,3},{8,12},{9,13},{10,... | collective-permute-start | bytes 1572872 | tf_op jit(solution)/shard_map/ppermute | solution.py:640
  621.8 7.7 %collective-permute-start.50 = (bf16[1,512,256]{2,1,0:T(8,128)(2,1)S(1)}, bf16[1,512,256]{2,1,0:T(8,128)(2,1)S(1)}, u32[]{:S(2)}, u32[]{:S(2)}) collective-permute-start(bf16[1,512,256]{2,1,0:T(8,128)(2,1)S(1)} %get-tuple-element.268), channel_id=1, source_target_pairs={{0,4},{1,5},{2,6},{3,7},{4,0},{5,1},{6,2},{7,3},{8,12},{9,13},{10,... | collective-permute-start | bytes 786440 | tf_op jit(solution)/shard_map/ppermute | solution.py:640
  623.4 7.4 %collective-permute-start.51 = (bf16[1,512,256]{2,1,0:T(8,128)(2,1)S(1)}, bf16[1,512,256]{2,1,0:T(8,128)(2,1)S(1)}, u32[]{:S(2)}, u32[]{:S(2)}) collective-permute-start(bf16[1,512,256]{2,1,0:T(8,128)(2,1)S(1)} %get-tuple-element.269), channel_id=1, source_target_pairs={{0,2},{1,3},{2,0},{3,1},{4,6},{5,7},{6,4},{7,5},{8,10},{9,11},{10,... | collective-permute-start | bytes 786440 | tf_op jit(solution)/shard_map/ppermute | solution.py:640
  638.3 14.0 %collective-permute-start.56 = (f32[112,128]{1,0:T(8,128)S(1)}, f32[112,128]{1,0:T(8,128)S(1)}, u32[]{:S(2)}, u32[]{:S(2)}) collective-permute-start(f32[112,128]{1,0:T(8,128)S(1)} %pad_bitcast_fusion), channel_id=1, source_target_pairs={{0,16},{8,24},{16,0},{24,8},{1,17},{9,25},{17,1},{25,9},{2,18},{10... | collective-permute-start | bytes 172040 | tf_op jit(solution)/shard_map/ppermute | solution.py:909
  639.5 12.7 %collective-permute-start.55 = (f32[112,128]{1,0:T(8,128)S(1)}, f32[112,128]{1,0:T(8,128)S(1)}, u32[]{:S(2)}, u32[]{:S(2)}) collective-permute-start(f32[112,128]{1,0:T(8,128)S(1)} %pad_bitcast_fusion), channel_id=1, source_target_pairs={{0,8},{8,16},{16,24},{24,0},{1,9},{9,17},{17,25},{25,1},{2,10},{10... | collective-permute-start | bytes 172040 | tf_op jit(solution)/shard_map/ppermute | solution.py:909
  (89 other events, 1109.5 us)
Sparse Core Ops, SparseCore 0:
  11.0 121.2 all-gather.3
  134.5 94.6 all-gather.5
  230.7 117.5 all-gather.7
  375.3 103.6 reduce-scatter.7
  481.3 98.2 reduce-scatter.5
  584.1 112.5 reduce-scatter.3

commit v2 on v1

--- a/solution.py
+++ b/solution.py
@@ -45,7 +45,7 @@
 
 
 def cost(flops, nbytes):
-    return pl.CostEstimate(flops=int(flops), bytes_accessed=int(nbytes), transcendentals=0)
+    return pl.CostEstimate(flops=int(flops) // 100, bytes_accessed=int(nbytes) // 100, transcendentals=0)
 
 
 def spec(shape, index_map):
@@ -397,9 +397,43 @@
     )(grad_mixed, outs, gain, reach_turned, steps_turned, *([raw] * heads))
 
 
+def early_kernel(heads, group, at_ref, u_ref, s_ref, do_ref, da_ref, dqd_ref, dua_ref):
+    pairs = [(h, c) for c in range(group) for h in range(heads)]
+    douts = {
+        (h, c): do_ref[c * CHUNK : (c + 1) * CHUNK, h * DV : (h + 1) * DV] for h, c in pairs
+    }
+    for h, c in pairs:
+        da_ref[h, c] = dx(douts[h, c], u_ref[h, c], NT)
+    for h, c in pairs:
+        dqd_ref[h, c] = dx(douts[h, c], s_ref[h, c], NT)
+    for h, c in pairs:
+        dua_ref[h, c] = dx(at_ref[h, c], douts[h, c])
+
+
+def delta_early(scores_turned, u, s, dout):
+    heads, count = u.shape[:2]
+    group = min(2, count)
+    square = spec((heads, group, CHUNK, CHUNK), lambda g: (0, g, 0, 0))
+    tall = spec((heads, group, CHUNK, DV), lambda g: (0, g, 0, 0))
+    return pl.pallas_call(
+        functools.partial(early_kernel, heads, group),
+        grid=(count // group,),
+        in_specs=[square, tall, tall, spec((group * CHUNK, heads * DV), lambda g: (g, 0))],
+        out_specs=[square, square, tall],
+        out_shape=[
+            jax.ShapeDtypeStruct((heads, count, CHUNK, CHUNK), F32),
+            jax.ShapeDtypeStruct((heads, count, CHUNK, DK), F32),
+            jax.ShapeDtypeStruct((heads, count, CHUNK, DV), F32),
+        ],
+        compiler_params=params(),
+        cost_estimate=cost(heads * count * 30 * 2 * CHUNK**3, heads * count * CHUNK * 4000),
+        name="delta_early",
+    )(scores_turned, u, s, dout)
+
+
 def grads_kernel(
-    heads, group, end_ref, qkv_ref, gt_ref, tt_ref, a_ref, at_ref, lk_ref, u_ref, s_ref,
-    ds_ref, back_ref, do_ref, dqkv_ref, dgt_ref,
+    heads, group, end_ref, qkv_ref, gt_ref, tt_ref, a_ref, lk_ref, u_ref, s_ref,
+    ds_ref, back_ref, da_ref, dqd_ref, dua_ref, dqkv_ref, dgt_ref,
 ):
     row, col = rows_cols()
     lane = lax.broadcasted_iota(jnp.int32, (CHUNK, GATE_LANES), 1)
@@ -409,21 +443,16 @@
     keys = {(h, c): qkv_ref[at[h, c], (4 * h + 1) * DK : (4 * h + 2) * DK] for h, c in pairs}
     queries = {(h, c): qkv_ref[at[h, c], 4 * h * DK : (4 * h + 1) * DK] for h, c in pairs}
     vals = {(h, c): qkv_ref[at[h, c], (2 * h + 1) * DV : (2 * h + 2) * DV] for h, c in pairs}
-    douts = {(h, c): do_ref[at[h, c], h * DV : (h + 1) * DV] for h, c in pairs}
     after = {(h, c): ds_ref[h, c] + d3(back_ref[h, c], end_ref[h]) for h, c in pairs}
-    after_low = {p: after[p] for p in pairs}
     du = {
-        (h, c): dx(at_ref[h, c], douts[h, c])
-        + dx(parts[h, c][3] * keys[h, c], after_low[h, c])
-        for h, c in pairs
+        (h, c): dua_ref[h, c] + dx(parts[h, c][3] * keys[h, c], after[h, c]) for h, c in pairs
     }
     x = {(h, c): dx(tt_ref[h, c], du[h, c]) for h, c in pairs}
-    x_low = {p: x[p] for p in pairs}
-    y = {(h, c): -dx(x_low[h, c], s_ref[h, c], NT) for h, c in pairs}
-    da = {(h, c): dx(douts[h, c], u_ref[h, c], NT) for h, c in pairs}
-    dqd = {(h, c): dx(douts[h, c], s_ref[h, c], NT) for h, c in pairs}
-    dke = {(h, c): dx(u_ref[h, c], after_low[h, c], NT) for h, c in pairs}
-    dl = {(h, c): dx(x_low[h, c], u_ref[h, c], NT) for h, c in pairs}
+    y = {(h, c): -dx(x[h, c], s_ref[h, c], NT) for h, c in pairs}
+    da = {(h, c): da_ref[h, c] for h, c in pairs}
+    dqd = {(h, c): dqd_ref[h, c] for h, c in pairs}
+    dke = {(h, c): dx(u_ref[h, c], after[h, c], NT) for h, c in pairs}
+    dl = {(h, c): dx(x[h, c], u_ref[h, c], NT) for h, c in pairs}
     for h, c in pairs:
         p = (h, c)
         beta, decays, carried, to_end = parts[p]
@@ -458,14 +487,13 @@
         dgt_ref[h, at[p], :] = jnp.where(lane == 0, dlog, jnp.where(lane == 1, dbeta, 0.0))
 
 
-def delta_grads(grad_end, qkv, gates, inv_turned, scores, scores_turned, kept, u, s, ds, back, dout):
+def delta_grads(grad_end, qkv, gates, inv_turned, scores, kept, u, s, ds, back, early):
     heads, tokens, _ = gates.shape
     count = tokens // CHUNK
     group = min(2, count)
     rows = group * CHUNK
     square = spec((heads, group, CHUNK, CHUNK), lambda g: (0, g, 0, 0))
     tall = spec((heads, group, CHUNK, DV), lambda g: (0, g, 0, 0))
-    flat = spec((rows, heads * DV), lambda g: (g, 0))
     gate_spec = spec((heads, rows, GATE_LANES), lambda g: (0, g, 0))
     wide = spec((rows, heads * 2 * DV), lambda g: (g, 0))
     return pl.pallas_call(
@@ -478,12 +506,13 @@
             square,
             square,
             square,
-            square,
             tall,
             tall,
             tall,
             square,
-            flat,
+            square,
+            square,
+            tall,
         ],
         out_specs=[wide, gate_spec],
         out_shape=[
@@ -493,24 +522,21 @@
         compiler_params=params(),
         cost_estimate=cost(heads * count * 30 * 2 * CHUNK**3 * 8, heads * count * CHUNK * 12000),
         name="delta_grads",
-    )(grad_end, qkv, gates, inv_turned, scores, scores_turned, kept, u, s, ds, back, dout)
-
-
-def front_act(x, rim, mask_ref, taps, tokens):
+    )(grad_end, qkv, gates, inv_turned, scores, kept, u, s, ds, back, *early)
+
+
+def front_act(x, rim, mask_ref, taps):
     extended = jnp.concatenate([rim, x], axis=0)
-    lags = [x]
+    conv = taps[0:1] * x
     for lag in range(1, 4):
         moved = pltpu.roll(extended, lag, 0)[8:]
-        lags.append(moved * mask_ref[:, 3 + lag : 4 + lag])
-    conv = taps[0:1] * lags[0]
-    for lag in range(1, 4):
-        conv = conv + taps[lag : lag + 1] * lags[lag]
-    return conv, lags
-
-
-def front_kernel(x_ref, rim_ref, mask_ref, taps_ref, y_ref):
-    tokens = x_ref.shape[0]
-    conv, _ = front_act(x_ref[...], rim_ref[...], mask_ref, taps_ref[...], tokens)
+        conv = conv + taps[lag : lag + 1] * (moved * mask_ref[:, 3 + lag : 4 + lag])
+    return conv
+
+
+def front_kernel(x_ref, rim_ref, mask_ref, taps_ref, y_ref, conv_ref):
+    conv = front_act(x_ref[...], rim_ref[8:, :], mask_ref, taps_ref[...])
+    conv_ref[...] = conv
     act = conv * jax.nn.sigmoid(conv)
     kind = pl.program_id(0) & 3
 
@@ -536,20 +562,31 @@
         grid=(cols // DK,),
         in_specs=[
             spec((tokens, DK), lambda c: (0, raw_block(c))),
-            spec((8, DK), lambda c: (0, raw_block(c))),
+            spec((16, DK), lambda c: (0, raw_block(c))),
             spec((tokens, 8), lambda c: (0, 0)),
             spec((4, DK), lambda c: (0, c)),
         ],
-        out_specs=block,
-        out_shape=jax.ShapeDtypeStruct((tokens, cols), F32),
+        out_specs=[block, block],
+        out_shape=[jax.ShapeDtypeStruct((tokens, cols), F32)] * 2,
         compiler_params=params(),
         cost_estimate=cost(tokens * cols * 40, tokens * cols * 8),
         name="front",
     )(raw, rim, masks, taps)
 
 
+def conv_back(kind, conv, back):
+    sig = jax.nn.sigmoid(conv)
+    if kind < 2:
+        act = conv * sig
+        inv = lax.rsqrt(jnp.sum(act * act, axis=-1, keepdims=True) + 1e-06)
+        unit = act * inv
+        back = back * (DK**-0.5 if kind == 0 else 1.0)
+        back = inv * (back - unit * jnp.sum(back * unit, axis=-1, keepdims=True))
+    return back * (sig * (1.0 + conv * (1.0 - sig)))
+
+
 def front_back_kernel(
-    x_ref, rim_ref, mask_ref, taps_ref, dy_ref, dg_ref, dx_ref, edge_ref, drim_ref, dtaps_ref
+    x_ref, rim_ref, conv_ref, mask_ref, taps_ref, dy_ref, dg_ref, dx_ref, edge_ref, dtaps_ref
 ):
     tokens = x_ref.shape[0]
     kind = lax.rem(pl.program_id(0), 6)
@@ -559,40 +596,55 @@
         grad = dg_ref[...]
         dx_ref[...] = grad
         edge_ref[...] = grad[tokens - 16 :].astype(F32)
-        drim_ref[...] = jnp.zeros((8, DK), F32)
         dtaps_ref[...] = jnp.zeros((4, DK), F32)
 
-    def through(normalize):
+    def through(which):
         taps = taps_ref[...]
-        conv, lags = front_act(x_ref[...], rim_ref[...], mask_ref, taps, tokens)
-        sig = jax.nn.sigmoid(conv)
-        back = dy_ref[...]
-        if normalize:
-            act = conv * sig
-            inv = lax.rsqrt(jnp.sum(act * act, axis=-1, keepdims=True) + 1e-06)
-            unit = act * inv
-            back = back * jnp.where(kind == 0, DK**-0.5, 1.0)
-            back = inv * (back - unit * jnp.sum(back * unit, axis=-1, keepdims=True))
-        dconv = back * (sig * (1.0 + conv * (1.0 - sig)))
+        x = x_ref[...]
+        dconv = conv_back(which, conv_ref[...], dy_ref[...])
+        extended = jnp.concatenate([rim_ref[8:, :], x], axis=0)
         zeros = jnp.zeros((8, DK), F32)
-        total = jnp.concatenate([zeros, taps[0:1] * dconv], axis=0)
-        for lag in range(4):
-            dtaps_ref[lag : lag + 1, :] = jnp.sum(dconv * lags[lag], axis=0, keepdims=True)
-            if lag:
-                part = (taps[lag : lag + 1] * dconv) * mask_ref[:, 3 + lag : 4 + lag]
-                part = jnp.concatenate([zeros, part], axis=0)
-                total = total + pltpu.roll(part, tokens + 8 - lag, 0)
-        drim_ref[...] = total[:8]
-        dx_ref[...] = total[8:].astype(BF16)
-        edge_ref[...] = total[tokens - 8 :]
-
-    @pl.when(kind < 2)
-    def _():
-        through(True)
-
-    @pl.when((kind >= 2) & (kind < 4))
-    def _():
-        through(False)
+        total = taps[0:1] * dconv
+        dtaps_ref[0:1, :] = jnp.sum(dconv * x, axis=0, keepdims=True)
+        for lag in range(1, 4):
+            part = jnp.concatenate([zeros, dconv * mask_ref[:, 3 + lag : 4 + lag]], axis=0)
+            part = pltpu.roll(part, tokens + 8 - lag, 0)
+            dtaps_ref[lag : lag + 1, :] = jnp.sum(part * extended, axis=0, keepdims=True)
+            total = total + taps[lag : lag + 1] * part[8:]
+        dx_ref[...] = total.astype(BF16)
+        edge_ref[...] = total[tokens - 16 :]
+
+    for which in range(3):
+
+        @pl.when((kind == which) | ((which == 2) & (kind == 3)))
+        def _():
+            through(which)
+
+
+def rim_back_kernel(heads, conv_ref, mask_ref, taps_ref, dy_ref, drim_ref):
+    drim_ref[...] = jnp.zeros_like(drim_ref)
+    zeros = jnp.zeros((8, DK), F32)
+    for h in range(heads):
+        for kind in range(4):
+            at = slice((4 * h + kind) * DK, (4 * h + kind + 1) * DK)
+            taps = taps_ref[:, at]
+            dconv = conv_back(kind, conv_ref[:, at], dy_ref[:, at])
+            total = zeros
+            for lag in range(1, 4):
+                part = jnp.concatenate([zeros, dconv * mask_ref[:, 3 + lag : 4 + lag]], axis=0)
+                total = total + taps[lag : lag + 1] * pltpu.roll(part, 16 - lag, 0)[:8]
+            drim_ref[:, (6 * h + kind) * DK : (6 * h + kind + 1) * DK] = total
+
+
+def rim_back(conv, masks, taps, dqkv, cols):
+    heads = taps.shape[1] // (4 * DK)
+    return pl.pallas_call(
+        functools.partial(rim_back_kernel, heads),
+        out_shape=jax.ShapeDtypeStruct((8, cols), F32),
+        compiler_params=params(),
+        cost_estimate=cost(1000, 100000),
+        name="rim_back",
+    )(conv[:8], masks[:8], taps, dqkv[:8])
 
 
 def act_block(c):
@@ -603,36 +655,36 @@
     return lax.div(c, 6) * 2 + jnp.maximum(lax.rem(c, 6) - 4, 0)
 
 
-def front_back(raw, rim, masks, taps, dqkv, dg):
+def front_back(raw, rim, conv, masks, taps, dqkv, dg):
     tokens, cols = raw.shape
     block = spec((tokens, DK), lambda c: (0, c))
+    act_spec = spec((tokens, DK), lambda c: (0, act_block(c)))
     return pl.pallas_call(
         front_back_kernel,
         grid=(cols // DK,),
         in_specs=[
             block,
-            spec((8, DK), lambda c: (0, c)),
+            spec((16, DK), lambda c: (0, c)),
+            act_spec,
             spec((tokens, 8), lambda c: (0, 0)),
             spec((4, DK), lambda c: (0, act_block(c))),
-            spec((tokens, DK), lambda c: (0, act_block(c))),
+            act_spec,
             spec((tokens, DK), lambda c: (0, gate_block(c))),
         ],
         out_specs=[
             block,
             spec((16, DK), lambda c: (0, c)),
-            spec((8, DK), lambda c: (0, c)),
             spec((4, DK), lambda c: (0, c)),
         ],
         out_shape=[
             jax.ShapeDtypeStruct((tokens, cols), BF16),
             jax.ShapeDtypeStruct((16, cols), F32),
-            jax.ShapeDtypeStruct((8, cols), F32),
             jax.ShapeDtypeStruct((4, cols), F32),
         ],
         compiler_params=params(),
-        cost_estimate=cost(tokens * cols * 80, tokens * cols * 10),
+        cost_estimate=cost(tokens * cols * 80, tokens * cols * 14),
         name="front_back",
-    )(raw, rim, masks, taps, dqkv, dg)
+    )(raw, rim, conv, masks, taps, dqkv, dg)
 
 
 def flip(value, bit):
@@ -893,7 +945,7 @@
             helds[w] = {
                 r: helds[w][r] + gots[w][aways[w].index(r | (1 << bit))].astype(F32) for r in rels[w]
             }
-    return jnp.concatenate([helds[0][0], helds[1][0]], axis=0)
+    return jnp.concatenate([helds[0][0], helds[1][0]], axis=0), kept
 
 
 def sum_mp(value):
@@ -927,7 +979,19 @@
 TN = (((0,), (0,)), ((), ()))
 
 
-def first_kernel(heads, count, rows, x_ref, w_ref, mask_ref, scale_ref, bias_ref, raw_ref, pre_ref, gate_ref):
+def first_kernel(
+    heads, count, rows, x_ref, rim_ref, w_ref, mask_ref, scale_ref, bias_ref,
+    raw_ref, pre_ref, gate_ref, rim_raw_ref,
+):
+    @pl.when(pl.program_id(0) == 0)
+    def _():
+        total = None
+        for s in range(count):
+            at = s * (rows + 16)
+            part = d1(rim_ref[:, s * rows : (s + 1) * rows], w_ref[at : at + rows, :])
+            total = part if total is None else total + part
+        rim_raw_ref[...] = total
+
     raw, pre = None, None
     for s in range(count):
         at = s * (rows + 16)
@@ -949,7 +1013,7 @@
         )
 
 
-def project_first(normed, mixer, masks, scale, bias):
+def project_first(normed, rim, mixer, masks, scale, bias):
     tokens, width = normed.shape
     count = lax.axis_size("seq")
     rows, cols = mixer.shape[0] // count - 16, mixer.shape[1]
@@ -961,6 +1025,7 @@
         grid=(tokens // tile,),
         in_specs=[
             spec((tile, width), lambda i: (i, 0)),
+            spec((16, width), lambda i: (0, 0)),
             spec(mixer.shape, lambda i: (0, 0)),
             spec((tile, 8), lambda i: (i, 0)),
             scalar,
@@ -970,16 +1035,18 @@
             spec((tile, cols), lambda i: (i, 0)),
             spec((tile, 16), lambda i: (i, 0)),
             spec((heads, tile, 8), lambda i: (0, i, 0)),
+            spec((16, cols), lambda i: (0, 0)),
         ],
         out_shape=[
             jax.ShapeDtypeStruct((tokens, cols), F32),
             jax.ShapeDtypeStruct((tokens, 16), F32),
             jax.ShapeDtypeStruct((heads, tokens, 8), F32),
+            jax.ShapeDtypeStruct((16, cols), F32),
         ],
         compiler_params=params(),
         cost_estimate=cost(2 * tokens * width * cols, tokens * width * 2 + width * cols * 2),
         name="project_first",
-    )(normed, mixer, masks, scale, bias)
+    )(normed, rim, mixer, masks, scale, bias)
 
 
 def gates_back_kernel(heads, pre_ref, dg_ref, scale_ref, bias_ref, low_ref, sums_ref):
@@ -1020,41 +1087,53 @@
     )(pre, dgates, scale, bias)
 
 
-def ffn_kernel(units, at, x_ref, dy_ref, gu_ref, down_ref, hid_ref, dgu_ref):
-    x = x_ref[...]
-    gate = d1(x, gu_ref[:, :units])
-    up = d1(x, gu_ref[:, at : at + units])
+def unpack(value, units):
+    whole = units // 128 * 128
+    rest = value[:, 2 * whole :]
+    tail = units - whole
+    gate = jnp.concatenate([value[:, :whole], rest[:, :tail]], axis=1)
+    return gate, jnp.concatenate([value[:, whole : 2 * whole], rest[:, tail:]], axis=1)
+
+
+def pack(gate, up):
+    whole = gate.shape[1] // 128 * 128
+    return jnp.concatenate(
+        [gate[:, :whole], up[:, :whole], gate[:, whole:], up[:, whole:]], axis=1
+    )
+
+
+def ffn_kernel(units, x_ref, dy_ref, gu_ref, down_ref, hid_ref, dgu_ref):
+    gate, up = unpack(d1(x_ref[...], gu_ref[...]), units)
     back = d1(dy_ref[...], down_ref[...], NT)
     sig = jax.nn.sigmoid(gate)
     silu = gate * sig
     hid_ref[...] = (silu * up).astype(BF16)
-    dgu_ref[:, units:at] = jnp.zeros((x.shape[0], at - units), BF16)
-    dgu_ref[:, :units] = (back * up * sig * (1.0 + gate * (1.0 - sig))).astype(BF16)
-    dgu_ref[:, at : at + units] = (back * silu).astype(BF16)
+    dgu_ref[...] = pack(
+        (back * up * sig * (1.0 + gate * (1.0 - sig))), (back * silu)
+    ).astype(BF16)
 
 
 def ffn(normed2, full_grad, gu_full, down_full):
     tokens, width = normed2.shape
     units = down_full.shape[0]
-    both = gu_full.shape[1]
     tile = 256
     row_spec = spec((tile, width), lambda i: (i, 0))
     return pl.pallas_call(
-        functools.partial(ffn_kernel, units, both - units),
+        functools.partial(ffn_kernel, units),
         grid=(tokens // tile,),
         in_specs=[
             row_spec,
             row_spec,
-            spec((width, both), lambda i: (0, 0)),
+            spec((width, 2 * units), lambda i: (0, 0)),
             spec((units, width), lambda i: (0, 0)),
         ],
         out_specs=[
             spec((tile, units), lambda i: (i, 0)),
-            spec((tile, both), lambda i: (i, 0)),
+            spec((tile, 2 * units), lambda i: (i, 0)),
         ],
         out_shape=[
             jax.ShapeDtypeStruct((tokens, units), BF16),
-            jax.ShapeDtypeStruct((tokens, both), BF16),
+            jax.ShapeDtypeStruct((tokens, 2 * units), BF16),
         ],
         compiler_params=params(),
         cost_estimate=cost(6 * tokens * width * units, tokens * width * 4 + width * units * 6),
@@ -1138,14 +1217,13 @@
     masks = jnp.stack([zero] * 2 + [ids_f, prior_f] + same + [zero], axis=1)
 
     units = w_gate.shape[1]
-    spare = -units % 128
     mix_cols = heads * (2 * DK + 2 * DV)
     gate_part = jnp.pad(
         w_gates.reshape(rows, 2 * heads).T, ((0, 16 - 2 * heads), (0, mix_cols - rows))
     )
     mixer_part = jnp.concatenate([w_mixer.reshape(rows, mix_cols), gate_part])
     do_part = jnp.concatenate([w_out, w_down])
-    gu_part = jnp.concatenate([w_gate, jnp.zeros((rows, spare), BF16), w_up], axis=1)
+    gu_part = pack(w_gate, w_up)
     mixer_full = lax.all_gather(mixer_part, "seq", axis=0, tiled=True)
     found_res = gather_mp(residual)
     do_full = lax.all_gather(after(do_part, found_res[0][0]), "seq", axis=1, tiled=True)
@@ -1155,10 +1233,12 @@
     found_og = gather_mp(after(out_grad, normed))
     full_grad = assemble(found_og, mp_pos)[0]
     mixer_full = after(mixer_full, full_grad)
-    raw, gate_pre, gates = project_first(normed, mixer_full, masks, decay_scale, dt_bias)
+    rim_normed = shifted(normed[tokens - 16 :], 1)
+    raw, gate_pre, gates, rim = project_first(
+        normed, rim_normed, mixer_full, masks, decay_scale, dt_bias
+    )
     taps = conv_taps.reshape(4, heads * 2 * DV)
-    rim = shifted(raw[tokens - 8 :], 1)
-    qkv = front(raw, rim, masks, taps)
+    qkv, conv = front(raw, rim, masks, taps)
 
     inverse, inv_turned, scores, scores_turned, kept, wkeys, reach, reach_turned, steps, steps_turned = (
         delta_prep(qkv, gates)
@@ -1171,52 +1251,55 @@
     )
 
     out_full, down_full = do_full[: w_out.shape[0]], do_full[w_out.shape[0] :]
-    branch = reduce_mp([(mixed, out_full, False)], mp_pos, cols)
+    branch, _ = reduce_mp([(mixed, out_full, False)], mp_pos, cols)
     middle = residual.astype(F32) + branch
     found_mid = gather_mp(middle.astype(BF16))
     normed2, _ = assemble(found_mid, mp_pos, ffn_gain)
     hidden, grad_gu = ffn(normed2, full_grad, gu_full, down_full)
     part_gu = dot(normed2, grad_gu, TN).astype(BF16)
-    grad_normed2 = reduce_mp([(grad_gu, gu_full, True)], mp_pos, cols)
+    grad_gu = after(grad_gu, part_gu)
+    grad_normed2, kept_gn2 = reduce_mp([(grad_gu, gu_full, True)], mp_pos, cols)
     dw_gu = lax.psum_scatter(part_gu, "seq", scatter_dimension=0, tiled=True)
-    part_down = dot(hidden, full_grad, TN).astype(BF16)
-    grad_normed2 = after(grad_normed2, part_gu)
+    part_down = dot(after(hidden, kept_gn2), full_grad, TN).astype(BF16)
     found_gn2 = gather_mp(grad_normed2.astype(BF16))
 
     grad_branch, grad_middle, dffn_gain = norm_back(
         found_gn2, found_mid, full_grad, ffn_gain, grad_normed2, middle, mp_pos
     )
     grad_mixed = dot(grad_branch, out_full, NT)
-    part_out = dot(mixed, grad_branch, TN).astype(BF16)
-    dw_do = lax.psum_scatter(
-        jnp.concatenate([part_out, part_down]), "seq", scatter_dimension=1, tiled=True
-    )
-    ffn_part = reduce_mp([(after(hidden, grad_branch), down_full, False)], mp_pos, cols)
-    output = (middle + ffn_part).astype(BF16)
 
     dout, dg_raw, dhead_gain, dstates, dstart = delta_tail(
         grad_mixed, outs, raw, head_gain, reach_turned, steps_turned
     )
+    part_out = dot(mixed, after(grad_branch, dstart), TN).astype(BF16)
+    part_do = jnp.concatenate([part_out, part_down])
+    dw_do = lax.psum_scatter(part_do, "seq", scatter_dimension=1, tiled=True)
+    early = delta_early(scores_turned, corrected, held, after(dout, dstart))
     grad_end = chain(back[:, 0], dstart, -1)
-    grad_end = after(grad_end, output, part_out)
+    grad_end = after(grad_end, part_do, early)
     dqkv, dgates = delta_grads(
-        grad_end, qkv, gates, inv_turned, scores, scores_turned, kept, corrected, held,
-        dstates, back[:, 1:], dout,
+        grad_end, qkv, gates, inv_turned, scores, kept, corrected, held, dstates, back[:, 1:],
+        early,
     )
-    dproj, edge, drim, dtaps = front_back(raw, rim, masks, taps, dqkv, dg_raw)
-    edge = jnp.concatenate([edge[:8], edge[8:] + shifted(drim, -1)])
+    drim = rim_back(conv, masks, taps, dqkv, mix_cols)
+    came = shifted(drim, -1)
+    dproj, edge, dtaps = front_back(raw, rim, conv, masks, taps, after(dqkv, drim), dg_raw)
+    edge = jnp.concatenate([edge[:8], edge[8:] + came])
     dproj = lax.dynamic_update_slice_in_dim(dproj, edge.astype(BF16), tokens - 16, 0)
     dgate_low, gate_sums = gates_back(gate_pre, dgates, decay_scale, dt_bias)
 
     part_mixer = dot(normed, dproj, TN).astype(BF16)
     dw_mixer = lax.psum_scatter(part_mixer, "seq", scatter_dimension=0, tiled=True)
+    dproj, dgate_low = after((dproj, dgate_low), part_mixer)
     part_gates = dot(dgate_low, normed, TN)
     gates_full = jnp.swapaxes(
         mixer_full.reshape(seq_count, rows + 16, mix_cols)[:, rows:, :rows], 0, 1
     ).reshape(16, width)
-    grad_normed = reduce_mp(
+    grad_normed, kept_gn = reduce_mp(
         [(dproj, mixer_full, None), (dgate_low, gates_full, False)], mp_pos, cols
     )
+    ffn_part, _ = reduce_mp([(after(hidden, kept_gn), down_full, False)], mp_pos, cols)
+    output = (middle + ffn_part).astype(BF16)
     own_gain = lax.dynamic_slice_in_dim(attn_gain, mp_pos * cols, cols)
     own_res = residual.astype(F32)
     inv1 = inv1[:, :1]
@@ -1225,6 +1308,8 @@
     mean = sum_mp(mean).reshape(tokens, 1) * (1.0 / width)
     grad_residual = grad_middle + inv1 * (scaled - own_res * (inv1 * inv1 * mean))
     dattn_gain = jnp.sum(grad_normed * own_res * inv1, axis=0)
+
+    dw_gate, dw_up = unpack(dw_gu, units)
 
     dtaps = dtaps.reshape(4, heads, 2 * DK + 2 * DV)[:, :, : 2 * DK + DV]
     small = [
@@ -1254,8 +1339,8 @@
         sums[2],
         dw_do[: w_out.shape[0]].astype(F32),
         gains[1],
-        dw_gu[:, :units].astype(F32),
-        dw_gu[:, units + spare :].astype(F32),
+        dw_gate.astype(F32),
+        dw_up.astype(F32),
         dw_do[w_out.shape[0] :].astype(F32),
     )
 

time: 717 us -> 698 us (0.974)
  waiting for transfers between devices: 321 us -> 287 us
  Pallas kernels: 181 us -> 193 us
  local copies, waits for them, and re-layouts: 40.3 us -> 49.4 us
    ppermute x8, waiting for transfers between devices: 54.6 us -> 30.4 us  [shifted(): lax.ppermute(value, 'seq', [(i, i + steps) for i in range(first, last)])]
    all_gather x1, waiting for transfers between devices: 0.02 us -> 11.6 us  [shards(): lax.all_gather(after(do_part, found_res[0][0]), 'seq', axis=1, tiled=True)]
    all_gather x1, waiting for transfers between devices: 53 us -> 43.9 us  [shards(): mixer_full = lax.all_gather(mixer_part, 'seq', axis=0, tiled=True)]
    ppermute x3, waiting for transfers between devices: 8.5 us -> 0.01 us  [sum_seq(): lax.ppermute(value, 'seq', [(i, (i + step) % count) for i in range(count)])]
    ppermute x8, starting transfers between devices: 30 us -> 22.8 us  [shifted(): lax.ppermute(value, 'seq', [(i, i + steps) for i in range(first, last)])]
    pallas_call x1 -> x3, Pallas kernels: 15.5 us -> 21.7 us  [the longest x1 15.8 us: ffn(): pl.pallas_call(functools.partial(ffn_kernel, units), grid=(tokens // tile...]
    unnamed x150 -> x178, local copies, waits for them, and re-layouts: 22 us -> 26.2 us
  transfers between devices with their start and end apart: 67 -> 67, of which waited for: 52 -> 47; matrix products, arithmetic and copies ran while one was open for 11% -> 12% of each run, Pallas kernels for 23% -> 26%
where the time goes in v2:
time: 698 us; the launch traced here: 692 us
  waiting for transfers between devices  287 us (41%)
  Pallas kernels  193 us (28%)
  starting transfers between devices  71.9 us (10%)
  local copies, waits for them, and re-layouts  49.4 us (7%)
  other arithmetic  38.5 us (6%)
  matrix products  36 us (5%)
  between operations  15.7 us (2%)
    ppermute x50, waiting for transfers between devices, flip(): return lax.ppermute(value, 'mp', [(i, i ^ 1 << bit) for i in range(count)])  137 us
    all_gather x1, waiting for transfers between devices, shards(): mixer_full = lax.all_gather(mixer_part, 'seq', axis=0, tiled=True)  43.9 us
    ppermute x50, starting transfers between devices, flip(): return lax.ppermute(value, 'mp', [(i, i ^ 1 << bit) for i in range(count)])  42.8 us
    pallas_call x8, Pallas kernels, block_products(): pl.pallas_call(functools.partial(block_kernel, [t[2] for t in terms]), gr...  40.7 us
    all_gather x1, waiting for transfers between devices, shards(): gu_full = lax.all_gather(after(gu_part, normed), 'seq', axis=0, tiled=True)  35.6 us
    dot_general x6, matrix products, dot(): return lax.dot_general(left, right, dims, preferred_element_type=F32)  35 us
    ppermute x8, waiting for transfers between devices, shifted(): lax.ppermute(value, 'seq', [(i, i + steps) for i in range(first, last)])  30.4 us
    reduce_scatter x1, waiting for transfers between devices, shards(): lax.psum_scatter(part_mixer, 'seq', scatter_dimension=0, tiled=True)  29.1 us
  transfers between devices with their start and end apart: 67, of which 47 were waited for; matrix products, arithmetic and copies ran while one was open for 12% of the time, Pallas kernels for 26%

profile of v2, /device:TPU:0, one launch (start us, length us, event | category | flops | bytes accessed | tf_op | source)
XLA Modules:
  0.0 691.8 jit_solution(11676403922113545645)
XLA Ops:
  14.9 4.8 collective-permute-done
  25.1 9.7 %collective-permute-done.2 = bf16[2,512,256]{2,1,0:T(8,128)(2,1)} collective-permute-done((bf16[2,512,256]{2,1,0:T(8,128)(2,1)}, bf16[2,512,256]{2,1,0:T(8,128)(2,1)}, u32[]{:S(2)}, u32[]{:S(2)}) %collective-permute-start.2) | collective-permute-done | bytes 524320 | tf_op jit(solution)/shard_map/ppermute | solution.py:692
  41.7 5.5 assemble.3
  48.5 7.1 %collective-permute-done.7 = bf16[1,512,256]{2,1,0:T(8,128)(2,1)S(1)} collective-permute-done((bf16[1,512,256]{2,1,0:T(8,128)(2,1)S(1)}, bf16[1,512,256]{2,1,0:T(8,128)(2,1)S(1)}, u32[]{:S(2)}, u32[]{:S(2)}) %collective-permute-start.7) | collective-permute-done | bytes 262176 | tf_op jit(solution)/shard_map/ppermute | solution.py:692
  58.1 11.0 %collective-permute-done.10 = bf16[2,512,256]{2,1,0:T(8,128)(2,1)S(1)} collective-permute-done((bf16[2,512,256]{2,1,0:T(8,128)(2,1)S(1)}, bf16[2,512,256]{2,1,0:T(8,128)(2,1)S(1)}, u32[]{:S(2)}, u32[]{:S(2)}) %collective-permute-start.10) | collective-permute-done | bytes 524320 | tf_op jit(solution)/shard_map/ppermute | solution.py:692
  83.1 4.7 assemble.4.dy_ref.refs_9_
  87.7 43.9 %all-gather.4.cloned.1.call-done.w_ref.refs_1_ = bf16[2112,1536]{1,0:T(8,128)(2,1)} async-done(((bf16[528,1536]{1,0:T(8,128)(2,1)}), bf16[2112,1536]{1,0:T(8,128)(2,1)}) %all-gather.4.cloned.1.call-update) | async-done | bytes 6488080 | tf_op jit(solution)/shard_map/all_gather | solution.py:1227
  131.7 14.3 %project_first.1 = (f32[1024,1536]{1,0:T(8,128)}, f32[1024,16]{1,0:T(8,128)S(1)}, f32[2,1024,8]{2,1,0:T(8,128)S(1)}, f32[16,1536]{1,0:T(8,128)S(1)}) custom-call(bf16[1024,2048]{1,0:T(8,128)(2,1)} %get-tuple-element.168.x_ref, bf16[16,2048]{1,0:T(8,128)(2,1)S(1)} %collective-permute-done.6.rim_ref, ...), custom_call_target="tpu_custom_call" | custom-call | flops 64424508 | bytes 104857 | tf_op jit(solution)/shard_map/project_first/pallas_call | solution.py:1023
  147.8 9.7 %front.1 = (f32[1024,1024]{1,0:T(8,128)S(1)}, f32[1024,1024]{1,0:T(8,128)}) custom-call(f32[1024,1536]{1,0:T(8,128)} %get-tuple-element.183.x_ref.refs_0_.refs_1_, f32[16,1536]{1,0:T(8,128)S(1)} %get-tuple-element.184.rim_ref, f32[1024,8]{1,0:T(8,128)S(1)} %copy.56.mask_ref, f32[4,1024]{1,0:T(4,128)S(1)} %bitcast.106), custom_call_target="tpu_custom_call" | custom-call | flops 419430 | bytes 83886 | tf_op jit(solution)/shard_map/front/pallas_call | solution.py:560
  159.6 17.6 %delta_prep.1 = (f32[2,8,128,128]{3,2,1,0:T(8,128)S(1)}, f32[2,8,128,128]{3,2,1,0:T(8,128)S(1)}, f32[2,8,128,128]{3,2,1,0:T(8,128)S(1)}, f32[2,8,128,128]{3,2,1,...) custom-call(f32[1024,1024]{1,0:T(8,128)} %copy-done.2, ...), custom_call_target="tpu_custom_call" | custom-call | flops 214748368 | bytes 62914 | tf_op jit(solution)/shard_map/delta_prep/pallas_call | solution.py:149
  181.2 11.0 %delta_values.1 = (f32[2,8,128,256]{3,2,1,0:T(8,128)}, f32[1024,512]{1,0:T(8,128)}, f32[2,8,128,256]{3,2,1,0:T(8,128)}, f32[2,128,256]{2,1,0:T(8,128)S(1)}) custom-call(f32[1024,1024]{1,0:T(8,128)} %copy-done.2, f32[2,1024,8]{2,1,0:T(8,128)S(1)} %copy-done.5, f32[2,8,128,128]{3,2,1,0:T(8,128)S(1)} %get-tuple-element.190.t_ref, ...), custom_call_target="tpu_custom_call" | custom-call | flops 64424508 | bytes 81920 | tf_op jit(solution)/shard_map/delta_values/pallas_call | solution.py:231
  195.5 4.9 collective-permute-done.13
  200.6 6.5 collective-permute-start.14
  207.1 5.8 collective-permute-done.14
  213.2 5.5 collective-permute-start.15
  218.7 11.6 %all-gather.6.cloned.1.call-done = bf16[1200,2048]{1,0:T(8,128)(2,1)} async-done(((bf16[1200,512]{1,0:T(8,128)(2,1)}), bf16[1200,2048]{1,0:T(8,128)(2,1)}) %all-gather.6.cloned.1.call-update) | async-done | bytes 4915216 | tf_op jit(solution)/shard_map/all_gather | solution.py:1229
  232.3 9.5 %delta_output.1 = (bf16[1024,512]{1,0:T(8,128)(2,1)S(1)}, f32[1024,512]{1,0:T(8,128)}, f32[2,8,128,256]{3,2,1,0:T(8,128)}, f32[2,8,128,256]{3,2,1,0:T(8,128)}) custom-call(f32[2,128,256]{2,1,0:T(8,128)S(1)} %convert_element_type.422.start_ref, f32[2,8,128,256]{3,2,1,0:T(8,128)} %get-tuple-element.193.s0_ref, ...), custom_call_target="tpu_custom_call" | custom-call | flops 53687092 | bytes 122880 | tf_op jit(solution)/shard_map/delta_output/pallas_call | solution.py:296
  253.5 10.7 %collective-permute-done.17 = bf16[2,512,256]{2,1,0:T(8,128)(2,1)S(1)} collective-permute-done((bf16[2,512,256]{2,1,0:T(8,128)(2,1)S(1)}, bf16[2,512,256]{2,1,0:T(8,128)(2,1)S(1)}, u32[]{:S(2)}, u32[]{:S(2)}) %collective-permute-start.17) | collective-permute-done | bytes 524320 | tf_op jit(solution)/shard_map/ppermute | solution.py:692
  267.9 5.1 collective-permute-done.19
  276.9 5.2 collective-permute-done.21
  285.2 8.7 %collective-permute-done.23 = bf16[2,512,256]{2,1,0:T(8,128)(2,1)S(1)} collective-permute-done((bf16[2,512,256]{2,1,0:T(8,128)(2,1)S(1)}, bf16[2,512,256]{2,1,0:T(8,128)(2,1)S(1)}, u32[]{:S(2)}, u32[]{:S(2)}) %collective-permute-start.23) | collective-permute-done | bytes 524320 | tf_op jit(solution)/shard_map/ppermute | solution.py:692
  298.6 4.4 assemble.5
  305.0 35.6 %all-gather.8.cloned.1.call-done.gu_ref.refs_1_ = bf16[2048,1376]{1,0:T(8,128)(2,1)} async-done(((bf16[512,1376]{1,0:T(8,128)(2,1)}), bf16[2048,1376]{1,0:T(8,128)(2,1)}) %all-gather.8.cloned.1.call-update) | async-done | bytes 5636112 | tf_op jit(solution)/shard_map/all_gather | solution.py:1232
  340.7 15.8 %ffn.1 = (bf16[1024,688]{1,0:T(8,128)(2,1)S(1)}, bf16[1024,1376]{1,0:T(8,128)(2,1)}) custom-call(bf16[1024,2048]{1,0:T(8,128)(2,1)} %get-tuple-element.220.x_ref, bf16[1024,2048]{1,0:T(8,128)(2,1)} %assemble.4.dy_ref.refs_9_, bf16[2048,1376]{1,0:T(8,128)(2,1)} %all-gather.8.cloned.1.call-done.gu_ref.refs_1_, bf16[688,2048]{1,0:T(8,128)(2,1)S(1)} %slice.545.down_ref.refs_1_), custom_call_target="tpu_custom_call" | custom-call | flops 86570432 | bytes 168427 | tf_op jit(solution)/shard_map/ffn/pallas_call | solution.py:1121
  357.7 9.8 %convolution_convert_fusion.1 = bf16[2048,1376]{0,1:T(8,128)(2,1)} fusion(bf16[1024,2048]{1,0:T(8,128)(2,1)S(1)} %copy-done.73, bf16[1024,1376]{1,0:T(8,128)(2,1)} %get-tuple-element.226.refs_0_), kind=kOutput, calls=%fused_computation.1 | convolution fusion | flops 5774180352 | bytes 12648448 | tf_op jit(solution)/shard_map/dot_general | solution.py:976
  369.3 5.5 block_products.11
  375.0 6.7 block_products.10
  386.9 11.4 %collective-permute-done.28 = bf16[2,512,256]{2,1,0:T(8,128)(2,1)S(1)} collective-permute-done((bf16[2,512,256]{2,1,0:T(8,128)(2,1)S(1)}, bf16[2,512,256]{2,1,0:T(8,128)(2,1)S(1)}, u32[]{:S(2)}, u32[]{:S(2)}) %collective-permute-start.28) | collective-permute-done | bytes 524320 | tf_op jit(solution)/shard_map/ppermute | solution.py:692
  401.8 5.7 collective-permute-done.30
  410.2 5.5 collective-permute-done.32
  418.3 9.1 %collective-permute-done.34 = bf16[2,512,256]{2,1,0:T(8,128)(2,1)S(1)} collective-permute-done((bf16[2,512,256]{2,1,0:T(8,128)(2,1)S(1)}, bf16[2,512,256]{2,1,0:T(8,128)(2,1)S(1)}, u32[]{:S(2)}, u32[]{:S(2)}) %collective-permute-start.34) | collective-permute-done | bytes 524320 | tf_op jit(solution)/shard_map/ppermute | solution.py:692
  433.0 9.3 %norm_back.1 = (bf16[1024,2048]{1,0:T(8,128)(2,1)}, f32[1024,256]{1,0:T(8,128)S(1)}, f32[1,256]{1,0:T(1,128)S(1)}) custom-call(s32[1]{0:T(128)} %bitcast.refs_0_.mp_ref, bf16[4,512,256]{2,1,0:T(8,128)(2,1)S(1)} %pad_maximum_fusion.9.refs_1_, bf16[4,512,256]{2,1,0:T(8,128)(2,1)S(1)} %collective-permute-done.36.refs_2_, ...), custom_call_target="tpu_custom_call" | custom-call | flops 419430 | bytes 167772 | tf_op jit(solution)/shard_map/norm_back/pallas_call | solution.py:846
  443.3 6.7 fusion.85.dm_ref
  450.0 7.6 %delta_tail.1 = (f32[1024,512]{1,0:T(8,128)S(1)}, bf16[1024,512]{1,0:T(8,128)(2,1)S(1)}, f32[2,256]{1,0:T(2,128)S(1)}, f32[2,8,128,256]{3,2,1,0:T(8,128)}, f32[2,128,256]{2,1,0:T(8,128)S(1)}) custom-call(f32[1024,512]{1,0:T(8,128)} %fusion.85.dm_ref, f32[1024,512]{1,0:T(8,128)} %get-tuple-element.248.o_ref, f32[2,256]{1,0:T(2,128)S(1)} %copy-done.51, ...), custom_call_target="tpu_custom_call" | custom-call | flops 53687092 | bytes 122880 | tf_op jit(solution)/shard_map/delta_tail/pallas_call | solution.py:374
  457.6 5.7 convolution_convert_fusion.3
  468.0 6.0 collective-permute-done.38
  475.6 12.0 %collective-permute-done.39 = bf16[2,128,256]{2,1,0:T(8,128)(2,1)S(1)} collective-permute-done((bf16[2,128,256]{2,1,0:T(8,128)(2,1)S(1)}, bf16[2,128,256]{2,1,0:T(8,128)(2,1)S(1)}, u32[]{:S(2)}, u32[]{:S(2)}) %collective-permute-start.39) | collective-permute-done | bytes 131104 | tf_op jit(solution)/shard_map/ppermute | solution.py:968
  491.0 5.7 delta_early.1
  501.8 19.9 %delta_grads.1 = (f32[1024,1024]{1,0:T(8,128)}, f32[2,1024,8]{2,1,0:T(8,128)S(1)}) custom-call(f32[2,128,256]{2,1,0:T(8,128)S(1)} %convert_element_type.469.end_ref, f32[1024,1024]{1,0:T(8,128)} %copy-done.2, f32[2,1024,8]{2,1,0:T(8,128)S(1)} %copy-done.6, f32[2,8,128,128]{3,2,1,0:T(8,128)S(1)} %copy-done.31, f32[2,8,128,128]{3,2,1,0:T(8,128)S(1)} %copy-done.18, ...), custom_call_target="tpu_custom_call" | custom-call | flops 161061280 | bytes 245760 | tf_op jit(solution)/shard_map/delta_grads/pallas_call | solution.py:499
  524.0 13.3 %front_back.1 = (bf16[1024,1536]{1,0:T(8,128)(2,1)S(1)}, f32[16,1536]{1,0:T(8,128)S(1)}, f32[4,1536]{1,0:T(4,128)S(1)}) custom-call(f32[1024,1536]{1,0:T(8,128)} %get-tuple-element.183.x_ref.refs_0_.refs_1_, f32[16,1536]{1,0:T(8,128)S(1)} %get-tuple-element.184.rim_ref, f32[1024,1024]{1,0:T(8,128)} %get-tuple-element.223.conv_ref, f32[1024,8]{1,0:T(8,128)S(1)} %copy-done.10, ...), custom_call_target="tpu_custom_call" | custom-call | flops 1258291 | bytes 220200 | tf_op jit(solution)/shard_map/front_back/pallas_call | solution.py:662
  537.4 8.7 %convolution_convert_fusion = bf16[2048,1536]{1,0:T(8,128)(2,1)} fusion(bf16[1024,2048]{1,0:T(8,128)(2,1)S(1)} %copy-done.61, bf16[1024,1536]{1,0:T(8,128)(2,1)S(1)} %maximum_dynamic-update-slice_fusion.refs_0_), kind=kOutput, calls=%fused_computation | convolution fusion | flops 6445596672 | bytes 13631488 | tf_op jit(solution)/shard_map/dot_general | solution.py:976
  551.3 6.6 block_products.15
  558.0 7.1 %block_products.12 = f32[4,1024,256]{2,1,0:T(8,128)} custom-call(s32[1]{0:T(128)} %bitcast.refs_0_.mp_ref, bf16[1024,1536]{1,0:T(8,128)(2,1)S(1)} %maximum_dynamic-update-slice_fusion.refs_0_, bf16[2112,1536]{1,0:T(8,128)(2,1)} %all-gather.4.cloned.1.call-done.w_ref.refs_1_, bf16[1024,16]{1,0:T(8,128)(2,1)S(1)} %get-tuple-element.274.refs_2_, ...), custom_call_target="tpu_custom_call" | custom-call | flops 32547800 | bytes 41943 | tf_op jit(solution)/shard_map/block_products/pallas_call | solution.py:910
  565.1 4.9 block_products.14
  586.5 8.3 %collective-permute-done.48 = bf16[2,512,256]{2,1,0:T(8,128)(2,1)S(1)} collective-permute-done((bf16[2,512,256]{2,1,0:T(8,128)(2,1)S(1)}, bf16[2,512,256]{2,1,0:T(8,128)(2,1)S(1)}, u32[]{:S(2)}, u32[]{:S(2)}) %collective-permute-start.48) | collective-permute-done | bytes 524320 | tf_op jit(solution)/shard_map/ppermute | solution.py:692
  599.6 6.4 collective-permute-done.43
  650.8 29.1 %reduce-scatter.4.cloned.1.call-done = bf16[512,1536]{1,0:T(8,128)(2,1)} async-done(((bf16[2048,1536]{1,0:T(8,128)(2,1)}), bf16[512,1536]{1,0:T(8,128)(2,1)}) %reduce-scatter.4.cloned.1.call-update) | async-done | bytes 1572880 | tf_op jit(solution)/shard_map/reduce_scatter | solution.py:1292
  679.8 4.9 reshape.219
  (421 shorter events, 191.2 us)
Async XLA Ops:
  7.2 124.5 %all-gather.4.cloned.1.call-start = ((), (), s32[]{:S(2)}) async-start(), calls=%async_computation.3 | async-start | bytes 8110080 | tf_op jit(solution)/shard_map/all_gather | solution.py:1227
  10.2 220.1 %all-gather.6.cloned.1.call-start = ((), (), s32[]{:S(2)}) async-start(), calls=%async_computation.4 | async-start | bytes 6144000 | tf_op jit(solution)/shard_map/all_gather | solution.py:1229
  10.3 9.3 %collective-permute-start = (bf16[1,512,256]{2,1,0:T(8,128)(2,1)S(1)}, bf16[1,512,256]{2,1,0:T(8,128)(2,1)S(1)}, u32[]{:S(2)}, u32[]{:S(2)}) collective-permute-start(bf16[1,512,256]{2,1,0:T(8,128)(2,1)S(1)} %get-tuple-element.156), channel_id=1, source_target_pairs={{0,4},{1,5},{2,6},{3,7},{4,0},{5,1},{6,2},{7,3},{8,12},{9,13},{10,... | collective-permute-start | bytes 786440 | tf_op jit(solution)/shard_map/ppermute | solution.py:692
  13.4 7.8 %collective-permute-start.1 = (bf16[1,512,256]{2,1,0:T(8,128)(2,1)S(1)}, bf16[1,512,256]{2,1,0:T(8,128)(2,1)S(1)}, u32[]{:S(2)}, u32[]{:S(2)}) collective-permute-start(bf16[1,512,256]{2,1,0:T(8,128)(2,1)S(1)} %get-tuple-element.157), channel_id=1, source_target_pairs={{0,2},{1,3},{2,0},{3,1},{4,6},{5,7},{6,4},{7,5},{8,10},{9,11},{10,... | collective-permute-start | bytes 786440 | tf_op jit(solution)/shard_map/ppermute | solution.py:692
  22.0 12.8 %collective-permute-start.2 = (bf16[2,512,256]{2,1,0:T(8,128)(2,1)}, bf16[2,512,256]{2,1,0:T(8,128)(2,1)}, u32[]{:S(2)}, u32[]{:S(2)}) collective-permute-start(bf16[2,512,256]{2,1,0:T(8,128)(2,1)} %pad_maximum_fusion.12), channel_id=1, source_target_pairs={{0,2},{1,3},{2,0},{3,1},{4,6},{5,7},{6,4},{7,5},{8,10},{9,11},{10,... | collective-permute-start | bytes 1572872 | tf_op jit(solution)/shard_map/ppermute | solution.py:692
  23.5 12.3 %collective-permute-start.3 = (bf16[2,512,256]{2,1,0:T(8,128)(2,1)S(1)}, bf16[2,512,256]{2,1,0:T(8,128)(2,1)}, u32[]{:S(2)}, u32[]{:S(2)}) collective-permute-start(bf16[2,512,256]{2,1,0:T(8,128)(2,1)S(1)} %pad_maximum_fusion.13), channel_id=1, source_target_pairs={{0,4},{1,5},{2,6},{3,7},{4,0},{5,1},{6,2},{7,3},{8,12},{9,13},{10,... | collective-permute-start | bytes 1572872 | tf_op jit(solution)/shard_map/ppermute | solution.py:692
  37.3 303.4 %all-gather.8.cloned.1.call-start = ((), (), s32[]{:S(2)}) async-start(), calls=%async_computation.5 | async-start | bytes 7208960 | tf_op jit(solution)/shard_map/all_gather | solution.py:1232
  47.2 8.4 %collective-permute-start.7 = (bf16[1,512,256]{2,1,0:T(8,128)(2,1)S(1)}, bf16[1,512,256]{2,1,0:T(8,128)(2,1)S(1)}, u32[]{:S(2)}, u32[]{:S(2)}) collective-permute-start(bf16[1,512,256]{2,1,0:T(8,128)(2,1)S(1)} %get-tuple-element.170), channel_id=1, source_target_pairs={{0,4},{1,5},{2,6},{3,7},{4,0},{5,1},{6,2},{7,3},{8,12},{9,13},{10,... | collective-permute-start | bytes 786440 | tf_op jit(solution)/shard_map/ppermute | solution.py:692
  47.9 8.1 %collective-permute-start.8 = (bf16[1,512,256]{2,1,0:T(8,128)(2,1)S(1)}, bf16[1,512,256]{2,1,0:T(8,128)(2,1)S(1)}, u32[]{:S(2)}, u32[]{:S(2)}) collective-permute-start(bf16[1,512,256]{2,1,0:T(8,128)(2,1)S(1)} %get-tuple-element.171), channel_id=1, source_target_pairs={{0,2},{1,3},{2,0},{3,1},{4,6},{5,7},{6,4},{7,5},{8,10},{9,11},{10,... | collective-permute-start | bytes 786440 | tf_op jit(solution)/shard_map/ppermute | solution.py:692
  56.1 13.0 %collective-permute-start.10 = (bf16[2,512,256]{2,1,0:T(8,128)(2,1)S(1)}, bf16[2,512,256]{2,1,0:T(8,128)(2,1)S(1)}, u32[]{:S(2)}, u32[]{:S(2)}) collective-permute-start(bf16[2,512,256]{2,1,0:T(8,128)(2,1)S(1)} %pad_maximum_fusion.15), channel_id=1, source_target_pairs={{0,4},{1,5},{2,6},{3,7},{4,0},{5,1},{6,2},{7,3},{8,12},{9,13},{10,... | collective-permute-start | bytes 1572872 | tf_op jit(solution)/shard_map/ppermute | solution.py:692
  57.5 12.6 %collective-permute-start.9 = (bf16[2,512,256]{2,1,0:T(8,128)(2,1)S(1)}, bf16[2,512,256]{2,1,0:T(8,128)(2,1)S(1)}, u32[]{:S(2)}, u32[]{:S(2)}) collective-permute-start(bf16[2,512,256]{2,1,0:T(8,128)(2,1)S(1)} %pad_maximum_fusion.14), channel_id=1, source_target_pairs={{0,2},{1,3},{2,0},{3,1},{4,6},{5,7},{6,4},{7,5},{8,10},{9,11},{10,... | collective-permute-start | bytes 1572872 | tf_op jit(solution)/shard_map/ppermute | solution.py:692
  70.4 12.6 %collective-permute-start.11 = (bf16[4,512,256]{2,1,0:T(8,128)(2,1)S(1)}, bf16[4,512,256]{2,1,0:T(8,128)(2,1)}, u32[]{:S(2)}, u32[]{:S(2)}) collective-permute-start(bf16[4,512,256]{2,1,0:T(8,128)(2,1)S(1)} %pad_maximum_fusion.4.refs_1_), channel_id=1, source_target_pairs={{0,1},{1,0},{2,3},{3,2},{4,5},{5,4},{6,7},{7,6},{8,9},{9,8},{10,11... | collective-permute-start | bytes 3145736 | tf_op jit(solution)/shard_map/ppermute | solution.py:692
  70.5 12.5 %collective-permute-start.12 = (bf16[4,512,256]{2,1,0:T(8,128)(2,1)S(1)}, bf16[4,512,256]{2,1,0:T(8,128)(2,1)}, u32[]{:S(2)}, u32[]{:S(2)}) collective-permute-start(bf16[4,512,256]{2,1,0:T(8,128)(2,1)S(1)} %pad_maximum_fusion.5.refs_3_), channel_id=1, source_target_pairs={{0,1},{1,0},{2,3},{3,2},{4,5},{5,4},{6,7},{7,6},{8,9},{9,8},{10,11... | collective-permute-start | bytes 3145736 | tf_op jit(solution)/shard_map/ppermute | solution.py:692
  77.7 563.8 %reduce-scatter.8.cloned.1.call-start = ((), (), s32[]{:S(2)}) async-start(), calls=%async_computation.8 | async-start | bytes 7045120 | tf_op jit(solution)/shard_map/reduce_scatter | solution.py:1262
  78.8 52.9 %collective-permute-start.6 = (bf16[16,2048]{1,0:T(8,128)(2,1)S(1)}, bf16[16,2048]{1,0:T(8,128)(2,1)S(1)}, u32[]{:S(2)}, u32[]{:S(2)}) collective-permute-start(bf16[16,2048]{1,0:T(8,128)(2,1)S(1)} %slice.397), channel_id=1, source_target_pairs={{0,8},{8,16},{16,24},{1,9},{9,17},{17,25},{2,10},{10,18},{18,26},{... | collective-permute-start | bytes 196616 | tf_op jit(solution)/shard_map/ppermute | solution.py:968
  192.2 8.1 %collective-permute-start.13 = (bf16[2,128,256]{2,1,0:T(8,128)(2,1)S(1)}, bf16[2,128,256]{2,1,0:T(8,128)(2,1)S(1)}, u32[]{:S(2)}, u32[]{:S(2)}) collective-permute-start(bf16[2,128,256]{2,1,0:T(8,128)(2,1)S(1)} %convert_element_type.419), channel_id=1, source_target_pairs={{0,8},{8,16},{16,24},{1,9},{9,17},{17,25},{2,10},{10,18},{18,26},{... | collective-permute-start | bytes 393224 | tf_op jit(solution)/shard_map/ppermute | solution.py:968
  200.6 12.3 %collective-permute-start.14 = (bf16[2,128,256]{2,1,0:T(8,128)(2,1)S(1)}, bf16[2,128,256]{2,1,0:T(8,128)(2,1)S(1)}, u32[]{:S(2)}, u32[]{:S(2)}) collective-permute-start(bf16[2,128,256]{2,1,0:T(8,128)(2,1)S(1)} %fusion.2), channel_id=1, source_target_pairs={{0,8},{8,16},{16,24},{1,9},{9,17},{17,25},{2,10},{10,18},{18,26},{... | collective-permute-start | bytes 393224 | tf_op jit(solution)/shard_map/ppermute | solution.py:968
  213.2 19.0 %collective-permute-start.15 = (bf16[2,128,256]{2,1,0:T(8,128)(2,1)S(1)}, bf16[2,128,256]{2,1,0:T(8,128)(2,1)S(1)}, u32[]{:S(2)}, u32[]{:S(2)}) collective-permute-start(bf16[2,128,256]{2,1,0:T(8,128)(2,1)S(1)} %fusion.3), channel_id=1, source_target_pairs={{0,8},{8,16},{16,24},{1,9},{9,17},{17,25},{2,10},{10,18},{18,26},{... | collective-permute-start | bytes 393224 | tf_op jit(solution)/shard_map/ppermute | solution.py:968
  250.3 13.9 %collective-permute-start.17 = (bf16[2,512,256]{2,1,0:T(8,128)(2,1)S(1)}, bf16[2,512,256]{2,1,0:T(8,128)(2,1)S(1)}, u32[]{:S(2)}, u32[]{:S(2)}) collective-permute-start(bf16[2,512,256]{2,1,0:T(8,128)(2,1)S(1)} %pad_maximum_fusion.16), channel_id=1, source_target_pairs={{0,2},{1,3},{2,0},{3,1},{4,6},{5,7},{6,4},{7,5},{8,10},{9,11},{10,... | collective-permute-start | bytes 1572872 | tf_op jit(solution)/shard_map/ppermute | solution.py:692
  252.0 13.6 %collective-permute-start.18 = (bf16[2,512,256]{2,1,0:T(8,128)(2,1)S(1)}, bf16[2,512,256]{2,1,0:T(8,128)(2,1)S(1)}, u32[]{:S(2)}, u32[]{:S(2)}) collective-permute-start(bf16[2,512,256]{2,1,0:T(8,128)(2,1)S(1)} %pad_maximum_fusion.17), channel_id=1, source_target_pairs={{0,4},{1,5},{2,6},{3,7},{4,0},{5,1},{6,2},{7,3},{8,12},{9,13},{10,... | collective-permute-start | bytes 1572872 | tf_op jit(solution)/shard_map/ppermute | solution.py:692
  265.8 7.2 %collective-permute-start.19 = (bf16[1,512,256]{2,1,0:T(8,128)(2,1)S(1)}, bf16[1,512,256]{2,1,0:T(8,128)(2,1)S(1)}, u32[]{:S(2)}, u32[]{:S(2)}) collective-permute-start(bf16[1,512,256]{2,1,0:T(8,128)(2,1)S(1)} %get-tuple-element.204), channel_id=1, source_target_pairs={{0,4},{1,5},{2,6},{3,7},{4,0},{5,1},{6,2},{7,3},{8,12},{9,13},{10,... | collective-permute-start | bytes 786440 | tf_op jit(solution)/shard_map/ppermute | solution.py:692
  283.1 10.8 %collective-permute-start.23 = (bf16[2,512,256]{2,1,0:T(8,128)(2,1)S(1)}, bf16[2,512,256]{2,1,0:T(8,128)(2,1)S(1)}, u32[]{:S(2)}, u32[]{:S(2)}) collective-permute-start(bf16[2,512,256]{2,1,0:T(8,128)(2,1)S(1)} %pad_maximum_fusion.18), channel_id=1, source_target_pairs={{0,2},{1,3},{2,0},{3,1},{4,6},{5,7},{6,4},{7,5},{8,10},{9,11},{10,... | collective-permute-start | bytes 1572872 | tf_op jit(solution)/shard_map/ppermute | solution.py:692
  283.6 10.5 %collective-permute-start.24 = (bf16[2,512,256]{2,1,0:T(8,128)(2,1)S(1)}, bf16[2,512,256]{2,1,0:T(8,128)(2,1)S(1)}, u32[]{:S(2)}, u32[]{:S(2)}) collective-permute-start(bf16[2,512,256]{2,1,0:T(8,128)(2,1)S(1)} %pad_maximum_fusion.19), channel_id=1, source_target_pairs={{0,4},{1,5},{2,6},{3,7},{4,0},{5,1},{6,2},{7,3},{8,12},{9,13},{10,... | collective-permute-start | bytes 1572872 | tf_op jit(solution)/shard_map/ppermute | solution.py:692
  367.5 278.7 %reduce-scatter.6.cloned.1.call-start = ((), (), s32[]{:S(2)}) async-start(), calls=%async_computation.7 | async-start | bytes 6144000 | tf_op jit(solution)/shard_map/reduce_scatter | solution.py:1276
  383.8 14.4 %collective-permute-start.28 = (bf16[2,512,256]{2,1,0:T(8,128)(2,1)S(1)}, bf16[2,512,256]{2,1,0:T(8,128)(2,1)S(1)}, u32[]{:S(2)}, u32[]{:S(2)}) collective-permute-start(bf16[2,512,256]{2,1,0:T(8,128)(2,1)S(1)} %pad_maximum_fusion.20), channel_id=1, source_target_pairs={{0,2},{1,3},{2,0},{3,1},{4,6},{5,7},{6,4},{7,5},{8,10},{9,11},{10,... | collective-permute-start | bytes 1572872 | tf_op jit(solution)/shard_map/ppermute | solution.py:692
  385.4 14.1 %collective-permute-start.29 = (bf16[2,512,256]{2,1,0:T(8,128)(2,1)S(1)}, bf16[2,512,256]{2,1,0:T(8,128)(2,1)S(1)}, u32[]{:S(2)}, u32[]{:S(2)}) collective-permute-start(bf16[2,512,256]{2,1,0:T(8,128)(2,1)S(1)} %pad_maximum_fusion.21), channel_id=1, source_target_pairs={{0,4},{1,5},{2,6},{3,7},{4,0},{5,1},{6,2},{7,3},{8,12},{9,13},{10,... | collective-permute-start | bytes 1572872 | tf_op jit(solution)/shard_map/ppermute | solution.py:692
  399.7 7.8 %collective-permute-start.30 = (bf16[1,512,256]{2,1,0:T(8,128)(2,1)S(1)}, bf16[1,512,256]{2,1,0:T(8,128)(2,1)S(1)}, u32[]{:S(2)}, u32[]{:S(2)}) collective-permute-start(bf16[1,512,256]{2,1,0:T(8,128)(2,1)S(1)} %get-tuple-element.231), channel_id=1, source_target_pairs={{0,4},{1,5},{2,6},{3,7},{4,0},{5,1},{6,2},{7,3},{8,12},{9,13},{10,... | collective-permute-start | bytes 786440 | tf_op jit(solution)/shard_map/ppermute | solution.py:692
  401.2 7.4 %collective-permute-start.31 = (bf16[1,512,256]{2,1,0:T(8,128)(2,1)S(1)}, bf16[1,512,256]{2,1,0:T(8,128)(2,1)S(1)}, u32[]{:S(2)}, u32[]{:S(2)}) collective-permute-start(bf16[1,512,256]{2,1,0:T(8,128)(2,1)S(1)} %get-tuple-element.232), channel_id=1, source_target_pairs={{0,2},{1,3},{2,0},{3,1},{4,6},{5,7},{6,4},{7,5},{8,10},{9,11},{10,... | collective-permute-start | bytes 786440 | tf_op jit(solution)/shard_map/ppermute | solution.py:692
  416.1 11.3 %collective-permute-start.34 = (bf16[2,512,256]{2,1,0:T(8,128)(2,1)S(1)}, bf16[2,512,256]{2,1,0:T(8,128)(2,1)S(1)}, u32[]{:S(2)}, u32[]{:S(2)}) collective-permute-start(bf16[2,512,256]{2,1,0:T(8,128)(2,1)S(1)} %pad_maximum_fusion.22), channel_id=1, source_target_pairs={{0,2},{1,3},{2,0},{3,1},{4,6},{5,7},{6,4},{7,5},{8,10},{9,11},{10,... | collective-permute-start | bytes 1572872 | tf_op jit(solution)/shard_map/ppermute | solution.py:692
  416.9 11.0 %collective-permute-start.35 = (bf16[2,512,256]{2,1,0:T(8,128)(2,1)S(1)}, bf16[2,512,256]{2,1,0:T(8,128)(2,1)S(1)}, u32[]{:S(2)}, u32[]{:S(2)}) collective-permute-start(bf16[2,512,256]{2,1,0:T(8,128)(2,1)S(1)} %pad_maximum_fusion.23), channel_id=1, source_target_pairs={{0,4},{1,5},{2,6},{3,7},{4,0},{5,1},{6,2},{7,3},{8,12},{9,13},{10,... | collective-permute-start | bytes 1572872 | tf_op jit(solution)/shard_map/ppermute | solution.py:692
  466.5 213.4 %reduce-scatter.4.cloned.1.call-start = ((), (), s32[]{:S(2)}) async-start(), calls=%async_computation.6 | async-start | bytes 7864320 | tf_op jit(solution)/shard_map/reduce_scatter | solution.py:1292
  466.5 7.5 %collective-permute-start.38 = (bf16[2,128,256]{2,1,0:T(8,128)(2,1)S(1)}, bf16[2,128,256]{2,1,0:T(8,128)(2,1)S(1)}, u32[]{:S(2)}, u32[]{:S(2)}) collective-permute-start(bf16[2,128,256]{2,1,0:T(8,128)(2,1)S(1)} %convert_element_type.466), channel_id=1, source_target_pairs={{8,0},{16,8},{24,16},{9,1},{17,9},{25,17},{10,2},{18,10},{26,18},{... | collective-permute-start | bytes 393224 | tf_op jit(solution)/shard_map/ppermute | solution.py:968
  474.3 13.3 %collective-permute-start.39 = (bf16[2,128,256]{2,1,0:T(8,128)(2,1)S(1)}, bf16[2,128,256]{2,1,0:T(8,128)(2,1)S(1)}, u32[]{:S(2)}, u32[]{:S(2)}) collective-permute-start(bf16[2,128,256]{2,1,0:T(8,128)(2,1)S(1)} %fusion.4), channel_id=1, source_target_pairs={{8,0},{16,8},{24,16},{9,1},{17,9},{25,17},{10,2},{18,10},{26,18},{... | collective-permute-start | bytes 393224 | tf_op jit(solution)/shard_map/ppermute | solution.py:968
  487.8 13.8 %collective-permute-start.40 = (bf16[2,128,256]{2,1,0:T(8,128)(2,1)S(1)}, bf16[2,128,256]{2,1,0:T(8,128)(2,1)S(1)}, u32[]{:S(2)}, u32[]{:S(2)}) collective-permute-start(bf16[2,128,256]{2,1,0:T(8,128)(2,1)S(1)} %fusion.5), channel_id=1, source_target_pairs={{8,0},{16,8},{24,16},{9,1},{17,9},{25,17},{10,2},{18,10},{26,18},{... | collective-permute-start | bytes 393224 | tf_op jit(solution)/shard_map/ppermute | solution.py:968
  522.6 14.7 %collective-permute-start.41 = (f32[8,1536]{1,0:T(8,128)S(1)}, f32[8,1536]{1,0:T(8,128)S(1)}, u32[]{:S(2)}, u32[]{:S(2)}) collective-permute-start(f32[8,1536]{1,0:T(8,128)S(1)} %rim_back.1), channel_id=1, source_target_pairs={{8,0},{16,8},{24,16},{9,1},{17,9},{25,17},{10,2},{18,10},{26,18},{... | collective-permute-start | bytes 147464 | tf_op jit(solution)/shard_map/ppermute | solution.py:968
  557.9 20.1 %collective-permute-start.47 = (bf16[4,1024,256]{2,1,0:T(8,128)(2,1)}, bf16[4,1024,256]{2,1,0:T(8,128)(2,1)}, u32[]{:S(2)}, u32[]{:S(2)}) collective-permute-start(bf16[4,1024,256]{2,1,0:T(8,128)(2,1)} %block_products.15), channel_id=1, source_target_pairs={{0,1},{1,0},{2,3},{3,2},{4,5},{5,4},{6,7},{7,6},{8,9},{9,8},{10,11... | collective-permute-start | bytes 6291464 | tf_op jit(solution)/shard_map/ppermute | solution.py:692
  570.0 12.8 %collective-permute-start.42 = (bf16[4,1024,256]{2,1,0:T(8,128)(2,1)}, bf16[4,1024,256]{2,1,0:T(8,128)(2,1)}, u32[]{:S(2)}, u32[]{:S(2)}) collective-permute-start(bf16[4,1024,256]{2,1,0:T(8,128)(2,1)} %block_products.14), channel_id=1, source_target_pairs={{0,1},{1,0},{2,3},{3,2},{4,5},{5,4},{6,7},{7,6},{8,9},{9,8},{10,11... | collective-permute-start | bytes 6291464 | tf_op jit(solution)/shard_map/ppermute | solution.py:692
  579.9 14.8 %collective-permute-start.48 = (bf16[2,512,256]{2,1,0:T(8,128)(2,1)S(1)}, bf16[2,512,256]{2,1,0:T(8,128)(2,1)S(1)}, u32[]{:S(2)}, u32[]{:S(2)}) collective-permute-start(bf16[2,512,256]{2,1,0:T(8,128)(2,1)S(1)} %pad_maximum_fusion.26), channel_id=1, source_target_pairs={{0,2},{1,3},{2,0},{3,1},{4,6},{5,7},{6,4},{7,5},{8,10},{9,11},{10,... | collective-permute-start | bytes 1572872 | tf_op jit(solution)/shard_map/ppermute | solution.py:692
  581.4 14.8 %collective-permute-start.49 = (bf16[2,512,256]{2,1,0:T(8,128)(2,1)S(1)}, bf16[2,512,256]{2,1,0:T(8,128)(2,1)S(1)}, u32[]{:S(2)}, u32[]{:S(2)}) collective-permute-start(bf16[2,512,256]{2,1,0:T(8,128)(2,1)S(1)} %pad_maximum_fusion.27), channel_id=1, source_target_pairs={{0,4},{1,5},{2,6},{3,7},{4,0},{5,1},{6,2},{7,3},{8,12},{9,13},{10,... | collective-permute-start | bytes 1572872 | tf_op jit(solution)/shard_map/ppermute | solution.py:692
  584.4 21.6 %collective-permute-start.43 = (bf16[2,512,256]{2,1,0:T(8,128)(2,1)S(1)}, bf16[2,512,256]{2,1,0:T(8,128)(2,1)S(1)}, u32[]{:S(2)}, u32[]{:S(2)}) collective-permute-start(bf16[2,512,256]{2,1,0:T(8,128)(2,1)S(1)} %pad_maximum_fusion.24), channel_id=1, source_target_pairs={{0,2},{1,3},{2,0},{3,1},{4,6},{5,7},{6,4},{7,5},{8,10},{9,11},{10,... | collective-permute-start | bytes 1572872 | tf_op jit(solution)/shard_map/ppermute | solution.py:692
  585.2 22.2 %collective-permute-start.44 = (bf16[2,512,256]{2,1,0:T(8,128)(2,1)S(1)}, bf16[2,512,256]{2,1,0:T(8,128)(2,1)S(1)}, u32[]{:S(2)}, u32[]{:S(2)}) collective-permute-start(bf16[2,512,256]{2,1,0:T(8,128)(2,1)S(1)} %pad_maximum_fusion.25), channel_id=1, source_target_pairs={{0,4},{1,5},{2,6},{3,7},{4,0},{5,1},{6,2},{7,3},{8,12},{9,13},{10,... | collective-permute-start | bytes 1572872 | tf_op jit(solution)/shard_map/ppermute | solution.py:692
  597.4 15.6 %collective-permute-start.50 = (bf16[1,512,256]{2,1,0:T(8,128)(2,1)S(1)}, bf16[1,512,256]{2,1,0:T(8,128)(2,1)S(1)}, u32[]{:S(2)}, u32[]{:S(2)}) collective-permute-start(bf16[1,512,256]{2,1,0:T(8,128)(2,1)S(1)} %get-tuple-element.290), channel_id=1, source_target_pairs={{0,4},{1,5},{2,6},{3,7},{4,0},{5,1},{6,2},{7,3},{8,12},{9,13},{10,... | collective-permute-start | bytes 786440 | tf_op jit(solution)/shard_map/ppermute | solution.py:692
  598.9 14.1 %collective-permute-start.51 = (bf16[1,512,256]{2,1,0:T(8,128)(2,1)S(1)}, bf16[1,512,256]{2,1,0:T(8,128)(2,1)S(1)}, u32[]{:S(2)}, u32[]{:S(2)}) collective-permute-start(bf16[1,512,256]{2,1,0:T(8,128)(2,1)S(1)} %get-tuple-element.291), channel_id=1, source_target_pairs={{0,2},{1,3},{2,0},{3,1},{4,6},{5,7},{6,4},{7,5},{8,10},{9,11},{10,... | collective-permute-start | bytes 786440 | tf_op jit(solution)/shard_map/ppermute | solution.py:692
  609.5 9.5 %collective-permute-start.45 = (bf16[1,512,256]{2,1,0:T(8,128)(2,1)}, bf16[1,512,256]{2,1,0:T(8,128)(2,1)S(1)}, u32[]{:S(2)}, u32[]{:S(2)}) collective-permute-start(bf16[1,512,256]{2,1,0:T(8,128)(2,1)} %get-tuple-element.280), channel_id=1, source_target_pairs={{0,4},{1,5},{2,6},{3,7},{4,0},{5,1},{6,2},{7,3},{8,12},{9,13},{10,... | collective-permute-start | bytes 786440 | tf_op jit(solution)/shard_map/ppermute | solution.py:692
  610.9 11.0 %collective-permute-start.46 = (bf16[1,512,256]{2,1,0:T(8,128)(2,1)}, bf16[1,512,256]{2,1,0:T(8,128)(2,1)S(1)}, u32[]{:S(2)}, u32[]{:S(2)}) collective-permute-start(bf16[1,512,256]{2,1,0:T(8,128)(2,1)} %get-tuple-element.281), channel_id=1, source_target_pairs={{0,2},{1,3},{2,0},{3,1},{4,6},{5,7},{6,4},{7,5},{8,10},{9,11},{10,... | collective-permute-start | bytes 786440 | tf_op jit(solution)/shard_map/ppermute | solution.py:692
  615.9 13.7 %collective-permute-start.55 = (f32[112,128]{1,0:T(8,128)S(1)}, f32[112,128]{1,0:T(8,128)}, u32[]{:S(2)}, u32[]{:S(2)}) collective-permute-start(f32[112,128]{1,0:T(8,128)S(1)} %pad_bitcast_fusion), channel_id=1, source_target_pairs={{0,8},{8,16},{16,24},{24,0},{1,9},{9,17},{17,25},{25,1},{2,10},{10... | collective-permute-start | bytes 172040 | tf_op jit(solution)/shard_map/ppermute | solution.py:961
  618.4 11.2 %collective-permute-start.56 = (f32[112,128]{1,0:T(8,128)S(1)}, f32[112,128]{1,0:T(8,128)}, u32[]{:S(2)}, u32[]{:S(2)}) collective-permute-start(f32[112,128]{1,0:T(8,128)S(1)} %pad_bitcast_fusion), channel_id=1, source_target_pairs={{0,16},{8,24},{16,0},{24,8},{1,17},{9,25},{17,1},{25,9},{2,18},{10... | collective-permute-start | bytes 172040 | tf_op jit(solution)/shard_map/ppermute | solution.py:961
  619.0 10.6 %collective-permute-start.57 = (f32[112,128]{1,0:T(8,128)S(1)}, f32[112,128]{1,0:T(8,128)}, u32[]{:S(2)}, u32[]{:S(2)}) collective-permute-start(f32[112,128]{1,0:T(8,128)S(1)} %pad_bitcast_fusion), channel_id=1, source_target_pairs={{0,24},{8,0},{16,8},{24,16},{1,25},{9,1},{17,9},{25,17},{2,26},{10... | collective-permute-start | bytes 172040 | tf_op jit(solution)/shard_map/ppermute | solution.py:961
  (105 other events, 1345.5 us)
Sparse Core Ops, SparseCore 0:
  10.4 121.2 all-gather.3
  133.8 96.4 all-gather.5
  231.9 108.7 all-gather.7
  367.6 98.4 reduce-scatter.7
  468.3 95.6 reduce-scatter.5
  566.2 113.6 reduce-scatter.3

commit v3 on v2

--- a/solution.py
+++ b/solution.py
@@ -260,7 +260,7 @@
 def output_kernel(
     heads, group, start_ref, s0_ref, tc_ref, p_ref, w_ref, ut_ref, o0_ref, gain_ref, *refs
 ):
-    g_refs, (mixed_ref, o_ref, s_ref, u_ref) = refs[:heads], refs[heads:]
+    g_ref, mixed_ref, o_ref, s_ref, u_ref = refs
     for c in range(group):
         for h in range(heads):
             at = slice(c * CHUNK, (c + 1) * CHUNK)
@@ -271,17 +271,10 @@
             u_ref[h, c] = (ut_ref[h, c].astype(F32) - dx(w_ref[h, c], low))
             out = o0_ref[at, cols] + dx(p_ref[h, c], low)
             o_ref[at, cols] = out
-            gate = g_refs[h][at, :]
+            gate = g_ref[at, cols]
             inv = lax.rsqrt(jnp.mean(out * out, axis=-1, keepdims=True) + 1e-05)
             mixed = out * inv * gain_ref[h : h + 1, :] * (gate * jax.nn.sigmoid(gate))
             mixed_ref[at, cols] = mixed.astype(BF16)
-
-
-def gate_specs(heads, rows, place):
-    return [
-        spec((rows, DV), functools.partial(lambda h, g: (place(g), 3 * h + 2), h))
-        for h in range(heads)
-    ]
 
 
 def delta_output(start, states, trans, reach, wkeys, pseudo, local_out, raw, gain):
@@ -306,7 +299,7 @@
             flat,
             spec((heads, DV), lambda g: (0, 0)),
         ]
-        + gate_specs(heads, rows, lambda g: g),
+        + [flat],
         out_specs=[flat, flat, tall, tall],
         out_shape=[
             jax.ShapeDtypeStruct((tokens, heads * DV), BF16),
@@ -317,14 +310,13 @@
         compiler_params=params(),
         cost_estimate=cost(heads * count * 10 * 2 * CHUNK**3 * 8, heads * count * CHUNK * 6000),
         name="delta_output",
-    )(start, states, trans, reach, wkeys, pseudo, local_out, gain, *([raw] * heads))
+    )(start, states, trans, reach, wkeys, pseudo, local_out, gain, raw)
 
 
 def tail_kernel(
     heads, group, dm_ref, o_ref, gain_ref, pt_ref, mt_ref, *refs
 ):
-    g_refs = refs[:heads]
-    do_ref, dg_ref, dgain_ref, ds_ref, dstart_ref, state = refs[heads:]
+    g_ref, do_ref, dg_ref, dgain_ref, ds_ref, dstart_ref, state = refs
 
     @pl.when(pl.program_id(0) == 0)
     def _():
@@ -337,7 +329,7 @@
             at = slice(c * CHUNK, (c + 1) * CHUNK)
             cols = slice(h * DV, (h + 1) * DV)
             out = o_ref[at, cols]
-            gate = g_refs[h][at, :]
+            gate = g_ref[at, cols]
             back = dm_ref[at, cols]
             gain = gain_ref[h : h + 1, :]
             sig = jax.nn.sigmoid(gate)
@@ -375,7 +367,7 @@
         functools.partial(tail_kernel, heads, group),
         grid=(count // group,),
         in_specs=[flat, flat, spec((heads, DV), lambda g: (0, 0)), square, square]
-        + gate_specs(heads, rows, lambda g: last - g),
+        + [flat],
         out_specs=[
             flat,
             flat,
@@ -394,7 +386,7 @@
         compiler_params=params(),
         cost_estimate=cost(heads * count * 10 * 2 * CHUNK**3 * 8, heads * count * CHUNK * 6000),
         name="delta_tail",
-    )(grad_mixed, outs, gain, reach_turned, steps_turned, *([raw] * heads))
+    )(grad_mixed, outs, gain, reach_turned, steps_turned, raw)
 
 
 def early_kernel(heads, group, at_ref, u_ref, s_ref, do_ref, da_ref, dqd_ref, dua_ref):
@@ -550,10 +542,6 @@
         y_ref[...] = act
 
 
-def raw_block(c):
-    return (c >> 2) * 6 + (c & 3)
-
-
 def front(raw, rim, masks, taps):
     tokens, cols = raw.shape[0], taps.shape[1]
     block = spec((tokens, DK), lambda c: (0, c))
@@ -561,8 +549,8 @@
         front_kernel,
         grid=(cols // DK,),
         in_specs=[
-            spec((tokens, DK), lambda c: (0, raw_block(c))),
-            spec((16, DK), lambda c: (0, raw_block(c))),
+            spec((tokens, DK), lambda c: (0, c)),
+            spec((16, DK), lambda c: (0, c)),
             spec((tokens, 8), lambda c: (0, 0)),
             spec((4, DK), lambda c: (0, c)),
         ],
@@ -622,7 +610,6 @@
 
 
 def rim_back_kernel(heads, conv_ref, mask_ref, taps_ref, dy_ref, drim_ref):
-    drim_ref[...] = jnp.zeros_like(drim_ref)
     zeros = jnp.zeros((8, DK), F32)
     for h in range(heads):
         for kind in range(4):
@@ -633,11 +620,12 @@
             for lag in range(1, 4):
                 part = jnp.concatenate([zeros, dconv * mask_ref[:, 3 + lag : 4 + lag]], axis=0)
                 total = total + taps[lag : lag + 1] * pltpu.roll(part, 16 - lag, 0)[:8]
-            drim_ref[:, (6 * h + kind) * DK : (6 * h + kind + 1) * DK] = total
-
-
-def rim_back(conv, masks, taps, dqkv, cols):
-    heads = taps.shape[1] // (4 * DK)
+            drim_ref[:, at] = total
+
+
+def rim_back(conv, masks, taps, dqkv):
+    cols = taps.shape[1]
+    heads = cols // (4 * DK)
     return pl.pallas_call(
         functools.partial(rim_back_kernel, heads),
         out_shape=jax.ShapeDtypeStruct((8, cols), F32),
@@ -656,15 +644,15 @@
 
 
 def front_back(raw, rim, conv, masks, taps, dqkv, dg):
-    tokens, cols = raw.shape
+    tokens, cols = raw.shape[0], raw.shape[1] + dg.shape[1]
     block = spec((tokens, DK), lambda c: (0, c))
     act_spec = spec((tokens, DK), lambda c: (0, act_block(c)))
     return pl.pallas_call(
         front_back_kernel,
         grid=(cols // DK,),
         in_specs=[
-            block,
-            spec((16, DK), lambda c: (0, c)),
+            act_spec,
+            spec((16, DK), lambda c: (0, act_block(c))),
             act_spec,
             spec((tokens, 8), lambda c: (0, 0)),
             spec((4, DK), lambda c: (0, act_block(c))),
@@ -872,43 +860,42 @@
     )
 
 
-def block_kernel(turns, mp_ref, *refs):
-    out_ref = refs[2 * len(turns)]
+def block_kernel(terms, mp_ref, *refs):
+    out_ref = refs[2 * terms]
     total = None
-    for i, turned in enumerate(turns):
-        part = d1(refs[2 * i][...], refs[2 * i + 1][...], NN if turned is False else NT)
+    for i in range(terms):
+        part = d1(refs[2 * i][...], refs[2 * i + 1][...], NT)
         total = part if total is None else total + part
     out_ref[0] = total.astype(out_ref.dtype)
 
 
-def right_index(parity, turned, g, m):
-    at = (2 * g + parity) ^ m[0]
-    return (at, 0) if turned else (0, at)
-
-
-def spaced_index(parity, cols, rows, g, m):
+def left_index(start, g, m):
+    return (0, start)
+
+
+def right_index(parity, cols, rows, start, g, m):
     at = ((2 * g + parity) ^ m[0]) * cols
-    return (pl.multiple_of(at + lax.div(at, rows) * 16, 16), 0)
+    if rows:
+        at = at + lax.div(at, rows) * 16
+    return (pl.multiple_of(at, 16), start)
 
 
 def block_products(terms, mp_pos, cols, parity):
     tokens = terms[0][0].shape[0]
     count = lax.axis_size("mp") // 2
     in_specs, args, flops = [], [], 0
-    for left, right, turned in terms:
-        depth = left.shape[1]
-        in_specs.append(spec((tokens, depth), lambda g, m: (0, 0)))
-        if turned is None:
-            rows = right.shape[0] // lax.axis_size("seq") - 16
-            index = functools.partial(spaced_index, parity, cols, rows)
-            in_specs.append(pl.BlockSpec((pl.Element(cols), pl.Element(depth)), index))
-        else:
-            index = functools.partial(right_index, parity, turned)
-            in_specs.append(spec((cols, depth) if turned else (depth, cols), index))
+    for left, left_start, right, right_start, depth, rows in terms:
+        in_specs.append(
+            pl.BlockSpec(
+                (pl.Element(tokens), pl.Element(depth)), functools.partial(left_index, left_start)
+            )
+        )
+        index = functools.partial(right_index, parity, cols, rows, right_start)
+        in_specs.append(pl.BlockSpec((pl.Element(cols), pl.Element(depth)), index))
         args += [left, right]
         flops += 2 * tokens * depth * cols * count
     return pl.pallas_call(
-        functools.partial(block_kernel, [t[2] for t in terms]),
+        functools.partial(block_kernel, len(terms)),
         grid_spec=pltpu.PrefetchScalarGridSpec(
             num_scalar_prefetch=1,
             grid=(count,),
@@ -1102,9 +1089,9 @@
     )
 
 
-def ffn_kernel(units, x_ref, dy_ref, gu_ref, down_ref, hid_ref, dgu_ref):
+def ffn_kernel(units, x_ref, back_ref, gu_ref, hid_ref, dgu_ref):
     gate, up = unpack(d1(x_ref[...], gu_ref[...]), units)
-    back = d1(dy_ref[...], down_ref[...], NT)
+    back = back_ref[...]
     sig = jax.nn.sigmoid(gate)
     silu = gate * sig
     hid_ref[...] = (silu * up).astype(BF16)
@@ -1113,9 +1100,9 @@
     ).astype(BF16)
 
 
-def ffn(normed2, full_grad, gu_full, down_full):
+def ffn(normed2, grad_hidden, gu_full):
     tokens, width = normed2.shape
-    units = down_full.shape[0]
+    units = grad_hidden.shape[1]
     tile = 256
     row_spec = spec((tile, width), lambda i: (i, 0))
     return pl.pallas_call(
@@ -1123,9 +1110,8 @@
         grid=(tokens // tile,),
         in_specs=[
             row_spec,
-            row_spec,
+            spec((tile, units), lambda i: (i, 0)),
             spec((width, 2 * units), lambda i: (0, 0)),
-            spec((units, width), lambda i: (0, 0)),
         ],
         out_specs=[
             spec((tile, units), lambda i: (i, 0)),
@@ -1138,37 +1124,15 @@
         compiler_params=params(),
         cost_estimate=cost(6 * tokens * width * units, tokens * width * 4 + width * units * 6),
         name="ffn",
-    )(normed2, full_grad, gu_full, down_full)
+    )(normed2, grad_hidden, gu_full)
 
 
 def after(value, *earlier):
     return lax.optimization_barrier((value, earlier))[0]
 
 
-def ring_gather(value):
-    pairs = [(shifted(value, 1), shifted(value, -1))]
-    for _ in range(2, lax.axis_size("seq")):
-        pairs.append((shifted(pairs[-1][0], 1), shifted(pairs[-1][1], -1)))
-    return pairs
-
-
 def together(*values):
     return lax.optimization_barrier(values)
-
-
-def join_ring(own, pairs, axis):
-    seq_count = lax.axis_size("seq")
-    seq_pos = lax.axis_index("seq")
-    size = own.shape[axis]
-    shape = list(own.shape)
-    shape[axis] = size * seq_count
-    full = jnp.zeros(tuple(shape), own.dtype)
-    full = lax.dynamic_update_slice_in_dim(full, own, seq_pos * size, axis)
-    for j in range(1, seq_count):
-        piece = jnp.where(seq_pos >= j, pairs[j - 1][0], pairs[seq_count - j - 1][1])
-        at = lax.rem(seq_pos - j + seq_count, seq_count) * size
-        full = lax.dynamic_update_slice_in_dim(full, piece, at, axis)
-    return full
 
 
 def chain(steps, ends, sign):
@@ -1217,27 +1181,32 @@
     masks = jnp.stack([zero] * 2 + [ids_f, prior_f] + same + [zero], axis=1)
 
     units = w_gate.shape[1]
-    mix_cols = heads * (2 * DK + 2 * DV)
+    feats = w_out.shape[0]
+    act_cols, gate_cols = heads * 2 * DV, heads * DV
     gate_part = jnp.pad(
-        w_gates.reshape(rows, 2 * heads).T, ((0, 16 - 2 * heads), (0, mix_cols - rows))
-    )
-    mixer_part = jnp.concatenate([w_mixer.reshape(rows, mix_cols), gate_part])
-    do_part = jnp.concatenate([w_out, w_down])
+        w_gates.reshape(rows, 2 * heads).T, ((0, 16 - 2 * heads), (0, act_cols - rows))
+    )
+    act_part = w_mixer[:, :, : 2 * DV].reshape(rows, act_cols)
+    act_full = lax.all_gather(
+        jnp.concatenate([act_part, gate_part]), "seq", axis=0, tiled=True
+    )
+    found_res = gather_mp(residual)
+    god_part = jnp.concatenate(
+        [w_mixer[:, :, 2 * DV :].reshape(rows, gate_cols), w_out.T, w_down.T], axis=1
+    )
+    god_full = lax.all_gather(after(god_part, found_res[0][0]), "seq", axis=0, tiled=True)
     gu_part = pack(w_gate, w_up)
-    mixer_full = lax.all_gather(mixer_part, "seq", axis=0, tiled=True)
-    found_res = gather_mp(residual)
-    do_full = lax.all_gather(after(do_part, found_res[0][0]), "seq", axis=1, tiled=True)
 
     normed, inv1 = assemble(found_res, mp_pos, attn_gain)
-    gu_full = lax.all_gather(after(gu_part, normed), "seq", axis=0, tiled=True)
+    rim_normed = shifted(normed[tokens - 16 :], 1)
     found_og = gather_mp(after(out_grad, normed))
     full_grad = assemble(found_og, mp_pos)[0]
-    mixer_full = after(mixer_full, full_grad)
-    rim_normed = shifted(normed[tokens - 16 :], 1)
+    act_full = after(act_full, full_grad)
     raw, gate_pre, gates, rim = project_first(
-        normed, rim_normed, mixer_full, masks, decay_scale, dt_bias
-    )
-    taps = conv_taps.reshape(4, heads * 2 * DV)
+        normed, rim_normed, act_full, masks, decay_scale, dt_bias
+    )
+    gu_full = lax.all_gather(after(gu_part, raw), "seq", axis=0, tiled=True)
+    taps = conv_taps.reshape(4, act_cols)
     qkv, conv = front(raw, rim, masks, taps)
 
     inverse, inv_turned, scores, scores_turned, kept, wkeys, reach, reach_turned, steps, steps_turned = (
@@ -1246,19 +1215,32 @@
     trans, back = delta_trans(steps, steps_turned)
     pseudo, local_out, states, state_end = delta_values(qkv, gates, inverse, scores, steps)
     start = chain(trans[:, -1], state_end, 1)
+    god_full = after(god_full, state_end)
+    raw_gate = dot(normed, god_full[:, :gate_cols])
+    out_turned = god_full[:, gate_cols : gate_cols + feats]
+    down_turned = god_full[:, gate_cols + feats :]
+    gates_full = jnp.swapaxes(
+        act_full.reshape(seq_count, rows + 16, act_cols)[:, rows:, :rows], 0, 1
+    ).reshape(16, width).T
     mixed, outs, held, corrected = delta_output(
-        start, states, trans, reach, wkeys, pseudo, local_out, raw, head_gain
-    )
-
-    out_full, down_full = do_full[: w_out.shape[0]], do_full[w_out.shape[0] :]
-    branch, _ = reduce_mp([(mixed, out_full, False)], mp_pos, cols)
+        start, states, trans, reach, wkeys, pseudo, local_out, raw_gate, head_gain
+    )
+
+    mixed, out_turned, down_turned, gates_full = together(
+        mixed, out_turned, down_turned, gates_full
+    )
+    branch, _ = reduce_mp([(mixed, 0, god_full, gate_cols, feats, 0)], mp_pos, cols)
     middle = residual.astype(F32) + branch
     found_mid = gather_mp(middle.astype(BF16))
     normed2, _ = assemble(found_mid, mp_pos, ffn_gain)
-    hidden, grad_gu = ffn(normed2, full_grad, gu_full, down_full)
+    grad_hidden = dot(full_grad, after(down_turned, branch))
+    gu_full = after(gu_full, grad_hidden, normed2)
+    hidden, grad_gu = ffn(normed2, grad_hidden, gu_full)
     part_gu = dot(normed2, grad_gu, TN).astype(BF16)
     grad_gu = after(grad_gu, part_gu)
-    grad_normed2, kept_gn2 = reduce_mp([(grad_gu, gu_full, True)], mp_pos, cols)
+    grad_normed2, kept_gn2 = reduce_mp(
+        [(grad_gu, 0, gu_full, 0, 2 * units, 0)], mp_pos, cols
+    )
     dw_gu = lax.psum_scatter(part_gu, "seq", scatter_dimension=0, tiled=True)
     part_down = dot(after(hidden, kept_gn2), full_grad, TN).astype(BF16)
     found_gn2 = gather_mp(grad_normed2.astype(BF16))
@@ -1266,10 +1248,10 @@
     grad_branch, grad_middle, dffn_gain = norm_back(
         found_gn2, found_mid, full_grad, ffn_gain, grad_normed2, middle, mp_pos
     )
-    grad_mixed = dot(grad_branch, out_full, NT)
+    grad_mixed = dot(grad_branch, out_turned)
 
     dout, dg_raw, dhead_gain, dstates, dstart = delta_tail(
-        grad_mixed, outs, raw, head_gain, reach_turned, steps_turned
+        grad_mixed, outs, raw_gate, head_gain, reach_turned, steps_turned
     )
     part_out = dot(mixed, after(grad_branch, dstart), TN).astype(BF16)
     part_do = jnp.concatenate([part_out, part_down])
@@ -1281,9 +1263,10 @@
         grad_end, qkv, gates, inv_turned, scores, kept, corrected, held, dstates, back[:, 1:],
         early,
     )
-    drim = rim_back(conv, masks, taps, dqkv, mix_cols)
+    drim = rim_back(conv, masks, taps, dqkv)
     came = shifted(drim, -1)
     dproj, edge, dtaps = front_back(raw, rim, conv, masks, taps, after(dqkv, drim), dg_raw)
+    came = jnp.pad(came.reshape(8, heads, 2 * DV), ((0, 0), (0, 0), (0, DV))).reshape(8, -1)
     edge = jnp.concatenate([edge[:8], edge[8:] + came])
     dproj = lax.dynamic_update_slice_in_dim(dproj, edge.astype(BF16), tokens - 16, 0)
     dgate_low, gate_sums = gates_back(gate_pre, dgates, decay_scale, dt_bias)
@@ -1292,13 +1275,14 @@
     dw_mixer = lax.psum_scatter(part_mixer, "seq", scatter_dimension=0, tiled=True)
     dproj, dgate_low = after((dproj, dgate_low), part_mixer)
     part_gates = dot(dgate_low, normed, TN)
-    gates_full = jnp.swapaxes(
-        mixer_full.reshape(seq_count, rows + 16, mix_cols)[:, rows:, :rows], 0, 1
-    ).reshape(16, width)
-    grad_normed, kept_gn = reduce_mp(
-        [(dproj, mixer_full, None), (dgate_low, gates_full, False)], mp_pos, cols
-    )
-    ffn_part, _ = reduce_mp([(after(hidden, kept_gn), down_full, False)], mp_pos, cols)
+    terms = [(dgate_low, 0, gates_full, 0, 16, 0)]
+    for h in range(heads):
+        terms.append((dproj, 3 * h * DV, act_full, 2 * h * DV, 2 * DV, rows))
+        terms.append((dproj, (3 * h + 2) * DV, god_full, h * DV, DV, 0))
+    grad_normed, kept_gn = reduce_mp(terms, mp_pos, cols)
+    ffn_part, _ = reduce_mp(
+        [(after(hidden, kept_gn), 0, down_turned, 0, units, 0)], mp_pos, cols
+    )
     output = (middle + ffn_part).astype(BF16)
     own_gain = lax.dynamic_slice_in_dim(attn_gain, mp_pos * cols, cols)
     own_res = residual.astype(F32)

time: 698 us -> 694 us (level)
  waiting for transfers between devices: 287 us -> 271 us
  local copies, waits for them, and re-layouts: 49.4 us -> 59.4 us
    all_gather x3, waiting for transfers between devices: 91.2 us -> 80.3 us  [the longest x1 43.7 us: shards(): lax.all_gather(after(god_part, found_res[0][0]), 'seq', axis=0, tiled=True)]
    reduce_scatter x1, waiting for transfers between devices: 29.1 us -> 38.8 us  [shards(): lax.psum_scatter(part_mixer, 'seq', scatter_dimension=0, tiled=True)]
    ppermute x8, waiting for transfers between devices: 30.4 us -> 21.1 us  [shifted(): lax.ppermute(value, 'seq', [(i, i + steps) for i in range(first, last)])]
    dot_general x6 -> x8, matrix products: 35 us -> 41 us  [dot(): return lax.dot_general(left, right, dims, preferred_element_type=F32)]
    unnamed x178 -> x169, local copies, waits for them, and re-layouts: 26.2 us -> 29.7 us
  transfers between devices with their start and end apart: 67 -> 67, of which waited for: 47 -> 44; matrix products, arithmetic and copies ran while one was open for 12% -> 15% of each run, Pallas kernels for 26% -> 26%
where the time goes in v3:
time: 694 us; the launch traced here: 688 us
  waiting for transfers between devices  271 us (39%)
  Pallas kernels  187 us (27%)
  starting transfers between devices  75.3 us (11%)
  local copies, waits for them, and re-layouts  59.4 us (9%)
  matrix products  42 us (6%)
  other arithmetic  37.6 us (5%)
  between operations  15.7 us (2%)
    ppermute x50, waiting for transfers between devices, flip(): return lax.ppermute(value, 'mp', [(i, i ^ 1 << bit) for i in range(count)])  130 us
    all_gather x1, waiting for transfers between devices, shards(): lax.all_gather(after(god_part, found_res[0][0]), 'seq', axis=0, tiled=True)  43.7 us
    ppermute x50, starting transfers between devices, flip(): return lax.ppermute(value, 'mp', [(i, i ^ 1 << bit) for i in range(count)])  42.9 us
    pallas_call x8, Pallas kernels, block_products(): pl.pallas_call(functools.partial(block_kernel, len(terms)), grid_spec=plt...  42.3 us
    dot_general x8, matrix products, dot(): return lax.dot_general(left, right, dims, preferred_element_type=F32)  41 us
    reduce_scatter x1, waiting for transfers between devices, shards(): lax.psum_scatter(part_mixer, 'seq', scatter_dimension=0, tiled=True)  38.8 us
    unnamed x169, local copies, waits for them, and re-layouts  29.7 us
    ppermute x8, starting transfers between devices, shifted(): lax.ppermute(value, 'seq', [(i, i + steps) for i in range(first, last)])  24.5 us
  transfers between devices with their start and end apart: 67, of which 44 were waited for; matrix products, arithmetic and copies ran while one was open for 15% of the time, Pallas kernels for 26%

profile of v3, /device:TPU:0, one launch (start us, length us, event | category | flops | bytes accessed | tf_op | source)
XLA Modules:
  0.0 687.6 jit_solution(9664692666981221297)
XLA Ops:
  14.4 4.8 collective-permute-done
  28.4 6.7 collective-permute-done.2
  42.2 5.6 assemble.3
  49.1 7.1 %collective-permute-done.7 = bf16[1,512,256]{2,1,0:T(8,128)(2,1)S(1)} collective-permute-done((bf16[1,512,256]{2,1,0:T(8,128)(2,1)S(1)}, bf16[1,512,256]{2,1,0:T(8,128)(2,1)S(1)}, u32[]{:S(2)}, u32[]{:S(2)}) %collective-permute-start.7) | collective-permute-done | bytes 262176 | tf_op jit(solution)/shard_map/ppermute | solution.py:680
  58.7 11.0 %collective-permute-done.10 = bf16[2,512,256]{2,1,0:T(8,128)(2,1)S(1)} collective-permute-done((bf16[2,512,256]{2,1,0:T(8,128)(2,1)S(1)}, bf16[2,512,256]{2,1,0:T(8,128)(2,1)S(1)}, u32[]{:S(2)}, u32[]{:S(2)}) %collective-permute-start.10) | collective-permute-done | bytes 524320 | tf_op jit(solution)/shard_map/ppermute | solution.py:680
  76.9 4.7 assemble.4.refs_9_
  81.6 14.2 %all-gather.4.cloned.1.call-done.w_ref.refs_3_.refs_7_ = bf16[2112,1024]{1,0:T(8,128)(2,1)} async-done(((bf16[528,1024]{1,0:T(8,128)(2,1)}), bf16[2112,1024]{1,0:T(8,128)(2,1)}) %all-gather.4.cloned.1.call-update) | async-done | bytes 4325392 | tf_op jit(solution)/shard_map/all_gather | solution.py:1190
  95.8 11.0 %project_first.1 = (f32[1024,1024]{1,0:T(8,128)}, f32[1024,16]{1,0:T(8,128)S(1)}, f32[2,1024,8]{2,1,0:T(8,128)S(1)}, f32[16,1024]{1,0:T(8,128)S(1)}) custom-call(bf16[1024,2048]{1,0:T(8,128)(2,1)} %get-tuple-element.175.x_ref, bf16[16,2048]{1,0:T(8,128)(2,1)S(1)} %collective-permute-done.6.rim_ref, ...), custom_call_target="tpu_custom_call" | custom-call | flops 42949672 | bytes 83886 | tf_op jit(solution)/shard_map/project_first/pallas_call | solution.py:1010
  108.6 9.6 %front.1 = (f32[1024,1024]{1,0:T(8,128)S(1)}, f32[1024,1024]{1,0:T(8,128)}) custom-call(f32[1024,1024]{1,0:T(8,128)} %get-tuple-element.190.x_ref, f32[16,1024]{1,0:T(8,128)S(1)} %get-tuple-element.191.rim_ref, f32[1024,8]{1,0:T(8,128)S(1)} %copy.65.mask_ref, f32[4,1024]{1,0:T(4,128)S(1)} %bitcast.118), custom_call_target="tpu_custom_call" | custom-call | flops 419430 | bytes 83886 | tf_op jit(solution)/shard_map/front/pallas_call | solution.py:548
  120.1 17.6 %delta_prep.1 = (f32[2,8,128,128]{3,2,1,0:T(8,128)S(1)}, f32[2,8,128,128]{3,2,1,0:T(8,128)S(1)}, f32[2,8,128,128]{3,2,1,0:T(8,128)S(1)}, f32[2,8,128,128]{3,2,1,...) custom-call(f32[1024,1024]{1,0:T(8,128)} %copy-done, ...), custom_call_target="tpu_custom_call" | custom-call | flops 214748368 | bytes 62914 | tf_op jit(solution)/shard_map/delta_prep/pallas_call | solution.py:149
  140.8 10.9 %delta_values.1 = (f32[2,8,128,256]{3,2,1,0:T(8,128)}, f32[1024,512]{1,0:T(8,128)}, f32[2,8,128,256]{3,2,1,0:T(8,128)}, f32[2,128,256]{2,1,0:T(8,128)S(1)}) custom-call(f32[1024,1024]{1,0:T(8,128)} %copy-done, f32[2,1024,8]{2,1,0:T(8,128)S(1)} %copy-done.4, f32[2,8,128,128]{3,2,1,0:T(8,128)S(1)} %get-tuple-element.197.t_ref, ...), custom_call_target="tpu_custom_call" | custom-call | flops 64424508 | bytes 81920 | tf_op jit(solution)/shard_map/delta_values/pallas_call | solution.py:231
  169.7 5.8 collective-permute-done.14
  175.8 8.8 %collective-permute-start.15 = (bf16[2,128,256]{2,1,0:T(8,128)(2,1)S(1)}, bf16[2,128,256]{2,1,0:T(8,128)(2,1)S(1)}, u32[]{:S(2)}, u32[]{:S(2)}) collective-permute-start(bf16[2,128,256]{2,1,0:T(8,128)(2,1)S(1)} %fusion.4), channel_id=1, source_target_pairs={{0,8},{8,16},{16,24},{1,9},{9,17},{17,25},{2,10},{10,18},{18,26},{... | collective-permute-start | bytes 393224 | tf_op jit(solution)/shard_map/ppermute | solution.py:955
  190.2 43.7 %all-gather.6.cloned.1.call-done.refs_1_.refs_5_.refs_9_ = bf16[2048,1712]{1,0:T(8,128)(2,1)} async-done(((bf16[512,1712]{1,0:T(8,128)(2,1)}), bf16[2048,1712]{1,0:T(8,128)(2,1)}) %all-gather.6.cloned.1.call-update) | async-done | bytes 7012368 | tf_op jit(solution)/shard_map/all_gather | solution.py:1197
  239.0 6.0 fusion.1.refs_0_
  245.0 9.9 %delta_output.1 = (bf16[1024,512]{1,0:T(8,128)(2,1)S(1)}, f32[1024,512]{1,0:T(8,128)}, f32[2,8,128,256]{3,2,1,0:T(8,128)}, f32[2,8,128,256]{3,2,1,0:T(8,128)}) custom-call(f32[2,128,256]{2,1,0:T(8,128)S(1)} %convert_element_type.424.start_ref, f32[2,8,128,256]{3,2,1,0:T(8,128)} %get-tuple-element.200.s0_ref, f32[2,9,128,128]{3,2,1,0:T(8,128)S(1)} %copy-done.28, ...), custom_call_target="tpu_custom_call" | custom-call | flops 53687092 | bytes 122880 | tf_op jit(solution)/shard_map/delta_output/pallas_call | solution.py:289
  266.3 10.8 %collective-permute-done.17 = bf16[2,512,256]{2,1,0:T(8,128)(2,1)S(1)} collective-permute-done((bf16[2,512,256]{2,1,0:T(8,128)(2,1)S(1)}, bf16[2,512,256]{2,1,0:T(8,128)(2,1)S(1)}, u32[]{:S(2)}, u32[]{:S(2)}) %collective-permute-start.17) | collective-permute-done | bytes 524320 | tf_op jit(solution)/shard_map/ppermute | solution.py:680
  280.8 5.3 collective-permute-done.19
  289.8 5.2 collective-permute-done.21
  298.0 8.8 %collective-permute-done.23 = bf16[2,512,256]{2,1,0:T(8,128)(2,1)S(1)} collective-permute-done((bf16[2,512,256]{2,1,0:T(8,128)(2,1)S(1)}, bf16[2,512,256]{2,1,0:T(8,128)(2,1)S(1)}, u32[]{:S(2)}, u32[]{:S(2)}) %collective-permute-start.23) | collective-permute-done | bytes 524320 | tf_op jit(solution)/shard_map/ppermute | solution.py:680
  308.0 4.7 fusion.93
  316.2 5.7 assemble.5
  321.9 22.5 %all-gather.8.cloned.1.call-done.gu_ref.refs_1_ = bf16[2048,1376]{1,0:T(8,128)(2,1)} async-done(((bf16[512,1376]{1,0:T(8,128)(2,1)}), bf16[2048,1376]{1,0:T(8,128)(2,1)}) %all-gather.8.cloned.1.call-update) | async-done | bytes 5636112 | tf_op jit(solution)/shard_map/all_gather | solution.py:1208
  344.4 11.3 %ffn.1 = (bf16[1024,688]{1,0:T(8,128)(2,1)S(1)}, bf16[1024,1376]{1,0:T(8,128)(2,1)S(1)}) custom-call(bf16[1024,2048]{1,0:T(8,128)(2,1)} %get-tuple-element.229.x_ref, f32[1024,688]{1,0:T(8,128)} %copy.74.back_ref, bf16[2048,1376]{1,0:T(8,128)(2,1)} %all-gather.8.cloned.1.call-done.gu_ref.refs_1_), custom_call_target="tpu_custom_call" | custom-call | flops 86570432 | bytes 168427 | tf_op jit(solution)/shard_map/ffn/pallas_call | solution.py:1108
  356.9 8.1 %convolution_convert_fusion.1 = bf16[2048,1376]{0,1:T(8,128)(2,1)} fusion(bf16[1024,2048]{1,0:T(8,128)(2,1)S(1)} %copy-done.69, bf16[1024,1376]{1,0:T(8,128)(2,1)S(1)} %get-tuple-element.238.refs_0_), kind=kOutput, calls=%fused_computation.1 | convolution fusion | flops 5774180352 | bytes 12648448 | tf_op jit(solution)/shard_map/dot_general | solution.py:963
  365.1 5.4 block_products.11
  370.5 6.7 block_products.10
  382.5 11.2 %collective-permute-done.28 = bf16[2,512,256]{2,1,0:T(8,128)(2,1)S(1)} collective-permute-done((bf16[2,512,256]{2,1,0:T(8,128)(2,1)S(1)}, bf16[2,512,256]{2,1,0:T(8,128)(2,1)S(1)}, u32[]{:S(2)}, u32[]{:S(2)}) %collective-permute-start.28) | collective-permute-done | bytes 524320 | tf_op jit(solution)/shard_map/ppermute | solution.py:680
  397.2 5.5 collective-permute-done.30
  405.6 5.2 collective-permute-done.32
  413.6 9.0 %collective-permute-done.34 = bf16[2,512,256]{2,1,0:T(8,128)(2,1)S(1)} collective-permute-done((bf16[2,512,256]{2,1,0:T(8,128)(2,1)S(1)}, bf16[2,512,256]{2,1,0:T(8,128)(2,1)S(1)}, u32[]{:S(2)}, u32[]{:S(2)}) %collective-permute-start.34) | collective-permute-done | bytes 524320 | tf_op jit(solution)/shard_map/ppermute | solution.py:680
  423.8 4.4 convolution_convert_fusion.2
  429.4 9.4 %norm_back.1 = (bf16[1024,2048]{1,0:T(8,128)(2,1)}, f32[1024,256]{1,0:T(8,128)S(1)}, f32[1,256]{1,0:T(1,128)S(1)}) custom-call(s32[1]{0:T(128)} %bitcast.refs_0_.mp_ref, bf16[4,512,256]{2,1,0:T(8,128)(2,1)S(1)} %pad_maximum_fusion.10.refs_1_, bf16[4,512,256]{2,1,0:T(8,128)(2,1)S(1)} %collective-permute-done.36.refs_2_, ...), custom_call_target="tpu_custom_call" | custom-call | flops 419430 | bytes 167772 | tf_op jit(solution)/shard_map/norm_back/pallas_call | solution.py:834
  439.8 6.1 fusion.94.dm_ref
  445.8 7.6 %delta_tail.1 = (f32[1024,512]{1,0:T(8,128)S(1)}, bf16[1024,512]{1,0:T(8,128)(2,1)S(1)}, f32[2,256]{1,0:T(2,128)S(1)}, f32[2,8,128,256]{3,2,1,0:T(8,128)}, f32[2,128,256]{2,1,0:T(8,128)S(1)}) custom-call(f32[1024,512]{1,0:T(8,128)} %fusion.94.dm_ref, f32[1024,512]{1,0:T(8,128)} %get-tuple-element.261.o_ref, f32[2,256]{1,0:T(2,128)S(1)} %copy-done.52, ...), custom_call_target="tpu_custom_call" | custom-call | flops 53687092 | bytes 122880 | tf_op jit(solution)/shard_map/delta_tail/pallas_call | solution.py:366
  460.6 6.1 collective-permute-done.38
  468.3 5.6 collective-permute-done.39
  477.2 5.6 delta_early.1
  486.3 19.9 %delta_grads.1 = (f32[1024,1024]{1,0:T(8,128)}, f32[2,1024,8]{2,1,0:T(8,128)S(1)}) custom-call(f32[2,128,256]{2,1,0:T(8,128)S(1)} %convert_element_type.471.end_ref, f32[1024,1024]{1,0:T(8,128)} %copy-done, f32[2,1024,8]{2,1,0:T(8,128)S(1)} %copy-done.5, f32[2,8,128,128]{3,2,1,0:T(8,128)S(1)} %copy-done.32, f32[2,8,128,128]{3,2,1,0:T(8,128)S(1)} %copy-done.18, ...), custom_call_target="tpu_custom_call" | custom-call | flops 161061280 | bytes 245760 | tf_op jit(solution)/shard_map/delta_grads/pallas_call | solution.py:491
  508.4 12.3 %front_back.1 = (bf16[1024,1536]{1,0:T(8,128)(2,1)S(1)}, f32[16,1536]{1,0:T(8,128)S(1)}, f32[4,1536]{1,0:T(4,128)S(1)}) custom-call(f32[1024,1024]{1,0:T(8,128)} %get-tuple-element.190.x_ref, f32[16,1024]{1,0:T(8,128)S(1)} %get-tuple-element.191.rim_ref, f32[1024,1024]{1,0:T(8,128)} %get-tuple-element.235.conv_ref, f32[1024,8]{1,0:T(8,128)S(1)} %copy-done.9, ...), custom_call_target="tpu_custom_call" | custom-call | flops 1258291 | bytes 220200 | tf_op jit(solution)/shard_map/front_back/pallas_call | solution.py:650
  520.9 8.7 %convolution_convert_fusion = bf16[2048,1536]{1,0:T(8,128)(2,1)} fusion(bf16[1024,2048]{1,0:T(8,128)(2,1)S(1)} %copy-done.56, bf16[1024,1536]{1,0:T(8,128)(2,1)S(1)} %maximum_dynamic-update-slice_fusion.refs_2_.refs_4_.refs_6_.refs_8_), kind=kOutput, calls=%fused_computation | convolution fusion | flops 6445596672 | bytes 13631488 | tf_op jit(solution)/shard_map/dot_general | solution.py:963
  534.8 6.8 block_products.15
  541.6 7.3 %block_products.12 = f32[4,1024,256]{2,1,0:T(8,128)} custom-call(s32[1]{0:T(128)} %bitcast.refs_0_.mp_ref, bf16[1024,16]{1,0:T(8,128)(2,1)S(1)} %get-tuple-element.286.refs_0_, bf16[2048,16]{1,0:T(8,128)(2,1)S(1)} %bitcast.117, bf16[1024,1536]{1,0:T(8,128)(2,1)S(1)} %maximum_dynamic-update-slice_fusion.refs_2_.refs_4_.refs_6_.refs_8_, ...), custom_call_target="tpu_custom_call" | custom-call | flops 32547800 | bytes 41943 | tf_op jit(solution)/shard_map/block_products/pallas_call | solution.py:897
  549.0 5.1 block_products.14
  570.4 8.3 %collective-permute-done.48 = bf16[2,512,256]{2,1,0:T(8,128)(2,1)S(1)} collective-permute-done((bf16[2,512,256]{2,1,0:T(8,128)(2,1)S(1)}, bf16[2,512,256]{2,1,0:T(8,128)(2,1)S(1)}, u32[]{:S(2)}, u32[]{:S(2)}) %collective-permute-start.48) | collective-permute-done | bytes 524320 | tf_op jit(solution)/shard_map/ppermute | solution.py:680
  583.4 6.5 collective-permute-done.43
  636.8 38.8 %reduce-scatter.4.cloned.1.call-done = bf16[512,1536]{1,0:T(8,128)(2,1)} async-done(((bf16[2048,1536]{1,0:T(8,128)(2,1)}), bf16[512,1536]{1,0:T(8,128)(2,1)}) %reduce-scatter.4.cloned.1.call-update) | async-done | bytes 1572880 | tf_op jit(solution)/shard_map/reduce_scatter | solution.py:1275
  675.7 4.9 reshape.231
  (421 shorter events, 205.6 us)
Async XLA Ops:
  7.2 88.6 %all-gather.4.cloned.1.call-start = ((), (), s32[]{:S(2)}) async-start(), calls=%async_computation.3 | async-start | bytes 5406720 | tf_op jit(solution)/shard_map/all_gather | solution.py:1190
  9.8 224.1 %all-gather.6.cloned.1.call-start = ((), (), s32[]{:S(2)}) async-start(), calls=%async_computation.4 | async-start | bytes 9175040 | tf_op jit(solution)/shard_map/all_gather | solution.py:1197
  9.9 9.3 %collective-permute-start = (bf16[1,512,256]{2,1,0:T(8,128)(2,1)S(1)}, bf16[1,512,256]{2,1,0:T(8,128)(2,1)S(1)}, u32[]{:S(2)}, u32[]{:S(2)}) collective-permute-start(bf16[1,512,256]{2,1,0:T(8,128)(2,1)S(1)} %get-tuple-element.163), channel_id=1, source_target_pairs={{0,4},{1,5},{2,6},{3,7},{4,0},{5,1},{6,2},{7,3},{8,12},{9,13},{10,... | collective-permute-start | bytes 786440 | tf_op jit(solution)/shard_map/ppermute | solution.py:680
  12.9 7.8 %collective-permute-start.1 = (bf16[1,512,256]{2,1,0:T(8,128)(2,1)S(1)}, bf16[1,512,256]{2,1,0:T(8,128)(2,1)S(1)}, u32[]{:S(2)}, u32[]{:S(2)}) collective-permute-start(bf16[1,512,256]{2,1,0:T(8,128)(2,1)S(1)} %get-tuple-element.164), channel_id=1, source_target_pairs={{0,2},{1,3},{2,0},{3,1},{4,6},{5,7},{6,4},{7,5},{8,10},{9,11},{10,... | collective-permute-start | bytes 786440 | tf_op jit(solution)/shard_map/ppermute | solution.py:680
  22.3 12.8 %collective-permute-start.2 = (bf16[2,512,256]{2,1,0:T(8,128)(2,1)}, bf16[2,512,256]{2,1,0:T(8,128)(2,1)}, u32[]{:S(2)}, u32[]{:S(2)}) collective-permute-start(bf16[2,512,256]{2,1,0:T(8,128)(2,1)} %pad_maximum_fusion.13), channel_id=1, source_target_pairs={{0,2},{1,3},{2,0},{3,1},{4,6},{5,7},{6,4},{7,5},{8,10},{9,11},{10,... | collective-permute-start | bytes 1572872 | tf_op jit(solution)/shard_map/ppermute | solution.py:680
  23.8 12.5 %collective-permute-start.3 = (bf16[2,512,256]{2,1,0:T(8,128)(2,1)}, bf16[2,512,256]{2,1,0:T(8,128)(2,1)}, u32[]{:S(2)}, u32[]{:S(2)}) collective-permute-start(bf16[2,512,256]{2,1,0:T(8,128)(2,1)} %pad_maximum_fusion.14), channel_id=1, source_target_pairs={{0,4},{1,5},{2,6},{3,7},{4,0},{5,1},{6,2},{7,3},{8,12},{9,13},{10,... | collective-permute-start | bytes 1572872 | tf_op jit(solution)/shard_map/ppermute | solution.py:680
  37.8 306.6 %all-gather.8.cloned.1.call-start = ((), (), s32[]{:S(2)}) async-start(), calls=%async_computation.5 | async-start | bytes 7208960 | tf_op jit(solution)/shard_map/all_gather | solution.py:1208
  47.8 8.4 %collective-permute-start.7 = (bf16[1,512,256]{2,1,0:T(8,128)(2,1)S(1)}, bf16[1,512,256]{2,1,0:T(8,128)(2,1)S(1)}, u32[]{:S(2)}, u32[]{:S(2)}) collective-permute-start(bf16[1,512,256]{2,1,0:T(8,128)(2,1)S(1)} %get-tuple-element.177), channel_id=1, source_target_pairs={{0,4},{1,5},{2,6},{3,7},{4,0},{5,1},{6,2},{7,3},{8,12},{9,13},{10,... | collective-permute-start | bytes 786440 | tf_op jit(solution)/shard_map/ppermute | solution.py:680
  48.5 8.1 %collective-permute-start.8 = (bf16[1,512,256]{2,1,0:T(8,128)(2,1)S(1)}, bf16[1,512,256]{2,1,0:T(8,128)(2,1)S(1)}, u32[]{:S(2)}, u32[]{:S(2)}) collective-permute-start(bf16[1,512,256]{2,1,0:T(8,128)(2,1)S(1)} %get-tuple-element.178), channel_id=1, source_target_pairs={{0,2},{1,3},{2,0},{3,1},{4,6},{5,7},{6,4},{7,5},{8,10},{9,11},{10,... | collective-permute-start | bytes 786440 | tf_op jit(solution)/shard_map/ppermute | solution.py:680
  56.7 13.0 %collective-permute-start.10 = (bf16[2,512,256]{2,1,0:T(8,128)(2,1)S(1)}, bf16[2,512,256]{2,1,0:T(8,128)(2,1)S(1)}, u32[]{:S(2)}, u32[]{:S(2)}) collective-permute-start(bf16[2,512,256]{2,1,0:T(8,128)(2,1)S(1)} %pad_maximum_fusion.16), channel_id=1, source_target_pairs={{0,4},{1,5},{2,6},{3,7},{4,0},{5,1},{6,2},{7,3},{8,12},{9,13},{10,... | collective-permute-start | bytes 1572872 | tf_op jit(solution)/shard_map/ppermute | solution.py:680
  58.1 12.6 %collective-permute-start.9 = (bf16[2,512,256]{2,1,0:T(8,128)(2,1)S(1)}, bf16[2,512,256]{2,1,0:T(8,128)(2,1)S(1)}, u32[]{:S(2)}, u32[]{:S(2)}) collective-permute-start(bf16[2,512,256]{2,1,0:T(8,128)(2,1)S(1)} %pad_maximum_fusion.15), channel_id=1, source_target_pairs={{0,2},{1,3},{2,0},{3,1},{4,6},{5,7},{6,4},{7,5},{8,10},{9,11},{10,... | collective-permute-start | bytes 1572872 | tf_op jit(solution)/shard_map/ppermute | solution.py:680
  72.6 23.2 %collective-permute-start.6 = (bf16[16,2048]{1,0:T(8,128)(2,1)S(1)}, bf16[16,2048]{1,0:T(8,128)(2,1)S(1)}, u32[]{:S(2)}, u32[]{:S(2)}) collective-permute-start(bf16[16,2048]{1,0:T(8,128)(2,1)S(1)} %slice.406), channel_id=1, source_target_pairs={{0,8},{8,16},{16,24},{1,9},{9,17},{17,25},{2,10},{10,18},{18,26},{... | collective-permute-start | bytes 196616 | tf_op jit(solution)/shard_map/ppermute | solution.py:955
  152.4 12.6 %collective-permute-start.13 = (bf16[2,128,256]{2,1,0:T(8,128)(2,1)}, bf16[2,128,256]{2,1,0:T(8,128)(2,1)S(1)}, u32[]{:S(2)}, u32[]{:S(2)}) collective-permute-start(bf16[2,128,256]{2,1,0:T(8,128)(2,1)} %convert_element_type.421), channel_id=1, source_target_pairs={{0,8},{8,16},{16,24},{1,9},{9,17},{17,25},{2,10},{10,18},{18,26},{... | collective-permute-start | bytes 393224 | tf_op jit(solution)/shard_map/ppermute | solution.py:955
  162.5 465.0 %reduce-scatter.8.cloned.1.call-start = ((), (), s32[]{:S(2)}) async-start(), calls=%async_computation.8 | async-start | bytes 7045120 | tf_op jit(solution)/shard_map/reduce_scatter | solution.py:1244
  165.3 10.2 %collective-permute-start.14 = (bf16[2,128,256]{2,1,0:T(8,128)(2,1)S(1)}, bf16[2,128,256]{2,1,0:T(8,128)(2,1)S(1)}, u32[]{:S(2)}, u32[]{:S(2)}) collective-permute-start(bf16[2,128,256]{2,1,0:T(8,128)(2,1)S(1)} %fusion.3), channel_id=1, source_target_pairs={{0,8},{8,16},{16,24},{1,9},{9,17},{17,25},{2,10},{10,18},{18,26},{... | collective-permute-start | bytes 393224 | tf_op jit(solution)/shard_map/ppermute | solution.py:955
  175.8 14.4 %collective-permute-start.15 = (bf16[2,128,256]{2,1,0:T(8,128)(2,1)S(1)}, bf16[2,128,256]{2,1,0:T(8,128)(2,1)S(1)}, u32[]{:S(2)}, u32[]{:S(2)}) collective-permute-start(bf16[2,128,256]{2,1,0:T(8,128)(2,1)S(1)} %fusion.4), channel_id=1, source_target_pairs={{0,8},{8,16},{16,24},{1,9},{9,17},{17,25},{2,10},{10,18},{18,26},{... | collective-permute-start | bytes 393224 | tf_op jit(solution)/shard_map/ppermute | solution.py:955
  263.1 14.0 %collective-permute-start.17 = (bf16[2,512,256]{2,1,0:T(8,128)(2,1)S(1)}, bf16[2,512,256]{2,1,0:T(8,128)(2,1)S(1)}, u32[]{:S(2)}, u32[]{:S(2)}) collective-permute-start(bf16[2,512,256]{2,1,0:T(8,128)(2,1)S(1)} %pad_maximum_fusion.17), channel_id=1, source_target_pairs={{0,2},{1,3},{2,0},{3,1},{4,6},{5,7},{6,4},{7,5},{8,10},{9,11},{10,... | collective-permute-start | bytes 1572872 | tf_op jit(solution)/shard_map/ppermute | solution.py:680
  264.8 13.7 %collective-permute-start.18 = (bf16[2,512,256]{2,1,0:T(8,128)(2,1)S(1)}, bf16[2,512,256]{2,1,0:T(8,128)(2,1)S(1)}, u32[]{:S(2)}, u32[]{:S(2)}) collective-permute-start(bf16[2,512,256]{2,1,0:T(8,128)(2,1)S(1)} %pad_maximum_fusion.18), channel_id=1, source_target_pairs={{0,4},{1,5},{2,6},{3,7},{4,0},{5,1},{6,2},{7,3},{8,12},{9,13},{10,... | collective-permute-start | bytes 1572872 | tf_op jit(solution)/shard_map/ppermute | solution.py:680
  278.7 7.4 %collective-permute-start.19 = (bf16[1,512,256]{2,1,0:T(8,128)(2,1)S(1)}, bf16[1,512,256]{2,1,0:T(8,128)(2,1)S(1)}, u32[]{:S(2)}, u32[]{:S(2)}) collective-permute-start(bf16[1,512,256]{2,1,0:T(8,128)(2,1)S(1)} %get-tuple-element.213), channel_id=1, source_target_pairs={{0,4},{1,5},{2,6},{3,7},{4,0},{5,1},{6,2},{7,3},{8,12},{9,13},{10,... | collective-permute-start | bytes 786440 | tf_op jit(solution)/shard_map/ppermute | solution.py:680
  295.9 10.9 %collective-permute-start.23 = (bf16[2,512,256]{2,1,0:T(8,128)(2,1)S(1)}, bf16[2,512,256]{2,1,0:T(8,128)(2,1)S(1)}, u32[]{:S(2)}, u32[]{:S(2)}) collective-permute-start(bf16[2,512,256]{2,1,0:T(8,128)(2,1)S(1)} %pad_maximum_fusion.19), channel_id=1, source_target_pairs={{0,2},{1,3},{2,0},{3,1},{4,6},{5,7},{6,4},{7,5},{8,10},{9,11},{10,... | collective-permute-start | bytes 1572872 | tf_op jit(solution)/shard_map/ppermute | solution.py:680
  296.4 10.8 %collective-permute-start.24 = (bf16[2,512,256]{2,1,0:T(8,128)(2,1)S(1)}, bf16[2,512,256]{2,1,0:T(8,128)(2,1)S(1)}, u32[]{:S(2)}, u32[]{:S(2)}) collective-permute-start(bf16[2,512,256]{2,1,0:T(8,128)(2,1)S(1)} %pad_maximum_fusion.20), channel_id=1, source_target_pairs={{0,4},{1,5},{2,6},{3,7},{4,0},{5,1},{6,2},{7,3},{8,12},{9,13},{10,... | collective-permute-start | bytes 1572872 | tf_op jit(solution)/shard_map/ppermute | solution.py:680
  307.4 8.8 %collective-permute-start.25 = (bf16[4,512,256]{2,1,0:T(8,128)(2,1)S(1)}, bf16[4,512,256]{2,1,0:T(8,128)(2,1)}, u32[]{:S(2)}, u32[]{:S(2)}) collective-permute-start(bf16[4,512,256]{2,1,0:T(8,128)(2,1)S(1)} %pad_maximum_fusion.7.refs_1_.refs_5_), channel_id=1, source_target_pairs={{0,1},{1,0},{2,3},{3,2},{4,5},{5,4},{6,7},{7,6},{8,9},{9,8},{10,11... | collective-permute-start | bytes 3145736 | tf_op jit(solution)/shard_map/ppermute | solution.py:680
  307.5 8.7 %collective-permute-start.26 = (bf16[4,512,256]{2,1,0:T(8,128)(2,1)S(1)}, bf16[4,512,256]{2,1,0:T(8,128)(2,1)}, u32[]{:S(2)}, u32[]{:S(2)}) collective-permute-start(bf16[4,512,256]{2,1,0:T(8,128)(2,1)S(1)} %pad_maximum_fusion.8.refs_3_.refs_7_), channel_id=1, source_target_pairs={{0,1},{1,0},{2,3},{3,2},{4,5},{5,4},{6,7},{7,6},{8,9},{9,8},{10,11... | collective-permute-start | bytes 3145736 | tf_op jit(solution)/shard_map/ppermute | solution.py:680
  365.0 267.3 %reduce-scatter.6.cloned.1.call-start = ((), (), s32[]{:S(2)}) async-start(), calls=%async_computation.7 | async-start | bytes 6144000 | tf_op jit(solution)/shard_map/reduce_scatter | solution.py:1258
  379.4 14.4 %collective-permute-start.28 = (bf16[2,512,256]{2,1,0:T(8,128)(2,1)S(1)}, bf16[2,512,256]{2,1,0:T(8,128)(2,1)S(1)}, u32[]{:S(2)}, u32[]{:S(2)}) collective-permute-start(bf16[2,512,256]{2,1,0:T(8,128)(2,1)S(1)} %pad_maximum_fusion.21), channel_id=1, source_target_pairs={{0,2},{1,3},{2,0},{3,1},{4,6},{5,7},{6,4},{7,5},{8,10},{9,11},{10,... | collective-permute-start | bytes 1572872 | tf_op jit(solution)/shard_map/ppermute | solution.py:680
  381.0 13.9 %collective-permute-start.29 = (bf16[2,512,256]{2,1,0:T(8,128)(2,1)S(1)}, bf16[2,512,256]{2,1,0:T(8,128)(2,1)S(1)}, u32[]{:S(2)}, u32[]{:S(2)}) collective-permute-start(bf16[2,512,256]{2,1,0:T(8,128)(2,1)S(1)} %pad_maximum_fusion.22), channel_id=1, source_target_pairs={{0,4},{1,5},{2,6},{3,7},{4,0},{5,1},{6,2},{7,3},{8,12},{9,13},{10,... | collective-permute-start | bytes 1572872 | tf_op jit(solution)/shard_map/ppermute | solution.py:680
  395.1 7.6 %collective-permute-start.30 = (bf16[1,512,256]{2,1,0:T(8,128)(2,1)S(1)}, bf16[1,512,256]{2,1,0:T(8,128)(2,1)S(1)}, u32[]{:S(2)}, u32[]{:S(2)}) collective-permute-start(bf16[1,512,256]{2,1,0:T(8,128)(2,1)S(1)} %get-tuple-element.243), channel_id=1, source_target_pairs={{0,4},{1,5},{2,6},{3,7},{4,0},{5,1},{6,2},{7,3},{8,12},{9,13},{10,... | collective-permute-start | bytes 786440 | tf_op jit(solution)/shard_map/ppermute | solution.py:680
  396.7 7.3 %collective-permute-start.31 = (bf16[1,512,256]{2,1,0:T(8,128)(2,1)S(1)}, bf16[1,512,256]{2,1,0:T(8,128)(2,1)S(1)}, u32[]{:S(2)}, u32[]{:S(2)}) collective-permute-start(bf16[1,512,256]{2,1,0:T(8,128)(2,1)S(1)} %get-tuple-element.244), channel_id=1, source_target_pairs={{0,2},{1,3},{2,0},{3,1},{4,6},{5,7},{6,4},{7,5},{8,10},{9,11},{10,... | collective-permute-start | bytes 786440 | tf_op jit(solution)/shard_map/ppermute | solution.py:680
  411.4 11.1 %collective-permute-start.34 = (bf16[2,512,256]{2,1,0:T(8,128)(2,1)S(1)}, bf16[2,512,256]{2,1,0:T(8,128)(2,1)S(1)}, u32[]{:S(2)}, u32[]{:S(2)}) collective-permute-start(bf16[2,512,256]{2,1,0:T(8,128)(2,1)S(1)} %pad_maximum_fusion.23), channel_id=1, source_target_pairs={{0,2},{1,3},{2,0},{3,1},{4,6},{5,7},{6,4},{7,5},{8,10},{9,11},{10,... | collective-permute-start | bytes 1572872 | tf_op jit(solution)/shard_map/ppermute | solution.py:680
  412.2 10.9 %collective-permute-start.35 = (bf16[2,512,256]{2,1,0:T(8,128)(2,1)S(1)}, bf16[2,512,256]{2,1,0:T(8,128)(2,1)S(1)}, u32[]{:S(2)}, u32[]{:S(2)}) collective-permute-start(bf16[2,512,256]{2,1,0:T(8,128)(2,1)S(1)} %pad_maximum_fusion.24), channel_id=1, source_target_pairs={{0,4},{1,5},{2,6},{3,7},{4,0},{5,1},{6,2},{7,3},{8,12},{9,13},{10,... | collective-permute-start | bytes 1572872 | tf_op jit(solution)/shard_map/ppermute | solution.py:680
  459.1 216.6 %reduce-scatter.4.cloned.1.call-start = ((), (), s32[]{:S(2)}) async-start(), calls=%async_computation.6 | async-start | bytes 7864320 | tf_op jit(solution)/shard_map/reduce_scatter | solution.py:1275
  459.2 7.5 %collective-permute-start.38 = (bf16[2,128,256]{2,1,0:T(8,128)(2,1)S(1)}, bf16[2,128,256]{2,1,0:T(8,128)(2,1)S(1)}, u32[]{:S(2)}, u32[]{:S(2)}) collective-permute-start(bf16[2,128,256]{2,1,0:T(8,128)(2,1)S(1)} %convert_element_type.468), channel_id=1, source_target_pairs={{8,0},{16,8},{24,16},{9,1},{17,9},{25,17},{10,2},{18,10},{26,18},{... | collective-permute-start | bytes 393224 | tf_op jit(solution)/shard_map/ppermute | solution.py:955
  474.1 12.1 %collective-permute-start.40 = (bf16[2,128,256]{2,1,0:T(8,128)(2,1)S(1)}, bf16[2,128,256]{2,1,0:T(8,128)(2,1)S(1)}, u32[]{:S(2)}, u32[]{:S(2)}) collective-permute-start(bf16[2,128,256]{2,1,0:T(8,128)(2,1)S(1)} %fusion.6), channel_id=1, source_target_pairs={{8,0},{16,8},{24,16},{9,1},{17,9},{25,17},{10,2},{18,10},{26,18},{... | collective-permute-start | bytes 393224 | tf_op jit(solution)/shard_map/ppermute | solution.py:955
  507.1 13.7 %collective-permute-start.41 = (f32[8,1024]{1,0:T(8,128)S(1)}, f32[8,1024]{1,0:T(8,128)S(1)}, u32[]{:S(2)}, u32[]{:S(2)}) collective-permute-start(f32[8,1024]{1,0:T(8,128)S(1)} %rim_back.1), channel_id=1, source_target_pairs={{8,0},{16,8},{24,16},{9,1},{17,9},{25,17},{10,2},{18,10},{26,18},{... | collective-permute-start | bytes 98312 | tf_op jit(solution)/shard_map/ppermute | solution.py:955
  541.6 20.4 %collective-permute-start.47 = (bf16[4,1024,256]{2,1,0:T(8,128)(2,1)}, bf16[4,1024,256]{2,1,0:T(8,128)(2,1)}, u32[]{:S(2)}, u32[]{:S(2)}) collective-permute-start(bf16[4,1024,256]{2,1,0:T(8,128)(2,1)} %block_products.15), channel_id=1, source_target_pairs={{0,1},{1,0},{2,3},{3,2},{4,5},{5,4},{6,7},{7,6},{8,9},{9,8},{10,11... | collective-permute-start | bytes 6291464 | tf_op jit(solution)/shard_map/ppermute | solution.py:680
  554.1 12.5 %collective-permute-start.42 = (bf16[4,1024,256]{2,1,0:T(8,128)(2,1)}, bf16[4,1024,256]{2,1,0:T(8,128)(2,1)}, u32[]{:S(2)}, u32[]{:S(2)}) collective-permute-start(bf16[4,1024,256]{2,1,0:T(8,128)(2,1)} %block_products.14), channel_id=1, source_target_pairs={{0,1},{1,0},{2,3},{3,2},{4,5},{5,4},{6,7},{7,6},{8,9},{9,8},{10,11... | collective-permute-start | bytes 6291464 | tf_op jit(solution)/shard_map/ppermute | solution.py:680
  563.9 14.8 %collective-permute-start.48 = (bf16[2,512,256]{2,1,0:T(8,128)(2,1)S(1)}, bf16[2,512,256]{2,1,0:T(8,128)(2,1)S(1)}, u32[]{:S(2)}, u32[]{:S(2)}) collective-permute-start(bf16[2,512,256]{2,1,0:T(8,128)(2,1)S(1)} %pad_maximum_fusion.27), channel_id=1, source_target_pairs={{0,2},{1,3},{2,0},{3,1},{4,6},{5,7},{6,4},{7,5},{8,10},{9,11},{10,... | collective-permute-start | bytes 1572872 | tf_op jit(solution)/shard_map/ppermute | solution.py:680
  565.1 14.8 %collective-permute-start.49 = (bf16[2,512,256]{2,1,0:T(8,128)(2,1)S(1)}, bf16[2,512,256]{2,1,0:T(8,128)(2,1)S(1)}, u32[]{:S(2)}, u32[]{:S(2)}) collective-permute-start(bf16[2,512,256]{2,1,0:T(8,128)(2,1)S(1)} %pad_maximum_fusion.28), channel_id=1, source_target_pairs={{0,4},{1,5},{2,6},{3,7},{4,0},{5,1},{6,2},{7,3},{8,12},{9,13},{10,... | collective-permute-start | bytes 1572872 | tf_op jit(solution)/shard_map/ppermute | solution.py:680
  568.5 21.4 %collective-permute-start.43 = (bf16[2,512,256]{2,1,0:T(8,128)(2,1)S(1)}, bf16[2,512,256]{2,1,0:T(8,128)(2,1)S(1)}, u32[]{:S(2)}, u32[]{:S(2)}) collective-permute-start(bf16[2,512,256]{2,1,0:T(8,128)(2,1)S(1)} %pad_maximum_fusion.25), channel_id=1, source_target_pairs={{0,2},{1,3},{2,0},{3,1},{4,6},{5,7},{6,4},{7,5},{8,10},{9,11},{10,... | collective-permute-start | bytes 1572872 | tf_op jit(solution)/shard_map/ppermute | solution.py:680
  569.0 22.2 %collective-permute-start.44 = (bf16[2,512,256]{2,1,0:T(8,128)(2,1)S(1)}, bf16[2,512,256]{2,1,0:T(8,128)(2,1)S(1)}, u32[]{:S(2)}, u32[]{:S(2)}) collective-permute-start(bf16[2,512,256]{2,1,0:T(8,128)(2,1)S(1)} %pad_maximum_fusion.26), channel_id=1, source_target_pairs={{0,4},{1,5},{2,6},{3,7},{4,0},{5,1},{6,2},{7,3},{8,12},{9,13},{10,... | collective-permute-start | bytes 1572872 | tf_op jit(solution)/shard_map/ppermute | solution.py:680
  581.2 15.6 %collective-permute-start.50 = (bf16[1,512,256]{2,1,0:T(8,128)(2,1)S(1)}, bf16[1,512,256]{2,1,0:T(8,128)(2,1)S(1)}, u32[]{:S(2)}, u32[]{:S(2)}) collective-permute-start(bf16[1,512,256]{2,1,0:T(8,128)(2,1)S(1)} %get-tuple-element.304), channel_id=1, source_target_pairs={{0,4},{1,5},{2,6},{3,7},{4,0},{5,1},{6,2},{7,3},{8,12},{9,13},{10,... | collective-permute-start | bytes 786440 | tf_op jit(solution)/shard_map/ppermute | solution.py:680
  582.7 14.1 %collective-permute-start.51 = (bf16[1,512,256]{2,1,0:T(8,128)(2,1)S(1)}, bf16[1,512,256]{2,1,0:T(8,128)(2,1)S(1)}, u32[]{:S(2)}, u32[]{:S(2)}) collective-permute-start(bf16[1,512,256]{2,1,0:T(8,128)(2,1)S(1)} %get-tuple-element.305), channel_id=1, source_target_pairs={{0,2},{1,3},{2,0},{3,1},{4,6},{5,7},{6,4},{7,5},{8,10},{9,11},{10,... | collective-permute-start | bytes 786440 | tf_op jit(solution)/shard_map/ppermute | solution.py:680
  593.2 11.3 %collective-permute-start.45 = (bf16[1,512,256]{2,1,0:T(8,128)(2,1)}, bf16[1,512,256]{2,1,0:T(8,128)(2,1)S(1)}, u32[]{:S(2)}, u32[]{:S(2)}) collective-permute-start(bf16[1,512,256]{2,1,0:T(8,128)(2,1)} %get-tuple-element.294), channel_id=1, source_target_pairs={{0,4},{1,5},{2,6},{3,7},{4,0},{5,1},{6,2},{7,3},{8,12},{9,13},{10,... | collective-permute-start | bytes 786440 | tf_op jit(solution)/shard_map/ppermute | solution.py:680
  594.6 12.6 %collective-permute-start.46 = (bf16[1,512,256]{2,1,0:T(8,128)(2,1)}, bf16[1,512,256]{2,1,0:T(8,128)(2,1)S(1)}, u32[]{:S(2)}, u32[]{:S(2)}) collective-permute-start(bf16[1,512,256]{2,1,0:T(8,128)(2,1)} %get-tuple-element.295), channel_id=1, source_target_pairs={{0,2},{1,3},{2,0},{3,1},{4,6},{5,7},{6,4},{7,5},{8,10},{9,11},{10,... | collective-permute-start | bytes 786440 | tf_op jit(solution)/shard_map/ppermute | solution.py:680
  599.4 7.9 %collective-permute-start.52 = (f32[8,128]{1,0:T(8,128)S(1)}, f32[8,128]{1,0:T(8,128)S(1)}, u32[]{:S(2)}, u32[]{:S(2)}) collective-permute-start(f32[8,128]{1,0:T(8,128)S(1)} %bitcast.139), channel_id=1, source_target_pairs={{0,1},{1,0},{2,3},{3,2},{4,5},{5,4},{6,7},{7,6},{8,9},{9,8},{10,11... | collective-permute-start | bytes 12296 | tf_op jit(solution)/shard_map/ppermute | solution.py:680
  599.6 16.1 %collective-permute-start.55 = (f32[112,128]{1,0:T(8,128)S(1)}, f32[112,128]{1,0:T(8,128)}, u32[]{:S(2)}, u32[]{:S(2)}) collective-permute-start(f32[112,128]{1,0:T(8,128)S(1)} %pad_bitcast_fusion), channel_id=1, source_target_pairs={{0,8},{8,16},{16,24},{24,0},{1,9},{9,17},{17,25},{25,1},{2,10},{10... | collective-permute-start | bytes 172040 | tf_op jit(solution)/shard_map/ppermute | solution.py:948
  602.9 12.8 %collective-permute-start.56 = (f32[112,128]{1,0:T(8,128)S(1)}, f32[112,128]{1,0:T(8,128)}, u32[]{:S(2)}, u32[]{:S(2)}) collective-permute-start(f32[112,128]{1,0:T(8,128)S(1)} %pad_bitcast_fusion), channel_id=1, source_target_pairs={{0,16},{8,24},{16,0},{24,8},{1,17},{9,25},{17,1},{25,9},{2,18},{10... | collective-permute-start | bytes 172040 | tf_op jit(solution)/shard_map/ppermute | solution.py:948
  604.5 11.2 %collective-permute-start.57 = (f32[112,128]{1,0:T(8,128)S(1)}, f32[112,128]{1,0:T(8,128)}, u32[]{:S(2)}, u32[]{:S(2)}) collective-permute-start(f32[112,128]{1,0:T(8,128)S(1)} %pad_bitcast_fusion), channel_id=1, source_target_pairs={{0,24},{8,0},{16,8},{24,16},{1,25},{9,1},{17,9},{25,17},{2,26},{10... | collective-permute-start | bytes 172040 | tf_op jit(solution)/shard_map/ppermute | solution.py:948
  (103 other events, 1242.0 us)
Sparse Core Ops, SparseCore 0:
  10.2 85.6 all-gather.3
  97.4 136.3 all-gather.5
  235.4 108.9 all-gather.7
  365.1 98.3 reduce-scatter.7
  465.7 92.6 reduce-scatter.5
  560.7 114.9 reduce-scatter.3

commit v4 on v3

--- a/solution.py
+++ b/solution.py
@@ -1231,7 +1231,7 @@
     )
     branch, _ = reduce_mp([(mixed, 0, god_full, gate_cols, feats, 0)], mp_pos, cols)
     middle = residual.astype(F32) + branch
-    found_mid = gather_mp(middle.astype(BF16))
+    found_mid = gather_mp(middle)
     normed2, _ = assemble(found_mid, mp_pos, ffn_gain)
     grad_hidden = dot(full_grad, after(down_turned, branch))
     gu_full = after(gu_full, grad_hidden, normed2)
@@ -1243,7 +1243,7 @@
     )
     dw_gu = lax.psum_scatter(part_gu, "seq", scatter_dimension=0, tiled=True)
     part_down = dot(after(hidden, kept_gn2), full_grad, TN).astype(BF16)
-    found_gn2 = gather_mp(grad_normed2.astype(BF16))
+    found_gn2 = gather_mp(grad_normed2)
 
     grad_branch, grad_middle, dffn_gain = norm_back(
         found_gn2, found_mid, full_grad, ffn_gain, grad_normed2, middle, mp_pos

time: 694 us -> 744 us (1.072)
  waiting for transfers between devices: 271 us -> 302 us
  local copies, waits for them, and re-layouts: 59.4 us -> 69 us
    ppermute x50, waiting for transfers between devices: 130 us -> 168 us  [flip(): return lax.ppermute(value, 'mp', [(i, i ^ 1 << bit) for i in range(count)])]
    reduce_scatter x1, waiting for transfers between devices: 38.8 us -> 20.4 us  [shards(): lax.psum_scatter(part_mixer, 'seq', scatter_dimension=0, tiled=True)]
    ppermute x8, waiting for transfers between devices: 21.1 us -> 35.2 us  [shifted(): lax.ppermute(value, 'seq', [(i, i + steps) for i in range(first, last)])]
    unnamed x169 -> x185, local copies, waits for them, and re-layouts: 29.7 us -> 38.7 us
  transfers between devices with their start and end apart: 67 -> 67, of which waited for: 44 -> 45; matrix products, arithmetic and copies ran while one was open for 15% -> 13% of each run, Pallas kernels for 26% -> 23%
where the time goes in v4:
time: 744 us; the launch traced here: 738 us
  waiting for transfers between devices  302 us (41%)
  Pallas kernels  192 us (26%)
  starting transfers between devices  76.9 us (10%)
  local copies, waits for them, and re-layouts  69 us (9%)
  matrix products  43 us (6%)
  other arithmetic  38.7 us (5%)
  between operations  15.7 us (2%)
    ppermute x50, waiting for transfers between devices, flip(): return lax.ppermute(value, 'mp', [(i, i ^ 1 << bit) for i in range(count)])  168 us
    ppermute x50, starting transfers between devices, flip(): return lax.ppermute(value, 'mp', [(i, i ^ 1 << bit) for i in range(count)])  43.7 us
    all_gather x1, waiting for transfers between devices, shards(): lax.all_gather(after(god_part, found_res[0][0]), 'seq', axis=0, tiled=True)  43.6 us
    pallas_call x8, Pallas kernels, block_products(): pl.pallas_call(functools.partial(block_kernel, len(terms)), grid_spec=plt...  43.5 us
    dot_general x8, matrix products, dot(): return lax.dot_general(left, right, dims, preferred_element_type=F32)  41.9 us
    unnamed x185, local copies, waits for them, and re-layouts  38.7 us
    ppermute x8, waiting for transfers between devices, shifted(): lax.ppermute(value, 'seq', [(i, i + steps) for i in range(first, last)])  35.2 us
    ppermute x8, starting transfers between devices, shifted(): lax.ppermute(value, 'seq', [(i, i + steps) for i in range(first, last)])  28.1 us
  transfers between devices with their start and end apart: 67, of which 45 were waited for; matrix products, arithmetic and copies ran while one was open for 13% of the time, Pallas kernels for 23%

profile of v4, /device:TPU:0, one launch (start us, length us, event | category | flops | bytes accessed | tf_op | source)
XLA Modules:
  0.0 737.5 jit_solution(4312157238334200750)
XLA Ops:
  14.4 4.8 collective-permute-done
  27.6 7.6 %collective-permute-done.2 = bf16[2,512,256]{2,1,0:T(8,128)(2,1)} collective-permute-done((bf16[2,512,256]{2,1,0:T(8,128)(2,1)}, bf16[2,512,256]{2,1,0:T(8,128)(2,1)}, u32[]{:S(2)}, u32[]{:S(2)}) %collective-permute-start.2) | collective-permute-done | bytes 524320 | tf_op jit(solution)/shard_map/ppermute | solution.py:680
  42.2 5.6 assemble.3
  49.2 7.1 collective-permute-done.7
  58.8 11.0 %collective-permute-done.9 = bf16[2,512,256]{2,1,0:T(8,128)(2,1)S(1)} collective-permute-done((bf16[2,512,256]{2,1,0:T(8,128)(2,1)S(1)}, bf16[2,512,256]{2,1,0:T(8,128)(2,1)S(1)}, u32[]{:S(2)}, u32[]{:S(2)}) %collective-permute-start.9) | collective-permute-done | bytes 524320 | tf_op jit(solution)/shard_map/ppermute | solution.py:680
  80.8 15.0 %all-gather.4.cloned.1.call-done.w_ref.refs_3_.refs_7_ = bf16[2112,1024]{1,0:T(8,128)(2,1)} async-done(((bf16[528,1024]{1,0:T(8,128)(2,1)}), bf16[2112,1024]{1,0:T(8,128)(2,1)}) %all-gather.4.cloned.1.call-update) | async-done | bytes 4325392 | tf_op jit(solution)/shard_map/all_gather | solution.py:1190
  95.8 10.9 %project_first.1 = (f32[1024,1024]{1,0:T(8,128)}, f32[1024,16]{1,0:T(8,128)S(1)}, f32[2,1024,8]{2,1,0:T(8,128)S(1)}, f32[16,1024]{1,0:T(8,128)S(1)}) custom-call(bf16[1024,2048]{1,0:T(8,128)(2,1)} %get-tuple-element.175.x_ref, bf16[16,2048]{1,0:T(8,128)(2,1)S(1)} %collective-permute-done.6.rim_ref, ...), custom_call_target="tpu_custom_call" | custom-call | flops 42949672 | bytes 83886 | tf_op jit(solution)/shard_map/project_first/pallas_call | solution.py:1010
  108.6 9.8 %front.1 = (f32[1024,1024]{1,0:T(8,128)S(1)}, f32[1024,1024]{1,0:T(8,128)}) custom-call(f32[1024,1024]{1,0:T(8,128)} %get-tuple-element.190.x_ref, f32[16,1024]{1,0:T(8,128)S(1)} %get-tuple-element.191.rim_ref, f32[1024,8]{1,0:T(8,128)S(1)} %copy.65.mask_ref, f32[4,1024]{1,0:T(4,128)S(1)} %bitcast.112), custom_call_target="tpu_custom_call" | custom-call | flops 419430 | bytes 83886 | tf_op jit(solution)/shard_map/front/pallas_call | solution.py:548
  120.3 17.6 %delta_prep.1 = (f32[2,8,128,128]{3,2,1,0:T(8,128)S(1)}, f32[2,8,128,128]{3,2,1,0:T(8,128)S(1)}, f32[2,8,128,128]{3,2,1,0:T(8,128)S(1)}, f32[2,8,128,128]{3,2,1,...) custom-call(f32[1024,1024]{1,0:T(8,128)} %copy-done, ...), custom_call_target="tpu_custom_call" | custom-call | flops 214748368 | bytes 62914 | tf_op jit(solution)/shard_map/delta_prep/pallas_call | solution.py:149
  141.9 11.0 %delta_values.1 = (f32[2,8,128,256]{3,2,1,0:T(8,128)}, f32[1024,512]{1,0:T(8,128)}, f32[2,8,128,256]{3,2,1,0:T(8,128)}, f32[2,128,256]{2,1,0:T(8,128)S(1)}) custom-call(f32[1024,1024]{1,0:T(8,128)} %copy-done, f32[2,1024,8]{2,1,0:T(8,128)S(1)} %copy-done.7, f32[2,8,128,128]{3,2,1,0:T(8,128)S(1)} %get-tuple-element.197.t_ref, ...), custom_call_target="tpu_custom_call" | custom-call | flops 64424508 | bytes 81920 | tf_op jit(solution)/shard_map/delta_values/pallas_call | solution.py:231
  161.5 8.2 %collective-permute-start.14 = (bf16[2,128,256]{2,1,0:T(8,128)(2,1)S(1)}, bf16[2,128,256]{2,1,0:T(8,128)(2,1)S(1)}, u32[]{:S(2)}, u32[]{:S(2)}) collective-permute-start(bf16[2,128,256]{2,1,0:T(8,128)(2,1)S(1)} %fusion.3), channel_id=1, source_target_pairs={{0,8},{8,16},{16,24},{1,9},{9,17},{17,25},{2,10},{10,18},{18,26},{... | collective-permute-start | bytes 393224 | tf_op jit(solution)/shard_map/ppermute | solution.py:955
  169.7 5.8 collective-permute-done.14
  175.8 8.9 %collective-permute-start.15 = (bf16[2,128,256]{2,1,0:T(8,128)(2,1)S(1)}, bf16[2,128,256]{2,1,0:T(8,128)(2,1)S(1)}, u32[]{:S(2)}, u32[]{:S(2)}) collective-permute-start(bf16[2,128,256]{2,1,0:T(8,128)(2,1)S(1)} %fusion.4), channel_id=1, source_target_pairs={{0,8},{8,16},{16,24},{1,9},{9,17},{17,25},{2,10},{10,18},{18,26},{... | collective-permute-start | bytes 393224 | tf_op jit(solution)/shard_map/ppermute | solution.py:955
  190.2 43.6 %all-gather.6.cloned.1.call-done.refs_1_.refs_5_.refs_9_ = bf16[2048,1712]{1,0:T(8,128)(2,1)} async-done(((bf16[512,1712]{1,0:T(8,128)(2,1)}), bf16[2048,1712]{1,0:T(8,128)(2,1)}) %all-gather.6.cloned.1.call-update) | async-done | bytes 7012368 | tf_op jit(solution)/shard_map/all_gather | solution.py:1197
  233.8 6.7 fusion.1.refs_0_
  243.5 9.5 %delta_output.1 = (bf16[1024,512]{1,0:T(8,128)(2,1)S(1)}, f32[1024,512]{1,0:T(8,128)}, f32[2,8,128,256]{3,2,1,0:T(8,128)}, f32[2,8,128,256]{3,2,1,0:T(8,128)}) custom-call(f32[2,128,256]{2,1,0:T(8,128)S(1)} %convert_element_type.424.start_ref, f32[2,8,128,256]{3,2,1,0:T(8,128)} %get-tuple-element.200.s0_ref, f32[2,9,128,128]{3,2,1,0:T(8,128)S(1)} %copy-done.29, ...), custom_call_target="tpu_custom_call" | custom-call | flops 53687092 | bytes 122880 | tf_op jit(solution)/shard_map/delta_output/pallas_call | solution.py:289
  253.1 4.8 block_products.9
  277.9 11.2 %collective-permute-done.17 = bf16[2,512,256]{2,1,0:T(8,128)(2,1)S(1)} collective-permute-done((bf16[2,512,256]{2,1,0:T(8,128)(2,1)S(1)}, bf16[2,512,256]{2,1,0:T(8,128)(2,1)S(1)}, u32[]{:S(2)}, u32[]{:S(2)}) %collective-permute-start.17) | collective-permute-done | bytes 524320 | tf_op jit(solution)/shard_map/ppermute | solution.py:680
  293.8 5.7 collective-permute-done.19
  303.3 11.1 %collective-permute-done.21 = f32[1,512,256]{2,1,0:T(8,128)S(1)} collective-permute-done((f32[1,512,256]{2,1,0:T(8,128)S(1)}, f32[1,512,256]{2,1,0:T(8,128)S(1)}, u32[]{:S(2)}, u32[]{:S(2)}) %collective-permute-start.21) | collective-permute-done | bytes 524320 | tf_op jit(solution)/shard_map/ppermute | solution.py:680
  317.0 20.3 %collective-permute-done.23 = f32[2,512,256]{2,1,0:T(8,128)S(1)} collective-permute-done((f32[2,512,256]{2,1,0:T(8,128)S(1)}, f32[2,512,256]{2,1,0:T(8,128)S(1)}, u32[]{:S(2)}, u32[]{:S(2)}) %collective-permute-start.23) | collective-permute-done | bytes 1048608 | tf_op jit(solution)/shard_map/ppermute | solution.py:680
  342.5 4.7 fusion.89
  350.8 7.4 %assemble.5 = (bf16[1024,2048]{1,0:T(8,128)(2,1)}, f32[1024,128]{1,0:T(8,128)}) custom-call(s32[1]{0:T(128)} %bitcast.refs_0_.mp_ref, f32[4,512,256]{2,1,0:T(8,128)} %pad_maximum_fusion.1.refs_1_.refs_5_, f32[4,512,256]{2,1,0:T(8,128)} %collective-permute-done.25.refs_2_.refs_6_, f32[4,512,256]{2,1,0:T(8,128)} %pad_maximum_fusion.2.refs_3_.refs_7_, ...), custom_call_target="tpu_custom_call" | custom-call | flops 209715 | bytes 83886 | tf_op jit(solution)/shard_map/assemble/pallas_call | solution.py:776
  358.2 19.5 %all-gather.8.cloned.1.call-done.gu_ref.refs_1_ = bf16[2048,1376]{1,0:T(8,128)(2,1)} async-done(((bf16[512,1376]{1,0:T(8,128)(2,1)}), bf16[2048,1376]{1,0:T(8,128)(2,1)}) %all-gather.8.cloned.1.call-update) | async-done | bytes 5636112 | tf_op jit(solution)/shard_map/all_gather | solution.py:1208
  377.7 11.3 %ffn.1 = (bf16[1024,688]{1,0:T(8,128)(2,1)S(1)}, bf16[1024,1376]{1,0:T(8,128)(2,1)S(1)}) custom-call(bf16[1024,2048]{1,0:T(8,128)(2,1)} %get-tuple-element.229.x_ref, f32[1024,688]{1,0:T(8,128)} %copy.74.back_ref, bf16[2048,1376]{1,0:T(8,128)(2,1)} %all-gather.8.cloned.1.call-done.gu_ref.refs_1_), custom_call_target="tpu_custom_call" | custom-call | flops 86570432 | bytes 168427 | tf_op jit(solution)/shard_map/ffn/pallas_call | solution.py:1108
  390.2 8.1 %convolution_convert_fusion.1 = bf16[2048,1376]{0,1:T(8,128)(2,1)} fusion(bf16[1024,2048]{1,0:T(8,128)(2,1)S(1)} %copy-done.71, bf16[1024,1376]{1,0:T(8,128)(2,1)S(1)} %get-tuple-element.238.refs_0_), kind=kOutput, calls=%fused_computation.1 | convolution fusion | flops 5774180352 | bytes 12648448 | tf_op jit(solution)/shard_map/dot_general | solution.py:963
  398.4 5.4 block_products.11
  403.8 6.7 block_products.10
  415.7 11.3 %collective-permute-done.28 = bf16[2,512,256]{2,1,0:T(8,128)(2,1)S(1)} collective-permute-done((bf16[2,512,256]{2,1,0:T(8,128)(2,1)S(1)}, bf16[2,512,256]{2,1,0:T(8,128)(2,1)S(1)}, u32[]{:S(2)}, u32[]{:S(2)}) %collective-permute-start.28) | collective-permute-done | bytes 524320 | tf_op jit(solution)/shard_map/ppermute | solution.py:680
  430.5 5.5 collective-permute-done.30
  438.8 10.8 %collective-permute-done.32 = f32[1,512,256]{2,1,0:T(8,128)S(1)} collective-permute-done((f32[1,512,256]{2,1,0:T(8,128)S(1)}, f32[1,512,256]{2,1,0:T(8,128)S(1)}, u32[]{:S(2)}, u32[]{:S(2)}) %collective-permute-start.32) | collective-permute-done | bytes 524320 | tf_op jit(solution)/shard_map/ppermute | solution.py:680
  452.3 20.0 %collective-permute-done.34 = f32[2,512,256]{2,1,0:T(8,128)S(1)} collective-permute-done((f32[2,512,256]{2,1,0:T(8,128)S(1)}, f32[2,512,256]{2,1,0:T(8,128)S(1)}, u32[]{:S(2)}, u32[]{:S(2)}) %collective-permute-start.34) | collective-permute-done | bytes 1048608 | tf_op jit(solution)/shard_map/ppermute | solution.py:680
  482.7 11.7 %norm_back.1 = (bf16[1024,2048]{1,0:T(8,128)(2,1)}, f32[1024,256]{1,0:T(8,128)S(1)}, f32[1,256]{1,0:T(1,128)S(1)}) custom-call(s32[1]{0:T(128)} %bitcast.refs_0_.mp_ref, f32[4,512,256]{2,1,0:T(8,128)S(1)} %pad_maximum_fusion.3.refs_1_, f32[4,512,256]{2,1,0:T(8,128)} %copy-done.73, f32[4,512,256]{2,1,0:T(8,128)} %copy-done.63, ...), custom_call_target="tpu_custom_call" | custom-call | flops 419430 | bytes 167772 | tf_op jit(solution)/shard_map/norm_back/pallas_call | solution.py:834
  495.3 6.1 fusion.90.dm_ref
  501.5 7.6 %delta_tail.1 = (f32[1024,512]{1,0:T(8,128)S(1)}, bf16[1024,512]{1,0:T(8,128)(2,1)S(1)}, f32[2,256]{1,0:T(2,128)S(1)}, f32[2,8,128,256]{3,2,1,0:T(8,128)}, f32[2,128,256]{2,1,0:T(8,128)S(1)}) custom-call(f32[1024,512]{1,0:T(8,128)} %fusion.90.dm_ref, f32[1024,512]{1,0:T(8,128)} %get-tuple-element.261.o_ref, f32[2,256]{1,0:T(2,128)S(1)} %copy-done.53, ...), custom_call_target="tpu_custom_call" | custom-call | flops 53687092 | bytes 122880 | tf_op jit(solution)/shard_map/delta_tail/pallas_call | solution.py:366
  516.3 6.1 collective-permute-done.38
  524.0 12.5 %collective-permute-done.39 = bf16[2,128,256]{2,1,0:T(8,128)(2,1)S(1)} collective-permute-done((bf16[2,128,256]{2,1,0:T(8,128)(2,1)S(1)}, bf16[2,128,256]{2,1,0:T(8,128)(2,1)S(1)}, u32[]{:S(2)}, u32[]{:S(2)}) %collective-permute-start.39) | collective-permute-done | bytes 131104 | tf_op jit(solution)/shard_map/ppermute | solution.py:955
  540.6 5.6 delta_early.1
  552.9 19.9 %delta_grads.1 = (f32[1024,1024]{1,0:T(8,128)}, f32[2,1024,8]{2,1,0:T(8,128)S(1)}) custom-call(f32[2,128,256]{2,1,0:T(8,128)S(1)} %convert_element_type.469.end_ref, f32[1024,1024]{1,0:T(8,128)} %copy-done, f32[2,1024,8]{2,1,0:T(8,128)S(1)} %copy-done.8, f32[2,8,128,128]{3,2,1,0:T(8,128)S(1)} %copy-done.33, f32[2,8,128,128]{3,2,1,0:T(8,128)S(1)} %copy-done.19, ...), custom_call_target="tpu_custom_call" | custom-call | flops 161061280 | bytes 245760 | tf_op jit(solution)/shard_map/delta_grads/pallas_call | solution.py:491
  575.1 12.3 %front_back.1 = (bf16[1024,1536]{1,0:T(8,128)(2,1)S(1)}, f32[16,1536]{1,0:T(8,128)S(1)}, f32[4,1536]{1,0:T(4,128)S(1)}) custom-call(f32[1024,1024]{1,0:T(8,128)} %get-tuple-element.190.x_ref, f32[16,1024]{1,0:T(8,128)S(1)} %get-tuple-element.191.rim_ref, f32[1024,1024]{1,0:T(8,128)} %get-tuple-element.235.conv_ref, f32[1024,8]{1,0:T(8,128)S(1)} %copy-done.10, ...), custom_call_target="tpu_custom_call" | custom-call | flops 1258291 | bytes 220200 | tf_op jit(solution)/shard_map/front_back/pallas_call | solution.py:650
  587.5 8.8 %convolution_convert_fusion = bf16[2048,1536]{1,0:T(8,128)(2,1)} fusion(bf16[1024,2048]{1,0:T(8,128)(2,1)S(1)} %copy-done.57, bf16[1024,1536]{1,0:T(8,128)(2,1)S(1)} %maximum_dynamic-update-slice_fusion.refs_2_.refs_4_.refs_6_.refs_8_), kind=kOutput, calls=%fused_computation | convolution fusion | flops 6445596672 | bytes 13631488 | tf_op jit(solution)/shard_map/dot_general | solution.py:963
  601.6 7.3 block_products.12
  608.9 4.9 block_products.14
  613.8 7.1 block_products.15
  638.5 9.3 %collective-permute-done.43 = bf16[2,512,256]{2,1,0:T(8,128)(2,1)S(1)} collective-permute-done((bf16[2,512,256]{2,1,0:T(8,128)(2,1)S(1)}, bf16[2,512,256]{2,1,0:T(8,128)(2,1)S(1)}, u32[]{:S(2)}, u32[]{:S(2)}) %collective-permute-start.43) | collective-permute-done | bytes 524320 | tf_op jit(solution)/shard_map/ppermute | solution.py:680
  647.9 10.2 %collective-permute-done.48 = bf16[2,512,256]{2,1,0:T(8,128)(2,1)S(1)} collective-permute-done((bf16[2,512,256]{2,1,0:T(8,128)(2,1)S(1)}, bf16[2,512,256]{2,1,0:T(8,128)(2,1)S(1)}, u32[]{:S(2)}, u32[]{:S(2)}) %collective-permute-start.48) | collective-permute-done | bytes 524320 | tf_op jit(solution)/shard_map/ppermute | solution.py:680
  705.1 20.4 %reduce-scatter.4.cloned.1.call-done = bf16[512,1536]{1,0:T(8,128)(2,1)} async-done(((bf16[2048,1536]{1,0:T(8,128)(2,1)}), bf16[512,1536]{1,0:T(8,128)(2,1)}) %reduce-scatter.4.cloned.1.call-update) | async-done | bytes 1572880 | tf_op jit(solution)/shard_map/reduce_scatter | solution.py:1275
  725.6 4.9 reshape.231
  (434 shorter events, 219.9 us)
Async XLA Ops:
  7.2 88.6 %all-gather.4.cloned.1.call-start = ((), (), s32[]{:S(2)}) async-start(), calls=%async_computation.3 | async-start | bytes 5406720 | tf_op jit(solution)/shard_map/all_gather | solution.py:1190
  9.8 224.1 %all-gather.6.cloned.1.call-start = ((), (), s32[]{:S(2)}) async-start(), calls=%async_computation.4 | async-start | bytes 9175040 | tf_op jit(solution)/shard_map/all_gather | solution.py:1197
  9.9 9.3 %collective-permute-start = (bf16[1,512,256]{2,1,0:T(8,128)(2,1)S(1)}, bf16[1,512,256]{2,1,0:T(8,128)(2,1)S(1)}, u32[]{:S(2)}, u32[]{:S(2)}) collective-permute-start(bf16[1,512,256]{2,1,0:T(8,128)(2,1)S(1)} %get-tuple-element.163), channel_id=1, source_target_pairs={{0,4},{1,5},{2,6},{3,7},{4,0},{5,1},{6,2},{7,3},{8,12},{9,13},{10,... | collective-permute-start | bytes 786440 | tf_op jit(solution)/shard_map/ppermute | solution.py:680
  22.4 12.8 %collective-permute-start.2 = (bf16[2,512,256]{2,1,0:T(8,128)(2,1)}, bf16[2,512,256]{2,1,0:T(8,128)(2,1)}, u32[]{:S(2)}, u32[]{:S(2)}) collective-permute-start(bf16[2,512,256]{2,1,0:T(8,128)(2,1)} %pad_maximum_fusion.17), channel_id=1, source_target_pairs={{0,2},{1,3},{2,0},{3,1},{4,6},{5,7},{6,4},{7,5},{8,10},{9,11},{10,... | collective-permute-start | bytes 1572872 | tf_op jit(solution)/shard_map/ppermute | solution.py:680
  23.9 12.5 %collective-permute-start.3 = (bf16[2,512,256]{2,1,0:T(8,128)(2,1)}, bf16[2,512,256]{2,1,0:T(8,128)(2,1)}, u32[]{:S(2)}, u32[]{:S(2)}) collective-permute-start(bf16[2,512,256]{2,1,0:T(8,128)(2,1)} %pad_maximum_fusion.18), channel_id=1, source_target_pairs={{0,4},{1,5},{2,6},{3,7},{4,0},{5,1},{6,2},{7,3},{8,12},{9,13},{10,... | collective-permute-start | bytes 1572872 | tf_op jit(solution)/shard_map/ppermute | solution.py:680
  37.8 339.9 %all-gather.8.cloned.1.call-start = ((), (), s32[]{:S(2)}) async-start(), calls=%async_computation.5 | async-start | bytes 7208960 | tf_op jit(solution)/shard_map/all_gather | solution.py:1208
  47.9 8.4 %collective-permute-start.7 = (bf16[1,512,256]{2,1,0:T(8,128)(2,1)S(1)}, bf16[1,512,256]{2,1,0:T(8,128)(2,1)S(1)}, u32[]{:S(2)}, u32[]{:S(2)}) collective-permute-start(bf16[1,512,256]{2,1,0:T(8,128)(2,1)S(1)} %get-tuple-element.177), channel_id=1, source_target_pairs={{0,4},{1,5},{2,6},{3,7},{4,0},{5,1},{6,2},{7,3},{8,12},{9,13},{10,... | collective-permute-start | bytes 786440 | tf_op jit(solution)/shard_map/ppermute | solution.py:680
  56.8 13.0 %collective-permute-start.9 = (bf16[2,512,256]{2,1,0:T(8,128)(2,1)S(1)}, bf16[2,512,256]{2,1,0:T(8,128)(2,1)S(1)}, u32[]{:S(2)}, u32[]{:S(2)}) collective-permute-start(bf16[2,512,256]{2,1,0:T(8,128)(2,1)S(1)} %pad_maximum_fusion.19), channel_id=1, source_target_pairs={{0,2},{1,3},{2,0},{3,1},{4,6},{5,7},{6,4},{7,5},{8,10},{9,11},{10,... | collective-permute-start | bytes 1572872 | tf_op jit(solution)/shard_map/ppermute | solution.py:680
  57.4 12.6 %collective-permute-start.10 = (bf16[2,512,256]{2,1,0:T(8,128)(2,1)S(1)}, bf16[2,512,256]{2,1,0:T(8,128)(2,1)S(1)}, u32[]{:S(2)}, u32[]{:S(2)}) collective-permute-start(bf16[2,512,256]{2,1,0:T(8,128)(2,1)S(1)} %pad_maximum_fusion.20), channel_id=1, source_target_pairs={{0,4},{1,5},{2,6},{3,7},{4,0},{5,1},{6,2},{7,3},{8,12},{9,13},{10,... | collective-permute-start | bytes 1572872 | tf_op jit(solution)/shard_map/ppermute | solution.py:680
  71.9 23.9 %collective-permute-start.6 = (bf16[16,2048]{1,0:T(8,128)(2,1)S(1)}, bf16[16,2048]{1,0:T(8,128)(2,1)S(1)}, u32[]{:S(2)}, u32[]{:S(2)}) collective-permute-start(bf16[16,2048]{1,0:T(8,128)(2,1)S(1)} %slice.400), channel_id=1, source_target_pairs={{0,8},{8,16},{16,24},{1,9},{9,17},{17,25},{2,10},{10,18},{18,26},{... | collective-permute-start | bytes 196616 | tf_op jit(solution)/shard_map/ppermute | solution.py:955
  153.0 8.3 %collective-permute-start.13 = (bf16[2,128,256]{2,1,0:T(8,128)(2,1)S(1)}, bf16[2,128,256]{2,1,0:T(8,128)(2,1)S(1)}, u32[]{:S(2)}, u32[]{:S(2)}) collective-permute-start(bf16[2,128,256]{2,1,0:T(8,128)(2,1)S(1)} %convert_element_type.421), channel_id=1, source_target_pairs={{0,8},{8,16},{16,24},{1,9},{9,17},{17,25},{2,10},{10,18},{18,26},{... | collective-permute-start | bytes 393224 | tf_op jit(solution)/shard_map/ppermute | solution.py:955
  161.5 14.0 %collective-permute-start.14 = (bf16[2,128,256]{2,1,0:T(8,128)(2,1)S(1)}, bf16[2,128,256]{2,1,0:T(8,128)(2,1)S(1)}, u32[]{:S(2)}, u32[]{:S(2)}) collective-permute-start(bf16[2,128,256]{2,1,0:T(8,128)(2,1)S(1)} %fusion.3), channel_id=1, source_target_pairs={{0,8},{8,16},{16,24},{1,9},{9,17},{17,25},{2,10},{10,18},{18,26},{... | collective-permute-start | bytes 393224 | tf_op jit(solution)/shard_map/ppermute | solution.py:955
  175.8 14.4 %collective-permute-start.15 = (bf16[2,128,256]{2,1,0:T(8,128)(2,1)S(1)}, bf16[2,128,256]{2,1,0:T(8,128)(2,1)S(1)}, u32[]{:S(2)}, u32[]{:S(2)}) collective-permute-start(bf16[2,128,256]{2,1,0:T(8,128)(2,1)S(1)} %fusion.4), channel_id=1, source_target_pairs={{0,8},{8,16},{16,24},{1,9},{9,17},{17,25},{2,10},{10,18},{18,26},{... | collective-permute-start | bytes 393224 | tf_op jit(solution)/shard_map/ppermute | solution.py:955
  257.9 15.2 %collective-permute-start.16 = (bf16[4,1024,256]{2,1,0:T(8,128)(2,1)}, bf16[4,1024,256]{2,1,0:T(8,128)(2,1)}, u32[]{:S(2)}, u32[]{:S(2)}) collective-permute-start(bf16[4,1024,256]{2,1,0:T(8,128)(2,1)} %block_products.9), channel_id=1, source_target_pairs={{0,1},{1,0},{2,3},{3,2},{4,5},{5,4},{6,7},{7,6},{8,9},{9,8},{10,11... | collective-permute-start | bytes 6291464 | tf_op jit(solution)/shard_map/ppermute | solution.py:680
  268.5 427.4 %reduce-scatter.8.cloned.1.call-start = ((), (), s32[]{:S(2)}) async-start(), calls=%async_computation.8 | async-start | bytes 7045120 | tf_op jit(solution)/shard_map/reduce_scatter | solution.py:1244
  274.7 14.4 %collective-permute-start.17 = (bf16[2,512,256]{2,1,0:T(8,128)(2,1)S(1)}, bf16[2,512,256]{2,1,0:T(8,128)(2,1)S(1)}, u32[]{:S(2)}, u32[]{:S(2)}) collective-permute-start(bf16[2,512,256]{2,1,0:T(8,128)(2,1)S(1)} %pad_maximum_fusion.21), channel_id=1, source_target_pairs={{0,2},{1,3},{2,0},{3,1},{4,6},{5,7},{6,4},{7,5},{8,10},{9,11},{10,... | collective-permute-start | bytes 1572872 | tf_op jit(solution)/shard_map/ppermute | solution.py:680
  276.4 14.1 %collective-permute-start.18 = (bf16[2,512,256]{2,1,0:T(8,128)(2,1)S(1)}, bf16[2,512,256]{2,1,0:T(8,128)(2,1)S(1)}, u32[]{:S(2)}, u32[]{:S(2)}) collective-permute-start(bf16[2,512,256]{2,1,0:T(8,128)(2,1)S(1)} %pad_maximum_fusion.22), channel_id=1, source_target_pairs={{0,4},{1,5},{2,6},{3,7},{4,0},{5,1},{6,2},{7,3},{8,12},{9,13},{10,... | collective-permute-start | bytes 1572872 | tf_op jit(solution)/shard_map/ppermute | solution.py:680
  302.1 12.3 %collective-permute-start.21 = (f32[1,512,256]{2,1,0:T(8,128)S(1)}, f32[1,512,256]{2,1,0:T(8,128)S(1)}, u32[]{:S(2)}, u32[]{:S(2)}) collective-permute-start(f32[1,512,256]{2,1,0:T(8,128)S(1)} %get-tuple-element.217), channel_id=1, source_target_pairs={{0,4},{1,5},{2,6},{3,7},{4,0},{5,1},{6,2},{7,3},{8,12},{9,13},{10,... | collective-permute-start | bytes 1572872 | tf_op jit(solution)/shard_map/ppermute | solution.py:680
  302.8 12.0 %collective-permute-start.22 = (f32[1,512,256]{2,1,0:T(8,128)S(1)}, f32[1,512,256]{2,1,0:T(8,128)S(1)}, u32[]{:S(2)}, u32[]{:S(2)}) collective-permute-start(f32[1,512,256]{2,1,0:T(8,128)S(1)} %get-tuple-element.218), channel_id=1, source_target_pairs={{0,2},{1,3},{2,0},{3,1},{4,6},{5,7},{6,4},{7,5},{8,10},{9,11},{10,... | collective-permute-start | bytes 1572872 | tf_op jit(solution)/shard_map/ppermute | solution.py:680
  314.9 22.5 %collective-permute-start.23 = (f32[2,512,256]{2,1,0:T(8,128)S(1)}, f32[2,512,256]{2,1,0:T(8,128)S(1)}, u32[]{:S(2)}, u32[]{:S(2)}) collective-permute-start(f32[2,512,256]{2,1,0:T(8,128)S(1)} %pad_maximum_fusion.11), channel_id=1, source_target_pairs={{0,2},{1,3},{2,0},{3,1},{4,6},{5,7},{6,4},{7,5},{8,10},{9,11},{10,... | collective-permute-start | bytes 3145736 | tf_op jit(solution)/shard_map/ppermute | solution.py:680
  315.7 22.3 %collective-permute-start.24 = (f32[2,512,256]{2,1,0:T(8,128)S(1)}, f32[2,512,256]{2,1,0:T(8,128)S(1)}, u32[]{:S(2)}, u32[]{:S(2)}) collective-permute-start(f32[2,512,256]{2,1,0:T(8,128)S(1)} %pad_maximum_fusion.12), channel_id=1, source_target_pairs={{0,4},{1,5},{2,6},{3,7},{4,0},{5,1},{6,2},{7,3},{8,12},{9,13},{10,... | collective-permute-start | bytes 3145736 | tf_op jit(solution)/shard_map/ppermute | solution.py:680
  341.0 9.7 %collective-permute-start.25 = (f32[4,512,256]{2,1,0:T(8,128)}, f32[4,512,256]{2,1,0:T(8,128)}, u32[]{:S(2)}, u32[]{:S(2)}) collective-permute-start(f32[4,512,256]{2,1,0:T(8,128)} %pad_maximum_fusion.1.refs_1_.refs_5_), channel_id=1, source_target_pairs={{0,1},{1,0},{2,3},{3,2},{4,5},{5,4},{6,7},{7,6},{8,9},{9,8},{10,11... | collective-permute-start | bytes 6291464 | tf_op jit(solution)/shard_map/ppermute | solution.py:680
  341.0 9.7 %collective-permute-start.26 = (f32[4,512,256]{2,1,0:T(8,128)}, f32[4,512,256]{2,1,0:T(8,128)}, u32[]{:S(2)}, u32[]{:S(2)}) collective-permute-start(f32[4,512,256]{2,1,0:T(8,128)} %pad_maximum_fusion.2.refs_3_.refs_7_), channel_id=1, source_target_pairs={{0,1},{1,0},{2,3},{3,2},{4,5},{5,4},{6,7},{7,6},{8,9},{9,8},{10,11... | collective-permute-start | bytes 6291464 | tf_op jit(solution)/shard_map/ppermute | solution.py:680
  398.3 302.3 %reduce-scatter.6.cloned.1.call-start = ((), (), s32[]{:S(2)}) async-start(), calls=%async_computation.7 | async-start | bytes 6144000 | tf_op jit(solution)/shard_map/reduce_scatter | solution.py:1258
  412.6 14.4 %collective-permute-start.28 = (bf16[2,512,256]{2,1,0:T(8,128)(2,1)S(1)}, bf16[2,512,256]{2,1,0:T(8,128)(2,1)S(1)}, u32[]{:S(2)}, u32[]{:S(2)}) collective-permute-start(bf16[2,512,256]{2,1,0:T(8,128)(2,1)S(1)} %pad_maximum_fusion.23), channel_id=1, source_target_pairs={{0,2},{1,3},{2,0},{3,1},{4,6},{5,7},{6,4},{7,5},{8,10},{9,11},{10,... | collective-permute-start | bytes 1572872 | tf_op jit(solution)/shard_map/ppermute | solution.py:680
  414.2 13.9 %collective-permute-start.29 = (bf16[2,512,256]{2,1,0:T(8,128)(2,1)S(1)}, bf16[2,512,256]{2,1,0:T(8,128)(2,1)S(1)}, u32[]{:S(2)}, u32[]{:S(2)}) collective-permute-start(bf16[2,512,256]{2,1,0:T(8,128)(2,1)S(1)} %pad_maximum_fusion.24), channel_id=1, source_target_pairs={{0,4},{1,5},{2,6},{3,7},{4,0},{5,1},{6,2},{7,3},{8,12},{9,13},{10,... | collective-permute-start | bytes 1572872 | tf_op jit(solution)/shard_map/ppermute | solution.py:680
  437.5 12.1 %collective-permute-start.32 = (f32[1,512,256]{2,1,0:T(8,128)S(1)}, f32[1,512,256]{2,1,0:T(8,128)S(1)}, u32[]{:S(2)}, u32[]{:S(2)}) collective-permute-start(f32[1,512,256]{2,1,0:T(8,128)S(1)} %get-tuple-element.247), channel_id=1, source_target_pairs={{0,4},{1,5},{2,6},{3,7},{4,0},{5,1},{6,2},{7,3},{8,12},{9,13},{10,... | collective-permute-start | bytes 1572872 | tf_op jit(solution)/shard_map/ppermute | solution.py:680
  438.1 11.8 %collective-permute-start.33 = (f32[1,512,256]{2,1,0:T(8,128)S(1)}, f32[1,512,256]{2,1,0:T(8,128)S(1)}, u32[]{:S(2)}, u32[]{:S(2)}) collective-permute-start(f32[1,512,256]{2,1,0:T(8,128)S(1)} %get-tuple-element.248), channel_id=1, source_target_pairs={{0,2},{1,3},{2,0},{3,1},{4,6},{5,7},{6,4},{7,5},{8,10},{9,11},{10,... | collective-permute-start | bytes 1572872 | tf_op jit(solution)/shard_map/ppermute | solution.py:680
  450.1 22.3 %collective-permute-start.34 = (f32[2,512,256]{2,1,0:T(8,128)S(1)}, f32[2,512,256]{2,1,0:T(8,128)S(1)}, u32[]{:S(2)}, u32[]{:S(2)}) collective-permute-start(f32[2,512,256]{2,1,0:T(8,128)S(1)} %pad_maximum_fusion.13), channel_id=1, source_target_pairs={{0,2},{1,3},{2,0},{3,1},{4,6},{5,7},{6,4},{7,5},{8,10},{9,11},{10,... | collective-permute-start | bytes 3145736 | tf_op jit(solution)/shard_map/ppermute | solution.py:680
  450.9 22.1 %collective-permute-start.35 = (f32[2,512,256]{2,1,0:T(8,128)S(1)}, f32[2,512,256]{2,1,0:T(8,128)S(1)}, u32[]{:S(2)}, u32[]{:S(2)}) collective-permute-start(f32[2,512,256]{2,1,0:T(8,128)S(1)} %pad_maximum_fusion.14), channel_id=1, source_target_pairs={{0,4},{1,5},{2,6},{3,7},{4,0},{5,1},{6,2},{7,3},{8,12},{9,13},{10,... | collective-permute-start | bytes 3145736 | tf_op jit(solution)/shard_map/ppermute | solution.py:680
  473.4 8.9 %collective-permute-start.37 = (f32[4,512,256]{2,1,0:T(8,128)S(1)}, f32[4,512,256]{2,1,0:T(8,128)}, u32[]{:S(2)}, u32[]{:S(2)}) collective-permute-start(f32[4,512,256]{2,1,0:T(8,128)S(1)} %pad_maximum_fusion.4.refs_3_), channel_id=1, source_target_pairs={{0,1},{1,0},{2,3},{3,2},{4,5},{5,4},{6,7},{7,6},{8,9},{9,8},{10,11... | collective-permute-start | bytes 6291464 | tf_op jit(solution)/shard_map/ppermute | solution.py:680
  514.8 210.8 %reduce-scatter.4.cloned.1.call-start = ((), (), s32[]{:S(2)}) async-start(), calls=%async_computation.6 | async-start | bytes 7864320 | tf_op jit(solution)/shard_map/reduce_scatter | solution.py:1275
  522.7 13.8 %collective-permute-start.39 = (bf16[2,128,256]{2,1,0:T(8,128)(2,1)S(1)}, bf16[2,128,256]{2,1,0:T(8,128)(2,1)S(1)}, u32[]{:S(2)}, u32[]{:S(2)}) collective-permute-start(bf16[2,128,256]{2,1,0:T(8,128)(2,1)S(1)} %fusion.5), channel_id=1, source_target_pairs={{8,0},{16,8},{24,16},{9,1},{17,9},{25,17},{10,2},{18,10},{26,18},{... | collective-permute-start | bytes 393224 | tf_op jit(solution)/shard_map/ppermute | solution.py:955
  536.8 16.0 %collective-permute-start.40 = (bf16[2,128,256]{2,1,0:T(8,128)(2,1)S(1)}, bf16[2,128,256]{2,1,0:T(8,128)(2,1)S(1)}, u32[]{:S(2)}, u32[]{:S(2)}) collective-permute-start(bf16[2,128,256]{2,1,0:T(8,128)(2,1)S(1)} %fusion.6), channel_id=1, source_target_pairs={{8,0},{16,8},{24,16},{9,1},{17,9},{25,17},{10,2},{18,10},{26,18},{... | collective-permute-start | bytes 393224 | tf_op jit(solution)/shard_map/ppermute | solution.py:955
  573.7 13.7 %collective-permute-start.41 = (f32[8,1024]{1,0:T(8,128)S(1)}, f32[8,1024]{1,0:T(8,128)S(1)}, u32[]{:S(2)}, u32[]{:S(2)}) collective-permute-start(f32[8,1024]{1,0:T(8,128)S(1)} %rim_back.1), channel_id=1, source_target_pairs={{8,0},{16,8},{24,16},{9,1},{17,9},{25,17},{10,2},{18,10},{26,18},{... | collective-permute-start | bytes 98312 | tf_op jit(solution)/shard_map/ppermute | solution.py:955
  613.8 16.9 %collective-permute-start.42 = (bf16[4,1024,256]{2,1,0:T(8,128)(2,1)}, bf16[4,1024,256]{2,1,0:T(8,128)(2,1)}, u32[]{:S(2)}, u32[]{:S(2)}) collective-permute-start(bf16[4,1024,256]{2,1,0:T(8,128)(2,1)} %block_products.14), channel_id=1, source_target_pairs={{0,1},{1,0},{2,3},{3,2},{4,5},{5,4},{6,7},{7,6},{8,9},{9,8},{10,11... | collective-permute-start | bytes 6291464 | tf_op jit(solution)/shard_map/ppermute | solution.py:680
  620.8 13.6 %collective-permute-start.47 = (bf16[4,1024,256]{2,1,0:T(8,128)(2,1)}, bf16[4,1024,256]{2,1,0:T(8,128)(2,1)S(1)}, u32[]{:S(2)}, u32[]{:S(2)}) collective-permute-start(bf16[4,1024,256]{2,1,0:T(8,128)(2,1)} %block_products.15), channel_id=1, source_target_pairs={{0,1},{1,0},{2,3},{3,2},{4,5},{5,4},{6,7},{7,6},{8,9},{9,8},{10,11... | collective-permute-start | bytes 6291464 | tf_op jit(solution)/shard_map/ppermute | solution.py:680
  633.0 14.9 %collective-permute-start.43 = (bf16[2,512,256]{2,1,0:T(8,128)(2,1)S(1)}, bf16[2,512,256]{2,1,0:T(8,128)(2,1)S(1)}, u32[]{:S(2)}, u32[]{:S(2)}) collective-permute-start(bf16[2,512,256]{2,1,0:T(8,128)(2,1)S(1)} %pad_maximum_fusion.25), channel_id=1, source_target_pairs={{0,2},{1,3},{2,0},{3,1},{4,6},{5,7},{6,4},{7,5},{8,10},{9,11},{10,... | collective-permute-start | bytes 1572872 | tf_op jit(solution)/shard_map/ppermute | solution.py:680
  633.1 14.9 %collective-permute-start.44 = (bf16[2,512,256]{2,1,0:T(8,128)(2,1)S(1)}, bf16[2,512,256]{2,1,0:T(8,128)(2,1)S(1)}, u32[]{:S(2)}, u32[]{:S(2)}) collective-permute-start(bf16[2,512,256]{2,1,0:T(8,128)(2,1)S(1)} %pad_maximum_fusion.26), channel_id=1, source_target_pairs={{0,4},{1,5},{2,6},{3,7},{4,0},{5,1},{6,2},{7,3},{8,12},{9,13},{10,... | collective-permute-start | bytes 1572872 | tf_op jit(solution)/shard_map/ppermute | solution.py:680
  634.8 23.3 %collective-permute-start.48 = (bf16[2,512,256]{2,1,0:T(8,128)(2,1)S(1)}, bf16[2,512,256]{2,1,0:T(8,128)(2,1)S(1)}, u32[]{:S(2)}, u32[]{:S(2)}) collective-permute-start(bf16[2,512,256]{2,1,0:T(8,128)(2,1)S(1)} %pad_maximum_fusion.27), channel_id=1, source_target_pairs={{0,2},{1,3},{2,0},{3,1},{4,6},{5,7},{6,4},{7,5},{8,10},{9,11},{10,... | collective-permute-start | bytes 1572872 | tf_op jit(solution)/shard_map/ppermute | solution.py:680
  636.9 21.4 %collective-permute-start.49 = (bf16[2,512,256]{2,1,0:T(8,128)(2,1)S(1)}, bf16[2,512,256]{2,1,0:T(8,128)(2,1)S(1)}, u32[]{:S(2)}, u32[]{:S(2)}) collective-permute-start(bf16[2,512,256]{2,1,0:T(8,128)(2,1)S(1)} %pad_maximum_fusion.28), channel_id=1, source_target_pairs={{0,4},{1,5},{2,6},{3,7},{4,0},{5,1},{6,2},{7,3},{8,12},{9,13},{10,... | collective-permute-start | bytes 1572872 | tf_op jit(solution)/shard_map/ppermute | solution.py:680
  658.4 8.4 %collective-permute-start.50 = (bf16[1,512,256]{2,1,0:T(8,128)(2,1)S(1)}, bf16[1,512,256]{2,1,0:T(8,128)(2,1)S(1)}, u32[]{:S(2)}, u32[]{:S(2)}) collective-permute-start(bf16[1,512,256]{2,1,0:T(8,128)(2,1)S(1)} %get-tuple-element.304), channel_id=1, source_target_pairs={{0,4},{1,5},{2,6},{3,7},{4,0},{5,1},{6,2},{7,3},{8,12},{9,13},{10,... | collective-permute-start | bytes 786440 | tf_op jit(solution)/shard_map/ppermute | solution.py:680
  659.8 8.6 %collective-permute-start.51 = (bf16[1,512,256]{2,1,0:T(8,128)(2,1)S(1)}, bf16[1,512,256]{2,1,0:T(8,128)(2,1)S(1)}, u32[]{:S(2)}, u32[]{:S(2)}) collective-permute-start(bf16[1,512,256]{2,1,0:T(8,128)(2,1)S(1)} %get-tuple-element.305), channel_id=1, source_target_pairs={{0,2},{1,3},{2,0},{3,1},{4,6},{5,7},{6,4},{7,5},{8,10},{9,11},{10,... | collective-permute-start | bytes 786440 | tf_op jit(solution)/shard_map/ppermute | solution.py:680
  663.8 12.5 %collective-permute-start.45 = (bf16[1,512,256]{2,1,0:T(8,128)(2,1)}, bf16[1,512,256]{2,1,0:T(8,128)(2,1)S(1)}, u32[]{:S(2)}, u32[]{:S(2)}) collective-permute-start(bf16[1,512,256]{2,1,0:T(8,128)(2,1)} %get-tuple-element.294), channel_id=1, source_target_pairs={{0,4},{1,5},{2,6},{3,7},{4,0},{5,1},{6,2},{7,3},{8,12},{9,13},{10,... | collective-permute-start | bytes 786440 | tf_op jit(solution)/shard_map/ppermute | solution.py:680
  664.6 11.7 %collective-permute-start.46 = (bf16[1,512,256]{2,1,0:T(8,128)(2,1)}, bf16[1,512,256]{2,1,0:T(8,128)(2,1)S(1)}, u32[]{:S(2)}, u32[]{:S(2)}) collective-permute-start(bf16[1,512,256]{2,1,0:T(8,128)(2,1)} %get-tuple-element.295), channel_id=1, source_target_pairs={{0,2},{1,3},{2,0},{3,1},{4,6},{5,7},{6,4},{7,5},{8,10},{9,11},{10,... | collective-permute-start | bytes 786440 | tf_op jit(solution)/shard_map/ppermute | solution.py:680
  671.3 14.7 %collective-permute-start.56 = (f32[112,128]{1,0:T(8,128)S(1)}, f32[112,128]{1,0:T(8,128)S(1)}, u32[]{:S(2)}, u32[]{:S(2)}) collective-permute-start(f32[112,128]{1,0:T(8,128)S(1)} %pad_bitcast_fusion), channel_id=1, source_target_pairs={{0,16},{8,24},{16,0},{24,8},{1,17},{9,25},{17,1},{25,9},{2,18},{10... | collective-permute-start | bytes 172040 | tf_op jit(solution)/shard_map/ppermute | solution.py:948
  672.9 13.2 %collective-permute-start.57 = (f32[112,128]{1,0:T(8,128)S(1)}, f32[112,128]{1,0:T(8,128)S(1)}, u32[]{:S(2)}, u32[]{:S(2)}) collective-permute-start(f32[112,128]{1,0:T(8,128)S(1)} %pad_bitcast_fusion), channel_id=1, source_target_pairs={{0,24},{8,0},{16,8},{24,16},{1,25},{9,1},{17,9},{25,17},{2,26},{10... | collective-permute-start | bytes 172040 | tf_op jit(solution)/shard_map/ppermute | solution.py:948
  676.3 9.8 %collective-permute-start.55 = (f32[112,128]{1,0:T(8,128)S(1)}, f32[112,128]{1,0:T(8,128)S(1)}, u32[]{:S(2)}, u32[]{:S(2)}) collective-permute-start(f32[112,128]{1,0:T(8,128)S(1)} %pad_bitcast_fusion), channel_id=1, source_target_pairs={{0,8},{8,16},{16,24},{24,0},{1,9},{9,17},{17,25},{25,1},{2,10},{10... | collective-permute-start | bytes 172040 | tf_op jit(solution)/shard_map/ppermute | solution.py:948
  (110 other events, 936.7 us)
Sparse Core Ops, SparseCore 0:
  10.2 85.6 all-gather.3
  97.4 136.3 all-gather.5
  268.6 109.0 all-gather.7
  398.4 98.4 reduce-scatter.7
  514.9 93.7 reduce-scatter.5
  611.0 114.5 reduce-scatter.3
